TPU v7x, 128 devices: a whole 4x4x4 slice. The times are simulated.
128 devices in a mesh: rep: 2 (over x_lo), row: 64 (over y, x_hi, z, core).
Axes of the slice: x: 4 (x_hi: 2, x_lo: 2; x = x_hi * 2 + x_lo), y: 4, z: 4, core: 2. Of those that a mesh axis runs over, the one named last changes fastest.
Arguments:
- features: bfloat16 [65536, 256], P(('rep', 'row')), may hold values from -6 to 6
- tile_vals: bfloat16 [90112, 128, 128], P(('rep', 'row')), may hold values from 0 to 1, as said below
- tile_dst: int32 [90112], P(('rep', 'row')), may hold values from 0 to 7
- tile_src: int32 [90112], P(('rep', 'row')), may hold values from 0 to 255, as said below
- tile_count: int32 [128], P(('rep', 'row')), may hold values from 88 to 704
- degree: int32 [65536], P(('rep', 'row')), may hold values from 88 to 703
- w_self: bfloat16 [256, 256], replicated, may hold values from -0.375 to 0.375
- w_neigh: bfloat16 [256, 256], replicated, may hold values from -0.375 to 0.375
- out_bias: float32 [256], replicated, may hold values from -4 to 4
Outputs:
- result: bfloat16 [65536, 256], P(('rep', 'row'))
Inputs may be any that keep to these rules, and one draw needn't show every extreme that they name: Within each device's live slots the pairs (tile_src, tile_dst) are distinct and in ascending order of tile_src, then tile_dst. `tile_vals`: entries are 0 or 1.
All inputs are finite; a program needn't handle non-finite values.
Results may differ from a plain program's by a relative error of at most 0.0028.
Values may be sent and summed in bfloat16 or wider, within the bound.
No kernel may reach another device: no remote copies, remote signals or barrier semaphores. Data moves between devices by JAX's collectives and lax.ppermute only.
A program may use at most 128 MiB of HBM per device.

v0:
```python
import jax
import jax.numpy as jnp
from jax import lax
from jax.sharding import PartitionSpec as P


def pick_step(tile_total):
    for candidate in (64, 32, 16, 8, 4):
        return candidate
    return tile_total


def tile_products(running, tile_block, dst_block, src_block, live_mask, source_rows, first_block):
    picked = jnp.clip(src_block - first_block, 0, source_rows.shape[0] - 1)
    neighbour_rows = jnp.take(source_rows, picked, axis=0)
    products = jnp.einsum(
        "tij,tjh->tih", tile_block, neighbour_rows, preferred_element_type=jnp.float32
    )
    products = jnp.where(live_mask[:, None, None], products, jnp.zeros_like(products))
    return running.at[dst_block].add(products)


def on_device(
    features, tile_vals, tile_dst, tile_src, tile_count, degree, w_self, w_neigh, out_bias
):
    tile_edge = tile_vals.shape[1]
    feat_width = features.shape[1]
    tile_total = tile_vals.shape[0]
    dst_blocks = 2 * features.shape[0] // tile_edge
    live_tiles = tile_count[0]
    empty_sum = jnp.zeros((dst_blocks, tile_edge, feat_width), jnp.float32)

    def slot_slice(anchor_slot, width):
        return (
            lax.dynamic_slice_in_dim(tile_vals, anchor_slot, width, 0),
            lax.dynamic_slice_in_dim(tile_dst, anchor_slot, width, 0),
            lax.dynamic_slice_in_dim(tile_src, anchor_slot, width, 0),
        )

    tile_step = pick_step(tile_total)
    gathered = lax.all_gather(features, "row", axis=0, tiled=True)
    source_rows = gathered.reshape(-1, tile_edge, feat_width)
    round_count = (live_tiles + tile_step - 1) // tile_step

    def one_round(turn_index, running):
        begin_slot = turn_index * tile_step
        tile_block, dst_block, src_block = slot_slice(begin_slot, tile_step)
        live_mask = begin_slot + jnp.arange(tile_step, dtype=jnp.int32) < live_tiles
        return tile_products(running, tile_block, dst_block, src_block, live_mask, source_rows, 0)

    partial_value = lax.fori_loop(0, round_count, one_round, empty_sum)
    partial_value = partial_value.reshape(dst_blocks * tile_edge, feat_width)
    summed = lax.psum_scatter(partial_value, "rep", scatter_dimension=0, tiled=True)
    neighbours = (summed / jnp.sqrt(degree.astype(jnp.float32))[:, None]).astype(jnp.bfloat16)
    mixed = jnp.dot(features, w_self, preferred_element_type=jnp.float32)
    mixed = mixed + jnp.dot(neighbours, w_neigh, preferred_element_type=jnp.float32)
    mixed = mixed + out_bias[None, :]
    return jnp.maximum(mixed, 0.0).astype(jnp.bfloat16)


def solution(mesh):
    in_specs = (
        P(("rep", "row"), None),
        P(("rep", "row"), None, None),
        P(("rep", "row")),
        P(("rep", "row")),
        P(("rep", "row")),
        P(("rep", "row")),
        P(),
        P(),
        P(),
    )
    out_specs = P(("rep", "row"), None)
    return jax.shard_map(
        on_device, mesh=mesh, in_specs=in_specs, out_specs=out_specs, check_vma=False
    )
```

profile of v0, /device:TPU:0, one launch (start us, length us, event | category | flops | bytes accessed | tf_op | source)
XLA Modules:
  0.0 484.6 jit_solution(4216031191703694160)
XLA Ops:
  6.5 0.0 copy-start
  6.5 0.0 all-gather.2.cloned.1.call-start
  6.5 0.7 all-gather.2.cloned.1.call-update
  7.3 0.0 reduce-scatter.2.cloned.1.call-start
  8.0 110.3 %all-gather.2.cloned.1.call-done = bf16[32768,256]{1,0:T(8,128)(2,1)} async-done(((bf16[512,256]{1,0:T(8,128)(2,1)}), bf16[32768,256]{1,0:T(8,128)(2,1)}) %all-gather.2.cloned.1.call-update) | async-done | bytes 16777232 | tf_op jit(solution)/shard_map/all_gather | solution.py:41
  118.2 0.1 broadcast_in_dim.29
  118.3 0.0 copy-start.3
  118.3 0.0 copy-start.2
  118.3 0.0 copy-start.4
  118.4 0.0 copy-start.5
  118.4 152.6 %while.10 = (s32[]{:T(128)}, f32[8,128,256]{2,1,0:T(8,128)S(1)}, s32[]{:T(128)}, s32[704]{0:T(1024)}, s32[]{:T(128)}, /*index=5*/bf16[704,128,128]{2,1,0:T(8,128...) while((s32[]{:T(128)}, f32[8,128,256]{2,1,0:T(8,128)S(1)}, ...), condition=%wide.region_2.3_spmd, body=%wide.region_0.2_spmd.sunk | while | flops 543164160 | bytes 48240824 | solution.py:51
  118.4 1.5 compare_and_fusion.2
  119.9 8.5 %gather_fusion = bf16[64,128,256]{2,1,0:T(8,128)(2,1)} fusion(bf16[256,128,256]{2,1,0:T(8,128)(2,1)} %get-tuple-element.155, s32[1024]{0:T(1024)S(1)} %pad_clamp_fusion.2), kind=kCustom, calls=%fused_computation.clone.1 | custom fusion | bytes 8388864 | tf_op jit(solution)/shard_map/while/body/jit(_take)/gather | solution.py:15
  128.4 7.4 %broadcast_select_fusion.2 = f32[64,128,256]{2,1,0:T(8,128)} fusion(pred[64]{0:T(512)(128)(4,1)S(1)} %get-tuple-element.121, bf16[64,128,256]{2,1,0:T(8,128)(2,1)} %gather_fusion, pred[64]{0:T(512)(128)(4,1)S(1)} %get-tuple-element.123, bf16[704,128,128]{2,1,0:T(8,128)(2,1)} %get-tuple-element.153, s32[]{:T(128)S(6)} %select_n.42), kind=kOutput, calls=%fused_computation.2.clone.1 | convolution fusion | flops 541065216 | bytes 14680196 | tf_op jit(solution)/shard_map/while/body/tij,tjh->tih/dot_general | solution.py:16
  135.8 0.8 compare_select_fusion.4
  136.6 12.4 %scatter_fusion = f32[8,128,256]{2,1,0:T(8,128)S(1)} fusion(f32[8,128,256]{2,1,0:T(8,128)S(1)} %get-tuple-element.137, s32[64]{0:T(128)S(1)} %compare_select_fusion.4, f32[64,128,256]{2,1,0:T(8,128)} %broadcast_select_fusion.2), kind=kCustom, calls=%fused_computation.1.clone.1 | custom fusion | flops 2097152 | bytes 25166080 | tf_op jit(solution)/shard_map/while/body/scatter-add | solution.py:20
  148.9 1.4 compare_and_fusion.2
  150.4 8.5 %gather_fusion = bf16[64,128,256]{2,1,0:T(8,128)(2,1)} fusion(bf16[256,128,256]{2,1,0:T(8,128)(2,1)} %get-tuple-element.155, s32[1024]{0:T(1024)S(1)} %pad_clamp_fusion.2), kind=kCustom, calls=%fused_computation.clone.1 | custom fusion | bytes 8388864 | tf_op jit(solution)/shard_map/while/body/jit(_take)/gather | solution.py:15
  158.9 7.4 %broadcast_select_fusion.2 = f32[64,128,256]{2,1,0:T(8,128)} fusion(pred[64]{0:T(512)(128)(4,1)S(1)} %get-tuple-element.121, bf16[64,128,256]{2,1,0:T(8,128)(2,1)} %gather_fusion, pred[64]{0:T(512)(128)(4,1)S(1)} %get-tuple-element.123, bf16[704,128,128]{2,1,0:T(8,128)(2,1)} %get-tuple-element.153, s32[]{:T(128)S(6)} %select_n.42), kind=kOutput, calls=%fused_computation.2.clone.1 | convolution fusion | flops 541065216 | bytes 14680196 | tf_op jit(solution)/shard_map/while/body/tij,tjh->tih/dot_general | solution.py:16
  166.3 0.8 compare_select_fusion.4
  167.1 12.4 %scatter_fusion = f32[8,128,256]{2,1,0:T(8,128)S(1)} fusion(f32[8,128,256]{2,1,0:T(8,128)S(1)} %get-tuple-element.137, s32[64]{0:T(128)S(1)} %compare_select_fusion.4, f32[64,128,256]{2,1,0:T(8,128)} %broadcast_select_fusion.2), kind=kCustom, calls=%fused_computation.1.clone.1 | custom fusion | flops 2097152 | bytes 25166080 | tf_op jit(solution)/shard_map/while/body/scatter-add | solution.py:20
  179.5 1.4 compare_and_fusion.2
  180.9 8.5 %gather_fusion = bf16[64,128,256]{2,1,0:T(8,128)(2,1)} fusion(bf16[256,128,256]{2,1,0:T(8,128)(2,1)} %get-tuple-element.155, s32[1024]{0:T(1024)S(1)} %pad_clamp_fusion.2), kind=kCustom, calls=%fused_computation.clone.1 | custom fusion | bytes 8388864 | tf_op jit(solution)/shard_map/while/body/jit(_take)/gather | solution.py:15
  189.4 7.4 %broadcast_select_fusion.2 = f32[64,128,256]{2,1,0:T(8,128)} fusion(pred[64]{0:T(512)(128)(4,1)S(1)} %get-tuple-element.121, bf16[64,128,256]{2,1,0:T(8,128)(2,1)} %gather_fusion, pred[64]{0:T(512)(128)(4,1)S(1)} %get-tuple-element.123, bf16[704,128,128]{2,1,0:T(8,128)(2,1)} %get-tuple-element.153, s32[]{:T(128)S(6)} %select_n.42), kind=kOutput, calls=%fused_computation.2.clone.1 | convolution fusion | flops 541065216 | bytes 14680196 | tf_op jit(solution)/shard_map/while/body/tij,tjh->tih/dot_general | solution.py:16
  196.8 0.8 compare_select_fusion.4
  197.6 12.4 %scatter_fusion = f32[8,128,256]{2,1,0:T(8,128)S(1)} fusion(f32[8,128,256]{2,1,0:T(8,128)S(1)} %get-tuple-element.137, s32[64]{0:T(128)S(1)} %compare_select_fusion.4, f32[64,128,256]{2,1,0:T(8,128)} %broadcast_select_fusion.2), kind=kCustom, calls=%fused_computation.1.clone.1 | custom fusion | flops 2097152 | bytes 25166080 | tf_op jit(solution)/shard_map/while/body/scatter-add | solution.py:20
  210.0 1.4 compare_and_fusion.2
  211.4 8.5 %gather_fusion = bf16[64,128,256]{2,1,0:T(8,128)(2,1)} fusion(bf16[256,128,256]{2,1,0:T(8,128)(2,1)} %get-tuple-element.155, s32[1024]{0:T(1024)S(1)} %pad_clamp_fusion.2), kind=kCustom, calls=%fused_computation.clone.1 | custom fusion | bytes 8388864 | tf_op jit(solution)/shard_map/while/body/jit(_take)/gather | solution.py:15
  219.9 7.4 %broadcast_select_fusion.2 = f32[64,128,256]{2,1,0:T(8,128)} fusion(pred[64]{0:T(512)(128)(4,1)S(1)} %get-tuple-element.121, bf16[64,128,256]{2,1,0:T(8,128)(2,1)} %gather_fusion, pred[64]{0:T(512)(128)(4,1)S(1)} %get-tuple-element.123, bf16[704,128,128]{2,1,0:T(8,128)(2,1)} %get-tuple-element.153, s32[]{:T(128)S(6)} %select_n.42), kind=kOutput, calls=%fused_computation.2.clone.1 | convolution fusion | flops 541065216 | bytes 14680196 | tf_op jit(solution)/shard_map/while/body/tij,tjh->tih/dot_general | solution.py:16
  227.3 0.8 compare_select_fusion.4
  228.1 12.4 %scatter_fusion = f32[8,128,256]{2,1,0:T(8,128)S(1)} fusion(f32[8,128,256]{2,1,0:T(8,128)S(1)} %get-tuple-element.137, s32[64]{0:T(128)S(1)} %compare_select_fusion.4, f32[64,128,256]{2,1,0:T(8,128)} %broadcast_select_fusion.2), kind=kCustom, calls=%fused_computation.1.clone.1 | custom fusion | flops 2097152 | bytes 25166080 | tf_op jit(solution)/shard_map/while/body/scatter-add | solution.py:20
  240.5 1.4 compare_and_fusion.2
  241.9 8.5 %gather_fusion = bf16[64,128,256]{2,1,0:T(8,128)(2,1)} fusion(bf16[256,128,256]{2,1,0:T(8,128)(2,1)} %get-tuple-element.155, s32[1024]{0:T(1024)S(1)} %pad_clamp_fusion.2), kind=kCustom, calls=%fused_computation.clone.1 | custom fusion | bytes 8388864 | tf_op jit(solution)/shard_map/while/body/jit(_take)/gather | solution.py:15
  250.5 7.4 %broadcast_select_fusion.2 = f32[64,128,256]{2,1,0:T(8,128)} fusion(pred[64]{0:T(512)(128)(4,1)S(1)} %get-tuple-element.121, bf16[64,128,256]{2,1,0:T(8,128)(2,1)} %gather_fusion, pred[64]{0:T(512)(128)(4,1)S(1)} %get-tuple-element.123, bf16[704,128,128]{2,1,0:T(8,128)(2,1)} %get-tuple-element.153, s32[]{:T(128)S(6)} %select_n.42), kind=kOutput, calls=%fused_computation.2.clone.1 | convolution fusion | flops 541065216 | bytes 14680196 | tf_op jit(solution)/shard_map/while/body/tij,tjh->tih/dot_general | solution.py:16
  257.8 0.8 compare_select_fusion.4
  258.6 12.4 %scatter_fusion = f32[8,128,256]{2,1,0:T(8,128)S(1)} fusion(f32[8,128,256]{2,1,0:T(8,128)S(1)} %get-tuple-element.137, s32[64]{0:T(128)S(1)} %compare_select_fusion.4, f32[64,128,256]{2,1,0:T(8,128)} %broadcast_select_fusion.2), kind=kCustom, calls=%fused_computation.1.clone.1 | custom fusion | flops 2097152 | bytes 25166080 | tf_op jit(solution)/shard_map/while/body/scatter-add | solution.py:20
  271.0 0.0 copy-start.1
  271.0 1.0 copy-done.1
  272.0 0.0 reduce-scatter.2.cloned.1.call-update
  272.0 0.0 copy-done.3
  272.0 0.0 copy-done
  272.0 0.0 copy-done.2
  272.0 0.2 fusion.13
  272.2 203.5 %reduce-scatter.2.cloned.1.call-done = f32[512,256]{1,0:T(8,128)} async-done(((f32[1024,256]{1,0:T(8,128)}), f32[512,256]{1,0:T(8,128)}) %reduce-scatter.2.cloned.1.call-update) | async-done | bytes 524304 | tf_op jit(solution)/shard_map/reduce_scatter | solution.py:53
  475.7 0.0 copy-done.4
  475.7 0.0 copy-done.5
  475.7 2.0 fusion.11
  (6 shorter events, 0.0 us)
Async XLA Ops:
  6.5 265.5 %copy-start = (bf16[256,256]{1,0:T(8,128)(2,1)S(1)}, bf16[256,256]{1,0:T(8,128)(2,1)}, u32[]{:S(2)}) copy-start(bf16[256,256]{1,0:T(8,128)(2,1)} %param.17) | copy-start | bytes 393220
  6.5 111.7 %all-gather.2.cloned.1.call-start = ((), (), s32[]{:S(2)}) async-start(), calls=%async_computation.1 | async-start | bytes 17039360 | tf_op jit(solution)/shard_map/all_gather | solution.py:41
  7.3 468.5 %reduce-scatter.2.cloned.1.call-start = ((), (), s32[]{:S(2)}) async-start(), calls=%async_computation.2 | async-start | bytes 1572864 | tf_op jit(solution)/shard_map/reduce_scatter | solution.py:53
  118.3 153.7 %copy-start.3 = (s32[512]{0:T(512)S(1)}, s32[512]{0:T(512)}, u32[]{:S(2)}) copy-start(s32[512]{0:T(512)} %param.16) | copy-start | bytes 6148
  118.3 153.7 %copy-start.2 = (bf16[512,256]{1,0:T(8,128)(2,1)S(1)}, bf16[512,256]{1,0:T(8,128)(2,1)}, u32[]{:S(2)}) copy-start(bf16[512,256]{1,0:T(8,128)(2,1)} %param.11) | copy-start | bytes 786436
  118.3 357.4 %copy-start.4 = (bf16[256,256]{1,0:T(8,128)(2,1)S(1)}, bf16[256,256]{1,0:T(8,128)(2,1)}, u32[]{:S(2)}) copy-start(bf16[256,256]{1,0:T(8,128)(2,1)} %param.18) | copy-start | bytes 393220
  118.4 357.4 %copy-start.5 = (f32[256]{0:T(256)S(1)}, f32[256]{0:T(256)}, u32[]{:S(2)}) copy-start(f32[256]{0:T(256)} %param.19) | copy-start | bytes 3076
  271.0 1.0 copy-start.1
Sparse Core Ops, SparseCore 0:
  10.7 107.4 all-gather.1
  272.1 203.5 reduce-scatter.1
where the time goes:
time: 488 us; the launch traced here: 485 us
  waiting for transfers between devices  314 us (64%)
  other arithmetic  72.8 us (15%)
  local copies, waits for them, and re-layouts  43.8 us (9%)
  matrix products  39.2 us (8%)
  between operations  14.2 us (3%)
    reduce_scatter x1, waiting for transfers between devices, on_device(): lax.psum_scatter(partial_value, 'rep', scatter_dimension=0, tiled=True)  203 us
    all_gather x1, waiting for transfers between devices, on_device(): gathered = lax.all_gather(features, 'row', axis=0, tiled=True)  110 us
    scatter-add x5, other arithmetic, tile_products(): return running.at[dst_block].add(products)  61.8 us
    gather x5, local copies, waits for them, and re-layouts, tile_products(): neighbour_rows = jnp.take(source_rows, picked, axis=0)  42.7 us
    dot_general x5, matrix products, tile_products(): jnp.einsum('tij,tjh->tih', tile_block, neighbour_rows, preferred_element_...  36.9 us
  transfers between devices with their start and end apart: 2, of which 2 were waited for; matrix products, arithmetic and copies ran while one was open for 0% of the time, Pallas kernels for 0%

commit v1 on v0

v1 whole, which is shorter than its diff:
```python
import functools

import jax
import jax.numpy as jnp
from jax import lax
from jax.experimental import pallas as pl
from jax.experimental.pallas import tpu as pltpu
from jax.sharding import PartitionSpec as P

Y, X, Z, C = 4, 2, 4, 2
DEV_ROWS = 512
DEV_BLOCKS = 4
DSTS = 8
STEP = 2 * DSTS
SRC_BITS = 9
ZERO_BLOCK = 256
RING = 6
PHASE_STEPS = (48, 32, 32, 16)
PHASE_BASE = tuple(STEP * sum(PHASE_STEPS[:i]) for i in range(4))
SLOTS = STEP * sum(PHASE_STEPS)
LINE = (0, -1, 1, 2)


def row_id(y, x, z, c):
    return ((y % Y * X + x % X) * Z + z % Z) * C + c % C


def shift(y=(0, 0), x=0, z=(0, 0), c=0):
    return [
        (row_id(i, j, k, m), row_id(i + y[m], j + x, k + z[m], m + c))
        for i in range(Y) for j in range(X) for k in range(Z) for m in range(C)
    ]


def along_first(step):
    return shift(y=(step, 0), z=(0, step))


def along_second(step):
    return shift(y=(0, step), z=(step, 0))


def send(rows, pairs):
    return lax.ppermute(rows, "row", pairs)


def line_of(plane, second, places=LINE):
    return [(plane, first, second) for first in places]


def own_pieces(features):
    head, tail = LINE[:2], LINE[2:]
    from_minus = send(features, along_first(1))
    from_plus = send(features, along_first(-1))
    from_far = send(features, along_first(2))
    across = send(features, shift(x=1))
    from_minus, from_plus, from_far, across = lax.optimization_barrier(
        (from_minus, from_plus, from_far, across)
    )
    line = jnp.concatenate([features, from_minus, from_plus, from_far])
    minus = send(line, along_second(1))
    plus = send(line, along_second(-1))
    rest = send(line[DEV_ROWS:], shift(x=1))
    minus, plus = lax.optimization_barrier((minus, plus))
    far_head = send(minus[: 2 * DEV_ROWS], along_second(1))
    far_tail = send(plus[2 * DEV_ROWS :], along_second(-1))
    rest, _, _ = lax.optimization_barrier((rest, minus, plus))
    other = jnp.concatenate([across, rest])
    other_minus = send(other, along_second(1))
    other_plus = send(other, along_second(-1))
    other_head = send(other_minus[: 2 * DEV_ROWS], along_second(1))
    other_tail = send(other_plus[2 * DEV_ROWS :], along_second(-1))
    return (
        ((line, line_of(0, 0)), (minus, line_of(0, -1)), (plus, line_of(0, 1))),
        ((far_head, line_of(0, 2, head)), (far_tail, line_of(0, 2, tail)), (other, line_of(1, 0))),
        ((other_minus, line_of(1, -1)), (other_plus, line_of(1, 1))),
        ((other_head, line_of(1, 2, head)), (other_tail, line_of(1, 2, tail))),
    )


def owners(places, row, core):
    y, x, z = row // (X * Z * C), row // (Z * C) % X, row // C % Z
    found = []
    for plane, first, second in places:
        dy = jnp.where(core == 0, first, second)
        dz = jnp.where(core == 0, second, first)
        found.append(row_id(y + dy, x + plane, z + dz, core))
    return found


def phase_of(source, row):
    y, x, z = row // (X * Z * C), row // (Z * C) % X, row // C % Z
    dy = (source // (X * Z * C) - y) % Y
    dz = (source // C % Z - z) % Z
    second = jnp.where(source % C == 0, dz, dy)
    near = source // (Z * C) % X == x
    return jnp.where(
        near,
        jnp.where(second == 2, 1, 0),
        jnp.where(second == 0, 1, jnp.where(second == 2, 3, 2)),
    )


def work_list(tile_dst, tile_src, live_tiles, row):
    tiles = jnp.arange(tile_src.shape[0], dtype=jnp.int32)
    live = tiles < live_tiles
    phase = phase_of(tile_src // DEV_BLOCKS, row)
    key = jnp.where(live, phase * DSTS + tile_dst, -1)
    ahead = (key[:, None] == key[None, :]) & (tiles[None, :] < tiles[:, None])
    rank = jnp.sum(ahead.astype(jnp.int32), axis=1)
    base = jnp.where(
        phase == 0,
        PHASE_BASE[0],
        jnp.where(phase == 1, PHASE_BASE[1], jnp.where(phase == 2, PHASE_BASE[2], PHASE_BASE[3])),
    )
    place = jnp.where(live, base + rank // 2 * STEP + tile_dst * 2 + rank % 2, -1)
    value = (tiles << SRC_BITS) + tile_src - ZERO_BLOCK
    hit = place[None, :] == jnp.arange(SLOTS, dtype=jnp.int32)[:, None]
    listed = jnp.sum(jnp.where(hit, value[None, :], 0), axis=1) + ZERO_BLOCK
    buckets = jnp.arange(len(PHASE_STEPS) * DSTS, dtype=jnp.int32)
    counts = jnp.sum((key[None, :] == buckets[:, None]).astype(jnp.int32), axis=1)
    steps = jnp.max((counts.reshape(len(PHASE_STEPS), DSTS) + 1) // 2, axis=1)
    return listed, steps


def phase_kernel(phase, counts, spots, first, last, meta, tiles, *refs):
    pieces = refs[: len(counts)]
    refs = refs[len(counts) :]
    if not first:
        before, refs = refs[0], refs[1:]
    near, away, fbuf, ring, acc, fsem, tsem = refs
    steps = meta[SLOTS + 64 + phase]
    half = meta[SLOTS + 64 + 4]
    arrivals = []
    for piece, count, spot in zip(pieces, counts, spots):
        for i in range(count):
            arrivals.append(
                pltpu.make_async_copy(
                    piece.at[pl.ds(i * DEV_BLOCKS, DEV_BLOCKS)],
                    fbuf.at[pl.ds(meta[SLOTS + spot + i] * DEV_BLOCKS, DEV_BLOCKS)],
                    fsem,
                )
            )
    for copy in arrivals:
        copy.start()

    def fetch(step):
        slot = lax.rem(step, RING)
        for i in range(STEP):
            tile = meta[PHASE_BASE[phase] + step * STEP + i] >> SRC_BITS
            pltpu.make_async_copy(tiles.at[tile], ring.at[slot, i], tsem.at[slot]).start()

    def prime(step, carry):
        fetch(step)
        return carry

    lax.fori_loop(0, jnp.minimum(steps, RING), prime, 0)
    fbuf[ZERO_BLOCK] = jnp.zeros(fbuf.shape[1:], fbuf.dtype)
    acc[...] = jnp.zeros_like(acc)
    if not first:
        if last:
            acc[pl.ds(half * DEV_BLOCKS, DEV_BLOCKS)] = before[...]
        else:
            acc[...] = before[...]
    for copy in arrivals:
        copy.wait()

    def run(step, carry):
        slot = lax.rem(step, RING)
        pltpu.make_async_copy(tiles.at[pl.ds(0, STEP)], ring.at[slot], tsem.at[slot]).wait()
        for d in range(DSTS):
            entry = PHASE_BASE[phase] + step * STEP + 2 * d
            blocks = [fbuf[meta[entry + i] & ((1 << SRC_BITS) - 1)] for i in range(2)]
            left = jnp.concatenate([ring[slot, 2 * d], ring[slot, 2 * d + 1]], axis=1)
            acc[d] += jnp.dot(left, jnp.concatenate(blocks, axis=0), preferred_element_type=jnp.float32)

        @pl.when(step + RING < steps)
        def _():
            fetch(step + RING)

        return carry

    lax.fori_loop(0, steps, run, 0)
    if away is not None:
        near[...] = acc[pl.ds(half * DEV_BLOCKS, DEV_BLOCKS)]
        away[...] = acc[pl.ds((1 - half) * DEV_BLOCKS, DEV_BLOCKS)].astype(away.dtype)
    else:
        near[...] = acc[...]


def run_phase(phase, meta, tiles, pieces, counts, spots, before):
    first, last = phase == 0, phase == 3
    whole = (DSTS,) + (128, 256)
    part = (DEV_BLOCKS,) + (128, 256)
    vmem = pl.BlockSpec(memory_space=pltpu.VMEM)
    anyspace = pl.BlockSpec(memory_space=pl.ANY)
    split = phase >= 2
    if split:
        out_shape = (
            jax.ShapeDtypeStruct(part, jnp.float32),
            jax.ShapeDtypeStruct(part, jnp.bfloat16 if last else jnp.float32),
        )
    else:
        out_shape = (jax.ShapeDtypeStruct(whole, jnp.float32),)

    def body(*refs):
        refs = list(refs)
        if not split:
            refs.insert(len(refs) - 5, None)
        phase_kernel(phase, counts, spots, first, last, *refs)

    slots = STEP * PHASE_STEPS[phase]
    return pl.pallas_call(
        body,
        out_shape=out_shape,
        grid_spec=pltpu.PrefetchScalarGridSpec(
            num_scalar_prefetch=1,
            grid=(),
            in_specs=[anyspace] * (1 + len(pieces)) + ([] if first else [vmem]),
            out_specs=(vmem,) * len(out_shape),
            scratch_shapes=[
                pltpu.VMEM((ZERO_BLOCK + 1, 128, 256), jnp.bfloat16),
                pltpu.VMEM((RING, STEP, 128, 128), jnp.bfloat16),
                pltpu.VMEM(whole, jnp.float32),
                pltpu.SemaphoreType.DMA(()),
                pltpu.SemaphoreType.DMA((RING,)),
            ],
        ),
        compiler_params=pltpu.CompilerParams(vmem_limit_bytes=28 << 20),
        cost_estimate=pl.CostEstimate(
            flops=slots * 128 * 128 * 256, bytes_accessed=slots * 8 * 1024, transcendentals=0
        ),
        name="phase",
    )(meta, tiles, *pieces, *(() if first else (before,)))


def on_device(
    features, tile_vals, tile_dst, tile_src, tile_count, degree, w_self, w_neigh, out_bias
):
    row, rep = lax.axis_index("row"), lax.axis_index("rep")
    core = row % C
    phases = own_pieces(features)
    listed, steps = work_list(tile_dst, tile_src, tile_count[0], row)
    table, groups = [], []
    for own in phases:
        pieces, counts, spots = [], [], []
        for sibling in (False, True):
            for rows, places in own:
                spots.append(len(table))
                counts.append(len(places))
                table += owners(places, row, 1 - core if sibling else core)
                rows = send(rows, shift(c=1)) if sibling else rows
                pieces.append(rows.reshape(-1, 128, 256))
        groups.append((pieces, counts, spots))
    meta = jnp.concatenate([listed, jnp.stack(table), steps, rep[None]]).astype(jnp.int32)

    total = None
    for phase, (pieces, counts, spots) in enumerate(groups):
        if phase == 3:
            total, away = total
            early = lax.ppermute(away, "rep", [(0, 1), (1, 0)])
            total, away = run_phase(phase, meta, tile_vals, pieces, counts, spots, total)
            late = lax.ppermute(away, "rep", [(0, 1), (1, 0)])
        else:
            total = run_phase(phase, meta, tile_vals, pieces, counts, spots, total)
            if phase < 2:
                total = total[0]
    summed = (total + early + late.astype(jnp.float32)).reshape(DEV_ROWS, 256)
    neighbours = (summed / jnp.sqrt(degree.astype(jnp.float32))[:, None]).astype(jnp.bfloat16)
    mixed = jnp.dot(features, w_self, preferred_element_type=jnp.float32) + out_bias[None, :]
    mixed = mixed + jnp.dot(neighbours, w_neigh, preferred_element_type=jnp.float32)
    return jnp.maximum(mixed, 0.0).astype(jnp.bfloat16)


def solution(mesh):
    in_specs = (
        P(("rep", "row"), None),
        P(("rep", "row"), None, None),
        P(("rep", "row")),
        P(("rep", "row")),
        P(("rep", "row")),
        P(("rep", "row")),
        P(),
        P(),
        P(),
    )
    out_specs = P(("rep", "row"), None)
    return jax.shard_map(
        on_device, mesh=mesh, in_specs=in_specs, out_specs=out_specs, check_vma=False
    )
```

time: 488 us -> 131 us (0.27)
  the two profiles are of different devices: /device:TPU:0 before, /device:TPU:57 now
where the time goes in v1:
time: 131 us; the launch traced here: 129 us
  starting transfers between devices  50.9 us (39%)
  waiting for transfers between devices  39.1 us (30%)
  local copies, waits for them, and re-layouts  18.5 us (14%)
  Pallas kernels  16.4 us (13%)
  other arithmetic  1.66 us (1%)
  between operations  1.31 us (1%)
    ppermute x23, waiting for transfers between devices, send(): return lax.ppermute(rows, 'row', pairs)  33.2 us
    ppermute x23, starting transfers between devices, send(): return lax.ppermute(rows, 'row', pairs)  26.6 us
    ppermute x1, starting transfers between devices, on_device(): early = lax.ppermute(away, 'rep', [(0, 1), (1, 0)])  16.8 us
    pallas_call x4, Pallas kernels, run_phase(): pl.pallas_call(body, out_shape=out_shape, grid_spec=pltpu.PrefetchScalarG...  16.4 us
    unnamed x28, local copies, waits for them, and re-layouts  12.8 us
    ppermute x1, starting transfers between devices, on_device(): late = lax.ppermute(away, 'rep', [(0, 1), (1, 0)])  7.44 us
    ppermute x1, waiting for transfers between devices, on_device(): late = lax.ppermute(away, 'rep', [(0, 1), (1, 0)])  5.86 us
  transfers between devices with their start and end apart: 25, of which 10 were waited for; matrix products, arithmetic and copies ran while one was open for 7% of the time, Pallas kernels for 13%

profile of v1, /device:TPU:57, one launch (start us, length us, event | category | flops | bytes accessed | tf_op | source)
XLA Modules:
  0.0 128.9 jit_solution(15885718724814858133)
XLA Ops:
  0.0 1.6 %collective-permute-start = (bf16[512,256]{1,0:T(8,128)(2,1)}, bf16[512,256]{1,0:T(8,128)(2,1)S(1)}, u32[]{:S(2)}, u32[]{:S(2)}) collective-permute-start(bf16[512,256]{1,0:T(8,128)(2,1)} %param.9), channel_id=1, source_target_pairs={{0,16},{1,3},{2,18},{3,5},{4,20},{5,7},{6,22},{7,1},{8,24},{9,11},... | collective-permute-start | bytes 786440 | tf_op jit(solution)/shard_map/ppermute | solution.py:44
  1.6 2.5 %collective-permute-start.2 = (bf16[512,256]{1,0:T(8,128)(2,1)}, bf16[512,256]{1,0:T(8,128)(2,1)S(1)}, u32[]{:S(2)}, u32[]{:S(2)}) collective-permute-start(bf16[512,256]{1,0:T(8,128)(2,1)} %param.9), channel_id=1, source_target_pairs={{0,32},{1,5},{2,34},{3,7},{4,36},{5,1},{6,38},{7,3},{8,40},{9,13},... | collective-permute-start | bytes 786440 | tf_op jit(solution)/shard_map/ppermute | solution.py:44
  4.2 2.7 %collective-permute-start.3 = (bf16[512,256]{1,0:T(8,128)(2,1)}, bf16[512,256]{1,0:T(8,128)(2,1)S(1)}, u32[]{:S(2)}, u32[]{:S(2)}) collective-permute-start(bf16[512,256]{1,0:T(8,128)(2,1)} %param.9), channel_id=1, source_target_pairs={{0,8},{1,9},{2,10},{3,11},{4,12},{5,13},{6,14},{7,15},{8,0},{9,1},... | collective-permute-start | bytes 786440 | tf_op jit(solution)/shard_map/ppermute | solution.py:44
  6.9 1.0 constant_dynamic-update-slice_fusion.3
  7.9 3.3 %collective-permute-done.2 = bf16[512,256]{1,0:T(8,128)(2,1)S(1)} collective-permute-done((bf16[512,256]{1,0:T(8,128)(2,1)}, bf16[512,256]{1,0:T(8,128)(2,1)S(1)}, u32[]{:S(2)}, u32[]{:S(2)}) %collective-permute-start.2) | collective-permute-done | bytes 262176 | tf_op jit(solution)/shard_map/ppermute | solution.py:44
  11.2 2.7 %collective-permute-done.3 = bf16[512,256]{1,0:T(8,128)(2,1)S(1)} collective-permute-done((bf16[512,256]{1,0:T(8,128)(2,1)}, bf16[512,256]{1,0:T(8,128)(2,1)S(1)}, u32[]{:S(2)}, u32[]{:S(2)}) %collective-permute-start.3) | collective-permute-done | bytes 262176 | tf_op jit(solution)/shard_map/ppermute | solution.py:44
  14.1 1.5 %collective-permute-start.6 = (bf16[2048,256]{1,0:T(8,128)(2,1)S(1)}, bf16[2048,256]{1,0:T(8,128)(2,1)S(1)}, u32[]{:S(2)}, u32[]{:S(2)}) collective-permute-start(bf16[2048,256]{1,0:T(8,128)(2,1)S(1)} %constant_dynamic-update-slice_fusion), channel_id=1, source_target_pairs={{0,6},{1,49},{2,0},{3,51},{4,2},{5,53},{6,4},{7,55},{8,14},{9,57},... | collective-permute-start | bytes 3145736 | tf_op jit(solution)/shard_map/ppermute | solution.py:44
  15.6 1.2 collective-permute-start.20
  16.9 2.8 %collective-permute-start.4 = (bf16[1536,256]{1,0:T(8,128)(2,1)S(1)}, bf16[1536,256]{1,0:T(8,128)(2,1)S(1)}, u32[]{:S(2)}, u32[]{:S(2)}) collective-permute-start(bf16[1536,256]{1,0:T(8,128)(2,1)S(1)} %pad_maximum_fusion), channel_id=1, source_target_pairs={{0,8},{1,9},{2,10},{3,11},{4,12},{5,13},{6,14},{7,15},{8,0},{9,1},... | collective-permute-start | bytes 2359304 | tf_op jit(solution)/shard_map/ppermute | solution.py:44
  19.7 8.4 %collective-permute-done.5 = bf16[2048,256]{1,0:T(8,128)(2,1)S(1)} collective-permute-done((bf16[2048,256]{1,0:T(8,128)(2,1)S(1)}, bf16[2048,256]{1,0:T(8,128)(2,1)S(1)}, u32[]{:S(2)}, u32[]{:S(2)}) %collective-permute-start.5) | collective-permute-done | bytes 1048608 | tf_op jit(solution)/shard_map/ppermute | solution.py:44
  28.1 1.3 %collective-permute-done.6 = bf16[2048,256]{1,0:T(8,128)(2,1)S(1)} collective-permute-done((bf16[2048,256]{1,0:T(8,128)(2,1)S(1)}, bf16[2048,256]{1,0:T(8,128)(2,1)S(1)}, u32[]{:S(2)}, u32[]{:S(2)}) %collective-permute-start.6) | collective-permute-done | bytes 1048608 | tf_op jit(solution)/shard_map/ppermute | solution.py:44
  29.4 0.9 slice.16
  30.2 0.8 slice.17
  31.1 1.5 %collective-permute-start.16 = (bf16[1024,256]{1,0:T(8,128)(2,1)}, bf16[1024,256]{1,0:T(8,128)(2,1)}, u32[]{:S(2)}, u32[]{:S(2)}) collective-permute-start(bf16[1024,256]{1,0:T(8,128)(2,1)} %slice.17), channel_id=1, source_target_pairs={{0,6},{1,49},{2,0},{3,51},{4,2},{5,53},{6,4},{7,55},{8,14},{9,57},... | collective-permute-start | bytes 1572872 | tf_op jit(solution)/shard_map/ppermute | solution.py:44
  32.5 0.8 constant_dynamic-update-slice_fusion.5
  33.3 1.7 %collective-permute-start.21 = (bf16[2048,256]{1,0:T(8,128)(2,1)S(1)}, bf16[2048,256]{1,0:T(8,128)(2,1)}, u32[]{:S(2)}, u32[]{:S(2)}) collective-permute-start(bf16[2048,256]{1,0:T(8,128)(2,1)S(1)} %collective-permute-done.5), channel_id=1, source_target_pairs={{0,1},{1,0},{2,3},{3,2},{4,5},{5,4},{6,7},{7,6},{8,9},{9,8},{10,11... | collective-permute-start | bytes 3145736 | tf_op jit(solution)/shard_map/ppermute | solution.py:44
  35.0 2.6 %collective-permute-done.4 = bf16[1536,256]{1,0:T(8,128)(2,1)S(1)} collective-permute-done((bf16[1536,256]{1,0:T(8,128)(2,1)S(1)}, bf16[1536,256]{1,0:T(8,128)(2,1)S(1)}, u32[]{:S(2)}, u32[]{:S(2)}) %collective-permute-start.4) | collective-permute-done | bytes 786464 | tf_op jit(solution)/shard_map/ppermute | solution.py:44
  37.6 1.0 constant_dynamic-update-slice_fusion.4
  38.6 1.0 copy-done.4
  39.6 1.5 %collective-permute-start.9 = (bf16[2048,256]{1,0:T(8,128)(2,1)}, bf16[2048,256]{1,0:T(8,128)(2,1)}, u32[]{:S(2)}, u32[]{:S(2)}) collective-permute-start(bf16[2048,256]{1,0:T(8,128)(2,1)} %constant_dynamic-update-slice_fusion.4), channel_id=1, source_target_pairs={{0,6},{1,49},{2,0},{3,51},{4,2},{5,53},{6,4},{7,55},{8,14},{9,57},... | collective-permute-start | bytes 3145736 | tf_op jit(solution)/shard_map/ppermute | solution.py:44
  41.7 1.4 %collective-permute-start.22 = (bf16[2048,256]{1,0:T(8,128)(2,1)S(1)}, bf16[2048,256]{1,0:T(8,128)(2,1)}, u32[]{:S(2)}, u32[]{:S(2)}) collective-permute-start(bf16[2048,256]{1,0:T(8,128)(2,1)S(1)} %collective-permute-done.6), channel_id=1, source_target_pairs={{0,1},{1,0},{2,3},{3,2},{4,5},{5,4},{6,7},{7,6},{8,9},{9,8},{10,11... | collective-permute-start | bytes 3145736 | tf_op jit(solution)/shard_map/ppermute | solution.py:44
  43.4 0.3 convert_reduce_fusion
  43.8 0.5 collective-permute-start.17
  44.3 8.5 %collective-permute-done.7 = bf16[2048,256]{1,0:T(8,128)(2,1)S(1)} collective-permute-done((bf16[2048,256]{1,0:T(8,128)(2,1)}, bf16[2048,256]{1,0:T(8,128)(2,1)S(1)}, u32[]{:S(2)}, u32[]{:S(2)}) %collective-permute-start.7) | collective-permute-done | bytes 1048608 | tf_op jit(solution)/shard_map/ppermute | solution.py:44
  52.8 1.5 %collective-permute-start.13 = (bf16[2048,256]{1,0:T(8,128)(2,1)S(1)}, bf16[2048,256]{1,0:T(8,128)(2,1)}, u32[]{:S(2)}, u32[]{:S(2)}) collective-permute-start(bf16[2048,256]{1,0:T(8,128)(2,1)S(1)} %collective-permute-done.7), channel_id=1, source_target_pairs={{0,1},{1,0},{2,3},{3,2},{4,5},{5,4},{6,7},{7,6},{8,9},{9,8},{10,11... | collective-permute-start | bytes 3145736 | tf_op jit(solution)/shard_map/ppermute | solution.py:44
  54.4 0.4 collective-permute-done.9
  54.7 1.7 %collective-permute-start.14 = (bf16[2048,256]{1,0:T(8,128)(2,1)}, bf16[2048,256]{1,0:T(8,128)(2,1)}, u32[]{:S(2)}, u32[]{:S(2)}) collective-permute-start(bf16[2048,256]{1,0:T(8,128)(2,1)} %collective-permute-done.9), channel_id=1, source_target_pairs={{0,1},{1,0},{2,3},{3,2},{4,5},{5,4},{6,7},{7,6},{8,9},{9,8},{10,11... | collective-permute-start | bytes 3145736 | tf_op jit(solution)/shard_map/ppermute | solution.py:44
  56.8 0.8 slice.18
  57.6 1.9 %slice.19 = bf16[1024,256]{1,0:T(8,128)(2,1)} slice(bf16[2048,256]{1,0:T(8,128)(2,1)} %collective-permute-done.9), slice={[1024:2048], [0:256]} | slice | bytes 1048576 | tf_op jit(solution)/shard_map/slice | solution.py:72
  59.5 0.3 collective-permute-start.8
  59.8 1.2 collective-permute-start.10
  61.2 0.7 select_reduce_fusion
  61.9 0.5 collective-permute-start.18
  62.6 5.6 %collective-permute-done.8 = bf16[1024,256]{1,0:T(8,128)(2,1)} collective-permute-done((bf16[1024,256]{1,0:T(8,128)(2,1)}, bf16[1024,256]{1,0:T(8,128)(2,1)}, u32[]{:S(2)}, u32[]{:S(2)}) %collective-permute-start.8) | collective-permute-done | bytes 524320 | tf_op jit(solution)/shard_map/ppermute | solution.py:44
  68.2 0.9 collective-permute-start.11
  69.0 0.3 collective-permute-done.10
  69.4 1.4 %collective-permute-start.12 = (bf16[1024,256]{1,0:T(8,128)(2,1)}, bf16[1024,256]{1,0:T(8,128)(2,1)S(1)}, u32[]{:S(2)}, u32[]{:S(2)}) collective-permute-start(bf16[1024,256]{1,0:T(8,128)(2,1)} %collective-permute-done.10), channel_id=1, source_target_pairs={{0,1},{1,0},{2,3},{3,2},{4,5},{5,4},{6,7},{7,6},{8,9},{9,8},{10,11... | collective-permute-start | bytes 1572872 | tf_op jit(solution)/shard_map/ppermute | solution.py:44
  70.8 1.2 copy-done.3
  72.1 1.2 copy-done.5
  73.3 4.6 %phase.4.refs_8_ = f32[8,128,256]{2,1,0:T(8,128)S(1)} custom-call(s32[2117]{0:T(1024)S(1)} %concatenate.12.refs_0_, bf16[704,128,128]{2,1,0:T(8,128)(2,1)} %refs_1_.7, bf16[16,128,256]{2,1,0:T(8,128)(2,1)S(1)} %bitcast.99, bf16[16,128,256]{2,1,0:T(8,128)(2,1)S(1)} %bitcast.96, bf16[16,128,256]{2,1,0:T(8,128)(2,1)S(1)} %bitcast.97, ...), custom_call_target="tpu_custom_call" | custom-call | flops 3221225472 | bytes 6291456 | tf_op jit(solution)/shard_map/phase/pallas_call | solution.py:213
  77.9 4.2 %phase.5.refs_6_ = f32[8,128,256]{2,1,0:T(8,128)S(1)} custom-call(s32[2117]{0:T(1024)S(1)} %concatenate.12.refs_0_, bf16[704,128,128]{2,1,0:T(8,128)(2,1)} %refs_1_.7, bf16[8,128,256]{2,1,0:T(8,128)(2,1)} %bitcast.74.refs_2_, bf16[8,128,256]{2,1,0:T(8,128)(2,1)} %bitcast.75.refs_3_, bf16[16,128,256]{2,1,0:T(8,128)(2,1)} %bitcast.76.refs_4_, ...), custom_call_target="tpu_custom_call" | custom-call | flops 2147483648 | bytes 4194304 | tf_op jit(solution)/shard_map/phase/pallas_call | solution.py:213
  82.2 5.2 %phase.6 = (f32[4,128,256]{2,1,0:T(8,128)S(1)}, f32[4,128,256]{2,1,0:T(8,128)S(1)}) custom-call(s32[2117]{0:T(1024)S(1)} %concatenate.12.refs_0_, bf16[704,128,128]{2,1,0:T(8,128)(2,1)} %refs_1_.7, bf16[16,128,256]{2,1,0:T(8,128)(2,1)S(1)} %bitcast.98, bf16[16,128,256]{2,1,0:T(8,128)(2,1)} %bitcast.71.refs_3_, bf16[16,128,256]{2,1,0:T(8,128)(2,1)} %bitcast.72.refs_4_, ...), custom_call_target="tpu_custom_call" | custom-call | flops 2147483648 | bytes 4194304 | tf_op jit(solution)/shard_map/phase/pallas_call | solution.py:213
  87.4 16.8 %collective-permute-start.23 = (f32[4,128,256]{2,1,0:T(8,128)S(1)}, f32[4,128,256]{2,1,0:T(8,128)S(1)}, u32[]{:S(2)}, u32[]{:S(2)}) collective-permute-start(f32[4,128,256]{2,1,0:T(8,128)S(1)} %get-tuple-element.25), channel_id=1, source_target_pairs={{0,64},{64,0},{1,65},{65,1},{2,66},{66,2},{3,67},{67,3},{4,68},{68... | collective-permute-start | bytes 1572872 | tf_op jit(solution)/shard_map/ppermute | solution.py:261
  104.3 7.6 %copy-done.1 = bf16[704,128,128]{2,1,0:T(8,128)(2,1)S(1)} copy-done((bf16[704,128,128]{2,1,0:T(8,128)(2,1)S(1)}, bf16[704,128,128]{2,1,0:T(8,128)(2,1)}, u32[]{:S(2)}) %copy-start.1) | copy-done | bytes 23068696
  111.8 2.3 %phase.7 = (f32[4,128,256]{2,1,0:T(8,128)S(1)}, bf16[4,128,256]{2,1,0:T(8,128)(2,1)S(1)}) custom-call(s32[2117]{0:T(1024)S(1)} %concatenate.12.refs_0_, bf16[704,128,128]{2,1,0:T(8,128)(2,1)S(1)} %copy-done.1, bf16[8,128,256]{2,1,0:T(8,128)(2,1)} %bitcast.66.refs_2_, bf16[8,128,256]{2,1,0:T(8,128)(2,1)} %bitcast.67.refs_3_, ...), custom_call_target="tpu_custom_call" | custom-call | flops 1073741824 | bytes 2097152 | tf_op jit(solution)/shard_map/phase/pallas_call | solution.py:213
  114.2 7.4 %collective-permute-start.24 = (bf16[4,128,256]{2,1,0:T(8,128)(2,1)S(1)}, bf16[4,128,256]{2,1,0:T(8,128)(2,1)S(1)}, u32[]{:S(2)}, u32[]{:S(2)}) collective-permute-start(bf16[4,128,256]{2,1,0:T(8,128)(2,1)S(1)} %get-tuple-element.26), channel_id=1, source_target_pairs={{0,64},{64,0},{1,65},{65,1},{2,66},{66,2},{3,67},{67,3},{4,68},{68... | collective-permute-start | bytes 786440 | tf_op jit(solution)/shard_map/ppermute | solution.py:263
  121.9 5.9 %collective-permute-done.24 = bf16[4,128,256]{2,1,0:T(8,128)(2,1)S(1)} collective-permute-done((bf16[4,128,256]{2,1,0:T(8,128)(2,1)S(1)}, bf16[4,128,256]{2,1,0:T(8,128)(2,1)S(1)}, u32[]{:S(2)}, u32[]{:S(2)}) %collective-permute-start.24) | collective-permute-done | bytes 262176 | tf_op jit(solution)/shard_map/ppermute | solution.py:263
  128.0 0.9 fusion.2
  (56 shorter events, 1.4 us)
Async XLA Ops:
  0.0 121.6 %copy-start = (bf16[256,256]{1,0:T(8,128)(2,1)S(1)}, bf16[256,256]{1,0:T(8,128)(2,1)}, u32[]{:S(2)}) copy-start(bf16[256,256]{1,0:T(8,128)(2,1)} %param.15) | copy-start | bytes 393220
  0.0 7.9 %collective-permute-start = (bf16[512,256]{1,0:T(8,128)(2,1)}, bf16[512,256]{1,0:T(8,128)(2,1)S(1)}, u32[]{:S(2)}, u32[]{:S(2)}) collective-permute-start(bf16[512,256]{1,0:T(8,128)(2,1)} %param.9), channel_id=1, source_target_pairs={{0,16},{1,3},{2,18},{3,5},{4,20},{5,7},{6,22},{7,1},{8,24},{9,11},... | collective-permute-start | bytes 786440 | tf_op jit(solution)/shard_map/ppermute | solution.py:44
  1.6 6.3 %collective-permute-start.1 = (bf16[512,256]{1,0:T(8,128)(2,1)}, bf16[512,256]{1,0:T(8,128)(2,1)S(1)}, u32[]{:S(2)}, u32[]{:S(2)}) collective-permute-start(bf16[512,256]{1,0:T(8,128)(2,1)} %param.9), channel_id=1, source_target_pairs={{0,48},{1,7},{2,50},{3,1},{4,52},{5,3},{6,54},{7,5},{8,56},{9,15},... | collective-permute-start | bytes 786440 | tf_op jit(solution)/shard_map/ppermute | solution.py:44
  1.6 9.6 %collective-permute-start.2 = (bf16[512,256]{1,0:T(8,128)(2,1)}, bf16[512,256]{1,0:T(8,128)(2,1)S(1)}, u32[]{:S(2)}, u32[]{:S(2)}) collective-permute-start(bf16[512,256]{1,0:T(8,128)(2,1)} %param.9), channel_id=1, source_target_pairs={{0,32},{1,5},{2,34},{3,7},{4,36},{5,1},{6,38},{7,3},{8,40},{9,13},... | collective-permute-start | bytes 786440 | tf_op jit(solution)/shard_map/ppermute | solution.py:44
  4.2 9.8 %collective-permute-start.3 = (bf16[512,256]{1,0:T(8,128)(2,1)}, bf16[512,256]{1,0:T(8,128)(2,1)S(1)}, u32[]{:S(2)}, u32[]{:S(2)}) collective-permute-start(bf16[512,256]{1,0:T(8,128)(2,1)} %param.9), channel_id=1, source_target_pairs={{0,8},{1,9},{2,10},{3,11},{4,12},{5,13},{6,14},{7,15},{8,0},{9,1},... | collective-permute-start | bytes 786440 | tf_op jit(solution)/shard_map/ppermute | solution.py:44
  14.1 24.5 %copy-start.2 = (bf16[2048,256]{1,0:T(8,128)(2,1)}, bf16[2048,256]{1,0:T(8,128)(2,1)S(1)}, u32[]{:S(2)}) copy-start(bf16[2048,256]{1,0:T(8,128)(2,1)S(1)} %constant_dynamic-update-slice_fusion) | copy-start | bytes 3145732
  14.1 14.0 %collective-permute-start.5 = (bf16[2048,256]{1,0:T(8,128)(2,1)S(1)}, bf16[2048,256]{1,0:T(8,128)(2,1)S(1)}, u32[]{:S(2)}, u32[]{:S(2)}) collective-permute-start(bf16[2048,256]{1,0:T(8,128)(2,1)S(1)} %constant_dynamic-update-slice_fusion), channel_id=1, source_target_pairs={{0,2},{1,17},{2,4},{3,19},{4,6},{5,21},{6,0},{7,23},{8,10},{9,25},... | collective-permute-start | bytes 3145736 | tf_op jit(solution)/shard_map/ppermute | solution.py:44
  14.1 15.2 %collective-permute-start.6 = (bf16[2048,256]{1,0:T(8,128)(2,1)S(1)}, bf16[2048,256]{1,0:T(8,128)(2,1)S(1)}, u32[]{:S(2)}, u32[]{:S(2)}) collective-permute-start(bf16[2048,256]{1,0:T(8,128)(2,1)S(1)} %constant_dynamic-update-slice_fusion), channel_id=1, source_target_pairs={{0,6},{1,49},{2,0},{3,51},{4,2},{5,53},{6,4},{7,55},{8,14},{9,57},... | collective-permute-start | bytes 3145736 | tf_op jit(solution)/shard_map/ppermute | solution.py:44
  15.6 23.0 %collective-permute-start.20 = (bf16[2048,256]{1,0:T(8,128)(2,1)S(1)}, bf16[2048,256]{1,0:T(8,128)(2,1)S(1)}, u32[]{:S(2)}, u32[]{:S(2)}) collective-permute-start(bf16[2048,256]{1,0:T(8,128)(2,1)S(1)} %constant_dynamic-update-slice_fusion), channel_id=1, source_target_pairs={{0,1},{1,0},{2,3},{3,2},{4,5},{5,4},{6,7},{7,6},{8,9},{9,8},{10,11... | collective-permute-start | bytes 3145736 | tf_op jit(solution)/shard_map/ppermute | solution.py:44
  16.8 26.4 %copy-start.8 = (s32[704]{0:T(1024)S(1)}, s32[704]{0:T(1024)}, u32[]{:S(2)}) copy-start(s32[704]{0:T(1024)} %param.11) | copy-start | bytes 8452
  16.9 26.4 %copy-start.9 = (s32[704]{0:T(1024)S(1)}, s32[704]{0:T(1024)}, u32[]{:S(2)}) copy-start(s32[704]{0:T(1024)} %param.12) | copy-start | bytes 8452
  16.9 20.8 %collective-permute-start.4 = (bf16[1536,256]{1,0:T(8,128)(2,1)S(1)}, bf16[1536,256]{1,0:T(8,128)(2,1)S(1)}, u32[]{:S(2)}, u32[]{:S(2)}) collective-permute-start(bf16[1536,256]{1,0:T(8,128)(2,1)S(1)} %pad_maximum_fusion), channel_id=1, source_target_pairs={{0,8},{1,9},{2,10},{3,11},{4,12},{5,13},{6,14},{7,15},{8,0},{9,1},... | collective-permute-start | bytes 2359304 | tf_op jit(solution)/shard_map/ppermute | solution.py:44
  30.2 11.5 %collective-permute-start.15 = (bf16[1024,256]{1,0:T(8,128)(2,1)}, bf16[1024,256]{1,0:T(8,128)(2,1)}, u32[]{:S(2)}, u32[]{:S(2)}) collective-permute-start(bf16[1024,256]{1,0:T(8,128)(2,1)} %slice.16), channel_id=1, source_target_pairs={{0,2},{1,17},{2,4},{3,19},{4,6},{5,21},{6,0},{7,23},{8,10},{9,25},... | collective-permute-start | bytes 1572872 | tf_op jit(solution)/shard_map/ppermute | solution.py:44
  31.1 12.1 %collective-permute-start.16 = (bf16[1024,256]{1,0:T(8,128)(2,1)}, bf16[1024,256]{1,0:T(8,128)(2,1)}, u32[]{:S(2)}, u32[]{:S(2)}) collective-permute-start(bf16[1024,256]{1,0:T(8,128)(2,1)} %slice.17), channel_id=1, source_target_pairs={{0,6},{1,49},{2,0},{3,51},{4,2},{5,53},{6,4},{7,55},{8,14},{9,57},... | collective-permute-start | bytes 1572872 | tf_op jit(solution)/shard_map/ppermute | solution.py:44
  33.3 10.5 %collective-permute-start.21 = (bf16[2048,256]{1,0:T(8,128)(2,1)S(1)}, bf16[2048,256]{1,0:T(8,128)(2,1)}, u32[]{:S(2)}, u32[]{:S(2)}) collective-permute-start(bf16[2048,256]{1,0:T(8,128)(2,1)S(1)} %collective-permute-done.5), channel_id=1, source_target_pairs={{0,1},{1,0},{2,3},{3,2},{4,5},{5,4},{6,7},{7,6},{8,9},{9,8},{10,11... | collective-permute-start | bytes 3145736 | tf_op jit(solution)/shard_map/ppermute | solution.py:44
  38.6 14.3 %collective-permute-start.7 = (bf16[2048,256]{1,0:T(8,128)(2,1)}, bf16[2048,256]{1,0:T(8,128)(2,1)S(1)}, u32[]{:S(2)}, u32[]{:S(2)}) collective-permute-start(bf16[2048,256]{1,0:T(8,128)(2,1)} %constant_dynamic-update-slice_fusion.4), channel_id=1, source_target_pairs={{0,2},{1,17},{2,4},{3,19},{4,6},{5,21},{6,0},{7,23},{8,10},{9,25},... | collective-permute-start | bytes 3145736 | tf_op jit(solution)/shard_map/ppermute | solution.py:44
  38.6 1.0 copy-start.4
  39.6 15.2 %collective-permute-start.9 = (bf16[2048,256]{1,0:T(8,128)(2,1)}, bf16[2048,256]{1,0:T(8,128)(2,1)}, u32[]{:S(2)}, u32[]{:S(2)}) collective-permute-start(bf16[2048,256]{1,0:T(8,128)(2,1)} %constant_dynamic-update-slice_fusion.4), channel_id=1, source_target_pairs={{0,6},{1,49},{2,0},{3,51},{4,2},{5,53},{6,4},{7,55},{8,14},{9,57},... | collective-permute-start | bytes 3145736 | tf_op jit(solution)/shard_map/ppermute | solution.py:44
  41.7 17.8 %collective-permute-start.22 = (bf16[2048,256]{1,0:T(8,128)(2,1)S(1)}, bf16[2048,256]{1,0:T(8,128)(2,1)}, u32[]{:S(2)}, u32[]{:S(2)}) collective-permute-start(bf16[2048,256]{1,0:T(8,128)(2,1)S(1)} %collective-permute-done.6), channel_id=1, source_target_pairs={{0,1},{1,0},{2,3},{3,2},{4,5},{5,4},{6,7},{7,6},{8,9},{9,8},{10,11... | collective-permute-start | bytes 3145736 | tf_op jit(solution)/shard_map/ppermute | solution.py:44
  43.1 16.7 %collective-permute-start.19 = (bf16[2048,256]{1,0:T(8,128)(2,1)}, bf16[2048,256]{1,0:T(8,128)(2,1)}, u32[]{:S(2)}, u32[]{:S(2)}) collective-permute-start(bf16[2048,256]{1,0:T(8,128)(2,1)} %constant_dynamic-update-slice_fusion.4), channel_id=1, source_target_pairs={{0,1},{1,0},{2,3},{3,2},{4,5},{5,4},{6,7},{7,6},{8,9},{9,8},{10,11... | collective-permute-start | bytes 3145736 | tf_op jit(solution)/shard_map/ppermute | solution.py:44
  43.8 18.1 %collective-permute-start.17 = (bf16[1024,256]{1,0:T(8,128)(2,1)}, bf16[1024,256]{1,0:T(8,128)(2,1)}, u32[]{:S(2)}, u32[]{:S(2)}) collective-permute-start(bf16[1024,256]{1,0:T(8,128)(2,1)} %collective-permute-done.15), channel_id=1, source_target_pairs={{0,1},{1,0},{2,3},{3,2},{4,5},{5,4},{6,7},{7,6},{8,9},{9,8},{10,11... | collective-permute-start | bytes 1572872 | tf_op jit(solution)/shard_map/ppermute | solution.py:44
  52.8 29.3 %collective-permute-start.13 = (bf16[2048,256]{1,0:T(8,128)(2,1)S(1)}, bf16[2048,256]{1,0:T(8,128)(2,1)}, u32[]{:S(2)}, u32[]{:S(2)}) collective-permute-start(bf16[2048,256]{1,0:T(8,128)(2,1)S(1)} %collective-permute-done.7), channel_id=1, source_target_pairs={{0,1},{1,0},{2,3},{3,2},{4,5},{5,4},{6,7},{7,6},{8,9},{9,8},{10,11... | collective-permute-start | bytes 3145736 | tf_op jit(solution)/shard_map/ppermute | solution.py:44
  54.7 27.4 %collective-permute-start.14 = (bf16[2048,256]{1,0:T(8,128)(2,1)}, bf16[2048,256]{1,0:T(8,128)(2,1)}, u32[]{:S(2)}, u32[]{:S(2)}) collective-permute-start(bf16[2048,256]{1,0:T(8,128)(2,1)} %collective-permute-done.9), channel_id=1, source_target_pairs={{0,1},{1,0},{2,3},{3,2},{4,5},{5,4},{6,7},{7,6},{8,9},{9,8},{10,11... | collective-permute-start | bytes 3145736 | tf_op jit(solution)/shard_map/ppermute | solution.py:44
  59.5 8.6 %collective-permute-start.8 = (bf16[1024,256]{1,0:T(8,128)(2,1)}, bf16[1024,256]{1,0:T(8,128)(2,1)}, u32[]{:S(2)}, u32[]{:S(2)}) collective-permute-start(bf16[1024,256]{1,0:T(8,128)(2,1)} %slice.18), channel_id=1, source_target_pairs={{0,2},{1,17},{2,4},{3,19},{4,6},{5,21},{6,0},{7,23},{8,10},{9,25},... | collective-permute-start | bytes 1572872 | tf_op jit(solution)/shard_map/ppermute | solution.py:44
  59.8 9.6 %collective-permute-start.10 = (bf16[1024,256]{1,0:T(8,128)(2,1)}, bf16[1024,256]{1,0:T(8,128)(2,1)}, u32[]{:S(2)}, u32[]{:S(2)}) collective-permute-start(bf16[1024,256]{1,0:T(8,128)(2,1)} %slice.19), channel_id=1, source_target_pairs={{0,6},{1,49},{2,0},{3,51},{4,2},{5,53},{6,4},{7,55},{8,14},{9,57},... | collective-permute-start | bytes 1572872 | tf_op jit(solution)/shard_map/ppermute | solution.py:44
  61.9 16.0 %collective-permute-start.18 = (bf16[1024,256]{1,0:T(8,128)(2,1)}, bf16[1024,256]{1,0:T(8,128)(2,1)}, u32[]{:S(2)}, u32[]{:S(2)}) collective-permute-start(bf16[1024,256]{1,0:T(8,128)(2,1)} %collective-permute-done.16), channel_id=1, source_target_pairs={{0,1},{1,0},{2,3},{3,2},{4,5},{5,4},{6,7},{7,6},{8,9},{9,8},{10,11... | collective-permute-start | bytes 1572872 | tf_op jit(solution)/shard_map/ppermute | solution.py:44
  68.2 36.1 %collective-permute-start.11 = (bf16[1024,256]{1,0:T(8,128)(2,1)}, bf16[1024,256]{1,0:T(8,128)(2,1)S(1)}, u32[]{:S(2)}, u32[]{:S(2)}) collective-permute-start(bf16[1024,256]{1,0:T(8,128)(2,1)} %collective-permute-done.8), channel_id=1, source_target_pairs={{0,1},{1,0},{2,3},{3,2},{4,5},{5,4},{6,7},{7,6},{8,9},{9,8},{10,11... | collective-permute-start | bytes 1572872 | tf_op jit(solution)/shard_map/ppermute | solution.py:44
  69.4 34.9 %collective-permute-start.12 = (bf16[1024,256]{1,0:T(8,128)(2,1)}, bf16[1024,256]{1,0:T(8,128)(2,1)S(1)}, u32[]{:S(2)}, u32[]{:S(2)}) collective-permute-start(bf16[1024,256]{1,0:T(8,128)(2,1)} %collective-permute-done.10), channel_id=1, source_target_pairs={{0,1},{1,0},{2,3},{3,2},{4,5},{5,4},{6,7},{7,6},{8,9},{9,8},{10,11... | collective-permute-start | bytes 1572872 | tf_op jit(solution)/shard_map/ppermute | solution.py:44
  70.8 1.2 copy-start.3
  72.1 1.2 copy-start.5
  87.4 40.3 %collective-permute-start.23 = (f32[4,128,256]{2,1,0:T(8,128)S(1)}, f32[4,128,256]{2,1,0:T(8,128)S(1)}, u32[]{:S(2)}, u32[]{:S(2)}) collective-permute-start(f32[4,128,256]{2,1,0:T(8,128)S(1)} %get-tuple-element.25), channel_id=1, source_target_pairs={{0,64},{64,0},{1,65},{65,1},{2,66},{66,2},{3,67},{67,3},{4,68},{68... | collective-permute-start | bytes 1572872 | tf_op jit(solution)/shard_map/ppermute | solution.py:261
  104.3 7.6 %copy-start.1 = (bf16[704,128,128]{2,1,0:T(8,128)(2,1)S(1)}, bf16[704,128,128]{2,1,0:T(8,128)(2,1)}, u32[]{:S(2)}) copy-start(bf16[704,128,128]{2,1,0:T(8,128)(2,1)} %refs_1_.7) | copy-start | bytes 69206016
  111.8 9.8 %copy-start.10 = (s32[512]{0:T(512)S(1)}, s32[512]{0:T(512)}, u32[]{:S(2)}) copy-start(s32[512]{0:T(512)} %param.14) | copy-start | bytes 6148
  111.8 9.8 %copy-start.6 = (bf16[512,256]{1,0:T(8,128)(2,1)S(1)}, bf16[512,256]{1,0:T(8,128)(2,1)}, u32[]{:S(2)}) copy-start(bf16[512,256]{1,0:T(8,128)(2,1)} %param.9) | copy-start | bytes 786436
  111.8 9.8 %copy-start.11 = (f32[256]{0:T(256)S(1)}, f32[256]{0:T(256)}, u32[]{:S(2)}) copy-start(f32[256]{0:T(256)} %param.17) | copy-start | bytes 3076
  114.1 13.8 %copy-start.7 = (bf16[256,256]{1,0:T(8,128)(2,1)S(1)}, bf16[256,256]{1,0:T(8,128)(2,1)}, u32[]{:S(2)}) copy-start(bf16[256,256]{1,0:T(8,128)(2,1)} %param.16) | copy-start | bytes 393220
  114.2 13.6 %collective-permute-start.24 = (bf16[4,128,256]{2,1,0:T(8,128)(2,1)S(1)}, bf16[4,128,256]{2,1,0:T(8,128)(2,1)S(1)}, u32[]{:S(2)}, u32[]{:S(2)}) collective-permute-start(bf16[4,128,256]{2,1,0:T(8,128)(2,1)S(1)} %get-tuple-element.26), channel_id=1, source_target_pairs={{0,64},{64,0},{1,65},{65,1},{2,66},{66,2},{3,67},{67,3},{4,68},{68... | collective-permute-start | bytes 786440 | tf_op jit(solution)/shard_map/ppermute | solution.py:263

commit v2 on v0

v2 whole, which is shorter than its diff:
```python
import functools

import jax
import jax.numpy as jnp
from jax import lax
from jax.experimental import pallas as pl
from jax.experimental.pallas import tpu as pltpu
from jax.sharding import PartitionSpec as P

Y, X, Z, C = 4, 2, 4, 2
DEV_ROWS = 512
DEV_BLOCKS = 4
DSTS = 8
DEPTH = 4
STEP = DEPTH * DSTS
BLOCK_BITS = 9
OWNER_TILES = DEV_BLOCKS * DSTS
CHUNK = 16
GROUP = 8
PHASE_GROUPS = (1, 3, 3, 1)
GROUP_BASE = tuple(sum(PHASE_GROUPS[:i]) for i in range(4))
GROUPS = sum(PHASE_GROUPS)
GROUP_STEPS = GROUP * DEV_BLOCKS // DEPTH
SLOTS = STEP * GROUP_STEPS * GROUPS
OWNERS = GROUP * GROUPS
STARTS, FILLS = SLOTS, SLOTS + OWNERS
STEPS_AT = FILLS + OWNERS
HALF_AT = STEPS_AT + GROUPS
SPLIT = (1, 3)
VMEM_BYTES = 44 << 20
LINE = (0, -1, 1, 2)
HEAD, TAIL = LINE[:2], LINE[2:]


def row_id(y, x, z, c):
    return ((y % Y * X + x % X) * Z + z % Z) * C + c % C


def shift(y=(0, 0), x=0, z=(0, 0), c=0):
    return [
        (row_id(i, j, k, m), row_id(i + y[m], j + x, k + z[m], m + c))
        for i in range(Y) for j in range(X) for k in range(Z) for m in range(C)
    ]


def along_first(step):
    return shift(y=(step, 0), z=(0, step))


def along_second(step):
    return shift(y=(0, step), z=(step, 0))


def send(rows, pairs):
    return lax.ppermute(rows, "row", pairs)


def line_of(plane, second, places=LINE):
    return [(plane, first, second) for first in places]


PLACES = (
    (line_of(0, 0),),
    (line_of(0, -1), line_of(0, 1), line_of(0, 2, HEAD), line_of(0, 2, TAIL)),
    (line_of(1, 0), line_of(1, -1), line_of(1, 1)),
    (line_of(1, 2, HEAD), line_of(1, 2, TAIL)),
)


def owners(places, row, core):
    y, x, z = row // (X * Z * C), row // (Z * C) % X, row // C % Z
    found = []
    for plane, first, second in places:
        dy = jnp.where(core == 0, first, second)
        dz = jnp.where(core == 0, second, first)
        found.append(row_id(y + dy, x + plane, z + dz, core))
    return found


def work_list(tile_dst, tile_src, live_tiles, row):
    core = row % C
    table = []
    for phase in PLACES:
        for holder in (core, 1 - core):
            for places in phase:
                table += owners(places, row, holder)
    table = jnp.stack(table)
    tiles = jnp.arange(tile_src.shape[0], dtype=jnp.int32)
    live = tiles < live_tiles
    owner = tile_src // DEV_BLOCKS
    below = live[None, :] & (owner[None, :] < table[:, None])
    upto = live[None, :] & (owner[None, :] <= table[:, None])
    starts = jnp.minimum(jnp.sum(below.astype(jnp.int32), axis=1), tile_src.shape[0] - OWNER_TILES)
    fills = jnp.sum(upto.astype(jnp.int32), axis=1) - starts
    mine = owner[:, None] == table[None, :]
    spots = jnp.arange(OWNERS, dtype=jnp.int32)
    spot = jnp.sum(jnp.where(mine, spots[None, :], 0), axis=1)
    start = jnp.sum(jnp.where(mine, starts[None, :], 0), axis=1)
    group = spot // GROUP
    first = sum(jnp.where(group >= base, GROUP * (base - last), 0) for last, base in zip(GROUP_BASE, GROUP_BASE[1:]))
    local = spot - first
    key = jnp.where(live, group * DSTS + tile_dst, -1)
    ahead = (key[:, None] == key[None, :]) & (tiles[None, :] < tiles[:, None])
    rank = jnp.sum(ahead.astype(jnp.int32), axis=1)
    step = group * GROUP_STEPS + rank // DEPTH
    place = jnp.where(live, step * STEP + tile_dst * DEPTH + rank % DEPTH, -1)
    held = local * OWNER_TILES + tiles - start
    value = (held << BLOCK_BITS) + 1 + local * DEV_BLOCKS + tile_src % DEV_BLOCKS
    hit = place[None, :] == jnp.arange(SLOTS, dtype=jnp.int32)[:, None]
    listed = jnp.sum(jnp.where(hit, value[None, :], 0), axis=1)
    buckets = jnp.arange(GROUPS * DSTS, dtype=jnp.int32)
    counts = jnp.sum((key[None, :] == buckets[:, None]).astype(jnp.int32), axis=1)
    steps = jnp.max((counts.reshape(GROUPS, DSTS) + DEPTH - 1) // DEPTH, axis=1)
    return listed, starts, fills, steps


def phase_kernel(phase, counts, meta, tiles, *refs):
    pieces = refs[: len(counts)]
    refs = refs[len(counts) :]
    if phase > 0:
        before, refs = refs[0], refs[1:]
    fbuf, tbuf, acc, sem = refs[-4:]
    outs = refs[:-4]
    half = meta[HALF_AT]
    groups = PHASE_GROUPS[phase]
    arrivals = [[] for _ in range(groups)]
    owner = 0
    for piece, count in zip(pieces, counts):
        blocks = fbuf.at[pl.ds(1 + owner * DEV_BLOCKS, count * DEV_BLOCKS)]
        group = owner // GROUP
        arrivals[group].append(pltpu.make_async_copy(piece, blocks, sem.at[group]))
        owner += count

    def tile_copy(i, part):
        start = meta[STARTS + GROUP_BASE[phase] * GROUP + i] + part * CHUNK
        held = tbuf.at[pl.ds(i * OWNER_TILES + part * CHUNK, CHUNK)]
        return pltpu.make_async_copy(tiles.at[pl.ds(start, CHUNK)], held, sem.at[i // GROUP])

    def over(i):
        return meta[FILLS + GROUP_BASE[phase] * GROUP + i] > CHUNK

    for group in range(groups):
        mine = range(group * GROUP, (group + 1) * GROUP)
        arrivals[group] += [tile_copy(i, 0) for i in mine]
        for copy in arrivals[group]:
            copy.start()
        for i in mine:
            pl.when(over(i))(tile_copy(i, 1).start)
    fbuf[0] = jnp.zeros(fbuf.shape[1:], fbuf.dtype)
    if phase == 0:
        acc[...] = jnp.zeros_like(acc)
    elif phase - 1 in SPLIT:
        acc[...] = jnp.zeros_like(acc)
        acc[pl.ds(half * DEV_BLOCKS, DEV_BLOCKS)] = before[...]
    else:
        acc[...] = before[...]

    for group in range(groups):
        for copy in arrivals[group]:
            copy.wait()
        for i in range(group * GROUP, (group + 1) * GROUP):
            pl.when(over(i))(tile_copy(i, 1).wait)
        listed = (GROUP_BASE[phase] + group) * GROUP_STEPS * STEP

        def run(step, carry, listed=listed):
            for d in range(DSTS):
                at = listed + step * STEP + DEPTH * d
                entries = [meta[at + i] for i in range(DEPTH)]
                left = jnp.concatenate([tbuf[e >> BLOCK_BITS] for e in entries], axis=1)
                right = jnp.concatenate([fbuf[e & ((1 << BLOCK_BITS) - 1)] for e in entries], axis=0)
                acc[d] += jnp.dot(left, right, preferred_element_type=jnp.float32)
            return carry

        lax.fori_loop(0, meta[STEPS_AT + GROUP_BASE[phase] + group], run, 0)
    if len(outs) == 2:
        near, away = outs
        near[...] = acc[pl.ds(half * DEV_BLOCKS, DEV_BLOCKS)]
        away[...] = acc[pl.ds((1 - half) * DEV_BLOCKS, DEV_BLOCKS)].astype(away.dtype)
    else:
        outs[0][...] = acc[...]


def run_phase(phase, meta, tiles, pieces, before=None):
    edge, width = tiles.shape[1], pieces[0].shape[1]
    whole, part = (DSTS, edge, width), (DEV_BLOCKS, edge, width)
    vmem = pl.BlockSpec(memory_space=pltpu.VMEM)
    anyspace = pl.BlockSpec(memory_space=pl.ANY)
    f32 = functools.partial(jax.ShapeDtypeStruct, dtype=jnp.float32)
    sent = jnp.float32 if phase == SPLIT[0] else jnp.bfloat16
    out_shape = (f32(part), jax.ShapeDtypeStruct(part, sent)) if phase in SPLIT else (f32(whole),)
    count = GROUP * PHASE_GROUPS[phase]
    blocks = [piece.reshape(-1, edge, width) for piece in pieces]
    counts = [piece.shape[0] // DEV_BLOCKS for piece in blocks]
    slots = STEP * GROUP_STEPS * PHASE_GROUPS[phase] // 2
    results = pl.pallas_call(
        functools.partial(phase_kernel, phase, counts),
        out_shape=out_shape,
        grid_spec=pltpu.PrefetchScalarGridSpec(
            num_scalar_prefetch=1,
            grid=(),
            in_specs=[anyspace] * (1 + len(blocks)) + ([vmem] if phase else []),
            out_specs=(vmem,) * len(out_shape),
            scratch_shapes=[
                pltpu.VMEM((1 + count * DEV_BLOCKS, edge, width), pieces[0].dtype),
                pltpu.VMEM((count * OWNER_TILES, edge, edge), tiles.dtype),
                pltpu.VMEM(whole, jnp.float32),
                pltpu.SemaphoreType.DMA((PHASE_GROUPS[phase],)),
            ],
        ),
        compiler_params=pltpu.CompilerParams(vmem_limit_bytes=VMEM_BYTES),
        cost_estimate=pl.CostEstimate(
            flops=slots * 128 * 128 * 256 * 2, bytes_accessed=slots * 32 * 1024, transcendentals=0
        ),
        name="phase",
    )(meta, tiles, *blocks, *((before,) if phase else ()))
    return results if len(results) > 1 else results[0]


def both(pieces):
    return list(pieces) + [send(rows, shift(c=1)) for rows in pieces]


def on_device(
    features, tile_vals, tile_dst, tile_src, tile_count, degree, w_self, w_neigh, out_bias
):
    row, rep = lax.axis_index("row"), lax.axis_index("rep")
    swap = [(0, 1), (1, 0)]
    hold = lax.optimization_barrier
    from_minus = send(features, along_first(1))
    from_plus = send(features, along_first(-1))
    from_far = send(features, along_first(2))
    across = send(features, shift(x=1))
    listed, starts, fills, steps = work_list(tile_dst, tile_src, tile_count[0], row)
    meta = jnp.concatenate([listed, starts, fills, steps, rep[None]]).astype(jnp.int32)
    from_minus, from_plus, from_far, across, meta = hold((from_minus, from_plus, from_far, across, meta))
    line = jnp.concatenate([features, from_minus, from_plus, from_far])
    rest = send(line[DEV_ROWS:], shift(x=1))
    minus = send(line, along_second(1))
    plus = send(line, along_second(-1))
    total = run_phase(0, meta, tile_vals, both((line,)))
    minus, plus, total = hold((minus, plus, total))
    far_head = send(minus[: 2 * DEV_ROWS], along_second(1))
    far_tail = send(plus[2 * DEV_ROWS :], along_second(-1))
    near_siblings = both((minus, plus))[2:]
    other = jnp.concatenate([across, rest])
    other_minus = send(other, along_second(1))
    other_plus = send(other, along_second(-1))
    far_siblings = both((far_head, far_tail))[2:]

    pieces = [minus, plus, far_head, far_tail] + near_siblings + far_siblings
    near, away = run_phase(1, meta, tile_vals, pieces, total)
    early = lax.ppermute(away, "rep", swap)
    other_minus, other_plus, near = hold((other_minus, other_plus, near))
    last_head = send(other_minus[: 2 * DEV_ROWS], along_second(1))
    last_tail = send(other_plus[2 * DEV_ROWS :], along_second(-1))

    total = run_phase(2, meta, tile_vals, both((other, other_minus, other_plus)), near)
    last_head, last_tail, total, early = hold((last_head, last_tail, total, early))
    near, away = run_phase(3, meta, tile_vals, both((last_head, last_tail)), total)
    late = lax.ppermute(away, "rep", swap)
    summed = (near + early + late.astype(jnp.float32)).reshape(features.shape)
    neighbours = (summed / jnp.sqrt(degree.astype(jnp.float32))[:, None]).astype(jnp.bfloat16)
    mixed = jnp.dot(features, w_self, preferred_element_type=jnp.float32) + out_bias[None, :]
    mixed = mixed + jnp.dot(neighbours, w_neigh, preferred_element_type=jnp.float32)
    return jnp.maximum(mixed, 0.0).astype(jnp.bfloat16)


def solution(mesh):
    in_specs = (
        P(("rep", "row"), None),
        P(("rep", "row"), None, None),
        P(("rep", "row")),
        P(("rep", "row")),
        P(("rep", "row")),
        P(("rep", "row")),
        P(),
        P(),
        P(),
    )
    out_specs = P(("rep", "row"), None)
    return jax.shard_map(
        on_device, mesh=mesh, in_specs=in_specs, out_specs=out_specs, check_vma=False
    )
```

time: 488 us -> 91 us (0.19)
  waiting for transfers between devices: 314 us -> 32.1 us
  other arithmetic: 72.8 us -> 1.99 us
  local copies, waits for them, and re-layouts: 43.8 us -> 0.62 us
  matrix products: 39.2 us -> 1.17 us
  starting transfers between devices: 0.04 us -> 31.6 us
  Pallas kernels: 0 us -> 22.3 us
  between operations: 14.2 us -> 0.94 us
    reduce_scatter x1 -> x0, waiting for transfers between devices: 203 us -> none  [on_device(): lax.psum_scatter(partial_value, 'rep', scatter_dimension=0, tiled=True)]
    all_gather x1 -> x0, waiting for transfers between devices: 110 us -> none  [on_device(): gathered = lax.all_gather(features, 'row', axis=0, tiled=True)]
    scatter-add x5 -> x0, other arithmetic: 61.8 us -> none  [tile_products(): return running.at[dst_block].add(products)]
    gather x5 -> x0, local copies, waits for them, and re-layouts: 42.7 us -> none  [tile_products(): neighbour_rows = jnp.take(source_rows, picked, axis=0)]
    dot_general x6 -> x1, matrix products: 37.1 us -> 0.23 us  [on_device(): jnp.dot(features, w_self, preferred_element_type=jnp.float32)]
    ppermute x0 -> x25, waiting for transfers between devices: none -> 32.1 us  [the longest x23 20.9 us: send(): return lax.ppermute(rows, 'row', pairs)]
    ppermute x0 -> x25, starting transfers between devices: none -> 31.6 us  [the longest x23 28.1 us: send(): return lax.ppermute(rows, 'row', pairs)]
    pallas_call x0 -> x4, Pallas kernels: none -> 22.3 us  [run_phase(): pl.pallas_call(functools.partial(phase_kernel, phase, counts), out_shape=...]
  transfers between devices with their start and end apart: 2 -> 25, of which waited for: 2 -> 13; matrix products, arithmetic and copies ran while one was open for 0% -> 3% of each run, Pallas kernels for 0% -> 20%
where the time goes in v2:
time: 91 us; the launch traced here: 90.7 us
  waiting for transfers between devices  32.1 us (35%)
  starting transfers between devices  31.6 us (35%)
  Pallas kernels  22.3 us (25%)
  other arithmetic  1.99 us (2%)
  matrix products  1.17 us (1%)
  between operations  0.94 us (1%)
    ppermute x23, starting transfers between devices, send(): return lax.ppermute(rows, 'row', pairs)  28.1 us
    pallas_call x4, Pallas kernels, run_phase(): pl.pallas_call(functools.partial(phase_kernel, phase, counts), out_shape=...  22.3 us
    ppermute x23, waiting for transfers between devices, send(): return lax.ppermute(rows, 'row', pairs)  20.9 us
    ppermute x1, waiting for transfers between devices, on_device(): late = lax.ppermute(away, 'rep', swap)  6.6 us
    ppermute x1, waiting for transfers between devices, on_device(): early = lax.ppermute(away, 'rep', swap)  4.61 us
    ppermute x1, starting transfers between devices, on_device(): late = lax.ppermute(away, 'rep', swap)  2.04 us
  transfers between devices with their start and end apart: 25, of which 13 were waited for; matrix products, arithmetic and copies ran while one was open for 3% of the time, Pallas kernels for 20%

profile of v2, /device:TPU:0, one launch (start us, length us, event | category | flops | bytes accessed | tf_op | source)
XLA Modules:
  0.0 90.7 jit_solution(3692197601156095861)
XLA Ops:
  0.0 1.7 %collective-permute-start = (bf16[512,256]{1,0:T(8,128)(2,1)}, bf16[512,256]{1,0:T(8,128)(2,1)S(1)}, u32[]{:S(2)}, u32[]{:S(2)}) collective-permute-start(bf16[512,256]{1,0:T(8,128)(2,1)} %param.9), channel_id=1, source_target_pairs={{0,16},{1,3},{2,18},{3,5},{4,20},{5,7},{6,22},{7,1},{8,24},{9,11},... | collective-permute-start | bytes 786440 | tf_op jit(solution)/shard_map/ppermute | solution.py:55
  1.7 1.6 %collective-permute-start.1 = (bf16[512,256]{1,0:T(8,128)(2,1)}, bf16[512,256]{1,0:T(8,128)(2,1)S(1)}, u32[]{:S(2)}, u32[]{:S(2)}) collective-permute-start(bf16[512,256]{1,0:T(8,128)(2,1)} %param.9), channel_id=1, source_target_pairs={{0,48},{1,7},{2,50},{3,1},{4,52},{5,3},{6,54},{7,5},{8,56},{9,15},... | collective-permute-start | bytes 786440 | tf_op jit(solution)/shard_map/ppermute | solution.py:55
  3.3 2.1 %collective-permute-start.2 = (bf16[512,256]{1,0:T(8,128)(2,1)}, bf16[512,256]{1,0:T(8,128)(2,1)S(1)}, u32[]{:S(2)}, u32[]{:S(2)}) collective-permute-start(bf16[512,256]{1,0:T(8,128)(2,1)} %param.9), channel_id=1, source_target_pairs={{0,32},{1,5},{2,34},{3,7},{4,36},{5,1},{6,38},{7,3},{8,40},{9,13},... | collective-permute-start | bytes 786440 | tf_op jit(solution)/shard_map/ppermute | solution.py:55
  5.4 3.0 %collective-permute-start.3 = (bf16[512,256]{1,0:T(8,128)(2,1)}, bf16[512,256]{1,0:T(8,128)(2,1)S(1)}, u32[]{:S(2)}, u32[]{:S(2)}) collective-permute-start(bf16[512,256]{1,0:T(8,128)(2,1)} %param.9), channel_id=1, source_target_pairs={{0,8},{1,9},{2,10},{3,11},{4,12},{5,13},{6,14},{7,15},{8,0},{9,1},... | collective-permute-start | bytes 786440 | tf_op jit(solution)/shard_map/ppermute | solution.py:55
  9.1 0.1 stack.259
  9.3 0.2 convert_reduce_fusion.2
  9.5 0.1 fusion.4
  9.6 0.3 convert_reduce_fusion
  10.0 0.1 convert_reduce_fusion.1
  10.1 0.7 select_reduce_fusion
  11.0 0.1 fusion.14
  11.1 0.1 concatenate.12.meta
  11.2 0.8 collective-permute-done.2
  12.0 3.0 %collective-permute-done.3 = bf16[512,256]{1,0:T(8,128)(2,1)S(1)} collective-permute-done((bf16[512,256]{1,0:T(8,128)(2,1)}, bf16[512,256]{1,0:T(8,128)(2,1)S(1)}, u32[]{:S(2)}, u32[]{:S(2)}) %collective-permute-start.3) | collective-permute-done | bytes 262176 | tf_op jit(solution)/shard_map/ppermute | solution.py:55
  15.1 0.1 collective-permute-start.9
  15.2 1.1 %collective-permute-start.7 = (bf16[2048,256]{1,0:T(8,128)(2,1)S(1)}, bf16[2048,256]{1,0:T(8,128)(2,1)S(1)}, u32[]{:S(2)}, u32[]{:S(2)}) collective-permute-start(bf16[2048,256]{1,0:T(8,128)(2,1)S(1)} %constant_dynamic-update-slice_fusion.2), channel_id=1, source_target_pairs={{0,2},{1,17},{2,4},{3,19},{4,6},{5,21},{6,0},{7,23},{8,10},{9,25},... | collective-permute-start | bytes 3145736 | tf_op jit(solution)/shard_map/ppermute | solution.py:55
  16.3 2.2 %collective-permute-start.8 = (bf16[2048,256]{1,0:T(8,128)(2,1)S(1)}, bf16[2048,256]{1,0:T(8,128)(2,1)S(1)}, u32[]{:S(2)}, u32[]{:S(2)}) collective-permute-start(bf16[2048,256]{1,0:T(8,128)(2,1)S(1)} %constant_dynamic-update-slice_fusion.2), channel_id=1, source_target_pairs={{0,6},{1,49},{2,0},{3,51},{4,2},{5,53},{6,4},{7,55},{8,14},{9,57},... | collective-permute-start | bytes 3145736 | tf_op jit(solution)/shard_map/ppermute | solution.py:55
  18.5 3.1 %collective-permute-start.4 = (bf16[1536,256]{1,0:T(8,128)(2,1)S(1)}, bf16[1536,256]{1,0:T(8,128)(2,1)S(1)}, u32[]{:S(2)}, u32[]{:S(2)}) collective-permute-start(bf16[1536,256]{1,0:T(8,128)(2,1)S(1)} %pad_maximum_fusion), channel_id=1, source_target_pairs={{0,8},{1,9},{2,10},{3,11},{4,12},{5,13},{6,14},{7,15},{8,0},{9,1},... | collective-permute-start | bytes 2359304 | tf_op jit(solution)/shard_map/ppermute | solution.py:55
  21.6 4.0 %phase.4.refs_8_ = f32[8,128,256]{2,1,0:T(8,128)S(1)} custom-call(s32[2185]{0:T(1024)S(1)} %concatenate.12.meta, bf16[704,128,128]{2,1,0:T(8,128)(2,1)} %tiles.7, bf16[16,128,256]{2,1,0:T(8,128)(2,1)S(1)} %bitcast.101, bf16[16,128,256]{2,1,0:T(8,128)(2,1)S(1)} %bitcast.108), custom_call_target="tpu_custom_call" | custom-call | flops 1073741824 | bytes 4194304 | tf_op jit(solution)/shard_map/phase/pallas_call | solution.py:195
  25.7 5.6 %collective-permute-done.7 = bf16[2048,256]{1,0:T(8,128)(2,1)S(1)} collective-permute-done((bf16[2048,256]{1,0:T(8,128)(2,1)S(1)}, bf16[2048,256]{1,0:T(8,128)(2,1)S(1)}, u32[]{:S(2)}, u32[]{:S(2)}) %collective-permute-start.7) | collective-permute-done | bytes 1048608 | tf_op jit(solution)/shard_map/ppermute | solution.py:55
  31.3 1.2 %collective-permute-start.10 = (bf16[1024,256]{1,0:T(8,128)(2,1)S(1)}, bf16[1024,256]{1,0:T(8,128)(2,1)S(1)}, u32[]{:S(2)}, u32[]{:S(2)}) collective-permute-start(bf16[1024,256]{1,0:T(8,128)(2,1)S(1)} %slice.14), channel_id=1, source_target_pairs={{0,2},{1,17},{2,4},{3,19},{4,6},{5,21},{6,0},{7,23},{8,10},{9,25},... | collective-permute-start | bytes 1572872 | tf_op jit(solution)/shard_map/ppermute | solution.py:55
  32.5 0.8 collective-permute-start.13
  33.3 3.2 %collective-permute-start.11 = (bf16[1024,256]{1,0:T(8,128)(2,1)S(1)}, bf16[1024,256]{1,0:T(8,128)(2,1)S(1)}, u32[]{:S(2)}, u32[]{:S(2)}) collective-permute-start(bf16[1024,256]{1,0:T(8,128)(2,1)S(1)} %slice.15), channel_id=1, source_target_pairs={{0,6},{1,49},{2,0},{3,51},{4,2},{5,53},{6,4},{7,55},{8,14},{9,57},... | collective-permute-start | bytes 1572872 | tf_op jit(solution)/shard_map/ppermute | solution.py:55
  36.5 2.9 %collective-permute-done.4 = bf16[1536,256]{1,0:T(8,128)(2,1)S(1)} collective-permute-done((bf16[1536,256]{1,0:T(8,128)(2,1)S(1)}, bf16[1536,256]{1,0:T(8,128)(2,1)S(1)}, u32[]{:S(2)}, u32[]{:S(2)}) %collective-permute-start.4) | collective-permute-done | bytes 786464 | tf_op jit(solution)/shard_map/ppermute | solution.py:55
  39.5 0.8 collective-permute-start.5
  40.3 1.5 %collective-permute-done.10 = bf16[1024,256]{1,0:T(8,128)(2,1)S(1)} collective-permute-done((bf16[1024,256]{1,0:T(8,128)(2,1)S(1)}, bf16[1024,256]{1,0:T(8,128)(2,1)S(1)}, u32[]{:S(2)}, u32[]{:S(2)}) %collective-permute-start.10) | collective-permute-done | bytes 524320 | tf_op jit(solution)/shard_map/ppermute | solution.py:55
  41.8 2.0 %collective-permute-start.6 = (bf16[2048,256]{1,0:T(8,128)(2,1)S(1)}, bf16[2048,256]{1,0:T(8,128)(2,1)S(1)}, u32[]{:S(2)}, u32[]{:S(2)}) collective-permute-start(bf16[2048,256]{1,0:T(8,128)(2,1)S(1)} %constant_dynamic-update-slice_fusion), channel_id=1, source_target_pairs={{0,6},{1,49},{2,0},{3,51},{4,2},{5,53},{6,4},{7,55},{8,14},{9,57},... | collective-permute-start | bytes 3145736 | tf_op jit(solution)/shard_map/ppermute | solution.py:55
  43.8 0.5 collective-permute-start.15
  44.4 1.3 %collective-permute-done.14 = bf16[1024,256]{1,0:T(8,128)(2,1)S(1)} collective-permute-done((bf16[1024,256]{1,0:T(8,128)(2,1)S(1)}, bf16[1024,256]{1,0:T(8,128)(2,1)S(1)}, u32[]{:S(2)}, u32[]{:S(2)}) %collective-permute-start.14) | collective-permute-done | bytes 524320 | tf_op jit(solution)/shard_map/ppermute | solution.py:55
  45.7 0.7 collective-permute-done.15
  46.4 7.2 %phase.5 = (f32[4,128,256]{2,1,0:T(8,128)S(1)}, f32[4,128,256]{2,1,0:T(8,128)S(1)}) custom-call(s32[2185]{0:T(1024)S(1)} %concatenate.12.meta, bf16[704,128,128]{2,1,0:T(8,128)(2,1)} %tiles.7, bf16[16,128,256]{2,1,0:T(8,128)(2,1)S(1)} %bitcast.97, bf16[16,128,256]{2,1,0:T(8,128)(2,1)S(1)} %bitcast.98, bf16[8,128,256]{2,1,0:T(8,128)(2,1)S(1)} %bitcast.109, ...), custom_call_target="tpu_custom_call" | custom-call | flops 3221225472 | bytes 12582912 | tf_op jit(solution)/shard_map/phase/pallas_call | solution.py:195
  53.6 1.9 %collective-permute-done.5 = bf16[2048,256]{1,0:T(8,128)(2,1)S(1)} collective-permute-done((bf16[2048,256]{1,0:T(8,128)(2,1)S(1)}, bf16[2048,256]{1,0:T(8,128)(2,1)S(1)}, u32[]{:S(2)}, u32[]{:S(2)}) %collective-permute-start.5) | collective-permute-done | bytes 1048608 | tf_op jit(solution)/shard_map/ppermute | solution.py:55
  55.6 1.0 %collective-permute-done.6 = bf16[2048,256]{1,0:T(8,128)(2,1)S(1)} collective-permute-done((bf16[2048,256]{1,0:T(8,128)(2,1)S(1)}, bf16[2048,256]{1,0:T(8,128)(2,1)S(1)}, u32[]{:S(2)}, u32[]{:S(2)}) %collective-permute-start.6) | collective-permute-done | bytes 1048608 | tf_op jit(solution)/shard_map/ppermute | solution.py:55
  56.6 0.5 collective-permute-start.20
  57.2 3.5 %collective-permute-start.17 = (bf16[1024,256]{1,0:T(8,128)(2,1)S(1)}, bf16[1024,256]{1,0:T(8,128)(2,1)S(1)}, u32[]{:S(2)}, u32[]{:S(2)}) collective-permute-start(bf16[1024,256]{1,0:T(8,128)(2,1)S(1)} %slice.17), channel_id=1, source_target_pairs={{0,6},{1,49},{2,0},{3,51},{4,2},{5,53},{6,4},{7,55},{8,14},{9,57},... | collective-permute-start | bytes 1572872 | tf_op jit(solution)/shard_map/ppermute | solution.py:55
  60.7 1.5 %collective-permute-start.21 = (f32[4,128,256]{2,1,0:T(8,128)S(1)}, f32[4,128,256]{2,1,0:T(8,128)S(1)}, u32[]{:S(2)}, u32[]{:S(2)}) collective-permute-start(f32[4,128,256]{2,1,0:T(8,128)S(1)} %get-tuple-element.36), channel_id=1, source_target_pairs={{0,64},{64,0},{1,65},{65,1},{2,66},{66,2},{3,67},{67,3},{4,68},{68... | collective-permute-start | bytes 1572872 | tf_op jit(solution)/shard_map/ppermute | solution.py:252
  62.2 7.0 %phase.6.refs_4_ = f32[8,128,256]{2,1,0:T(8,128)S(1)} custom-call(s32[2185]{0:T(1024)S(1)} %concatenate.12.meta, bf16[704,128,128]{2,1,0:T(8,128)(2,1)} %tiles.7, bf16[16,128,256]{2,1,0:T(8,128)(2,1)S(1)} %bitcast.102, bf16[16,128,256]{2,1,0:T(8,128)(2,1)S(1)} %bitcast.99, bf16[16,128,256]{2,1,0:T(8,128)(2,1)S(1)} %bitcast.100, ...), custom_call_target="tpu_custom_call" | custom-call | flops 3221225472 | bytes 12582912 | tf_op jit(solution)/shard_map/phase/pallas_call | solution.py:195
  69.2 4.6 %collective-permute-done.21 = f32[4,128,256]{2,1,0:T(8,128)S(1)} collective-permute-done((f32[4,128,256]{2,1,0:T(8,128)S(1)}, f32[4,128,256]{2,1,0:T(8,128)S(1)}, u32[]{:S(2)}, u32[]{:S(2)}) %collective-permute-start.21) | collective-permute-done | bytes 524320 | tf_op jit(solution)/shard_map/ppermute | solution.py:252
  73.9 0.5 collective-permute-start.23
  74.4 1.4 %collective-permute-done.22 = bf16[1024,256]{1,0:T(8,128)(2,1)S(1)} collective-permute-done((bf16[1024,256]{1,0:T(8,128)(2,1)S(1)}, bf16[1024,256]{1,0:T(8,128)(2,1)S(1)}, u32[]{:S(2)}, u32[]{:S(2)}) %collective-permute-start.22) | collective-permute-done | bytes 524320 | tf_op jit(solution)/shard_map/ppermute | solution.py:55
  75.8 0.7 collective-permute-done.23
  76.5 4.1 %phase.7 = (f32[4,128,256]{2,1,0:T(8,128)S(1)}, bf16[4,128,256]{2,1,0:T(8,128)(2,1)S(1)}) custom-call(s32[2185]{0:T(1024)S(1)} %concatenate.12.meta, bf16[704,128,128]{2,1,0:T(8,128)(2,1)} %tiles.7, bf16[8,128,256]{2,1,0:T(8,128)(2,1)S(1)} %bitcast.113, bf16[8,128,256]{2,1,0:T(8,128)(2,1)S(1)} %bitcast.114, bf16[8,128,256]{2,1,0:T(8,128)(2,1)S(1)} %bitcast.115, ...), custom_call_target="tpu_custom_call" | custom-call | flops 1073741824 | bytes 4194304 | tf_op jit(solution)/shard_map/phase/pallas_call | solution.py:195
  80.6 2.0 %collective-permute-start.24 = (bf16[4,128,256]{2,1,0:T(8,128)(2,1)S(1)}, bf16[4,128,256]{2,1,0:T(8,128)(2,1)S(1)}, u32[]{:S(2)}, u32[]{:S(2)}) collective-permute-start(bf16[4,128,256]{2,1,0:T(8,128)(2,1)S(1)} %get-tuple-element.42), channel_id=1, source_target_pairs={{0,64},{64,0},{1,65},{65,1},{2,66},{66,2},{3,67},{67,3},{4,68},{68... | collective-permute-start | bytes 786440 | tf_op jit(solution)/shard_map/ppermute | solution.py:260
  82.7 0.2 convolution_add_fusion.1
  82.9 6.6 %collective-permute-done.24 = bf16[4,128,256]{2,1,0:T(8,128)(2,1)S(1)} collective-permute-done((bf16[4,128,256]{2,1,0:T(8,128)(2,1)S(1)}, bf16[4,128,256]{2,1,0:T(8,128)(2,1)S(1)}, u32[]{:S(2)}, u32[]{:S(2)}) %collective-permute-start.24) | collective-permute-done | bytes 262176 | tf_op jit(solution)/shard_map/ppermute | solution.py:260
  89.5 0.1 convert_add_fusion
  89.6 0.1 fusion.3
  89.7 0.9 %fusion.2 = bf16[512,256]{1,0:T(8,128)(2,1)} fusion(f32[512,256]{1,0:T(8,128)S(1)} %convolution_add_fusion.1, bf16[512,256]{1,0:T(8,128)(2,1)S(1)} %fusion.3, bf16[256,256]{1,0:T(8,128)(2,1)S(1)} %copy-done.2), kind=kOutput, calls=%fused_computation.8 | convolution fusion | flops 67502080 | bytes 1179648 | tf_op jit(solution)/shard_map/dot_general | solution.py:264
  (51 shorter events, 0.7 us)
Async XLA Ops:
  0.0 82.6 %copy-start = (bf16[256,256]{1,0:T(8,128)(2,1)S(1)}, bf16[256,256]{1,0:T(8,128)(2,1)}, u32[]{:S(2)}) copy-start(bf16[256,256]{1,0:T(8,128)(2,1)} %param.15) | copy-start | bytes 393220
  0.0 11.2 %copy-start.1 = (bf16[512,256]{1,0:T(8,128)(2,1)S(1)}, bf16[512,256]{1,0:T(8,128)(2,1)}, u32[]{:S(2)}) copy-start(bf16[512,256]{1,0:T(8,128)(2,1)} %param.9) | copy-start | bytes 786436
  0.0 9.1 %copy-start.4 = (s32[704]{0:T(1024)S(1)}, s32[704]{0:T(1024)}, u32[]{:S(2)}) copy-start(s32[704]{0:T(1024)} %param.12) | copy-start | bytes 8452
  0.0 9.6 %copy-start.3 = (s32[704]{0:T(1024)S(1)}, s32[704]{0:T(1024)}, u32[]{:S(2)}) copy-start(s32[704]{0:T(1024)} %param.11) | copy-start | bytes 8452
  0.0 11.2 %collective-permute-start = (bf16[512,256]{1,0:T(8,128)(2,1)}, bf16[512,256]{1,0:T(8,128)(2,1)S(1)}, u32[]{:S(2)}, u32[]{:S(2)}) collective-permute-start(bf16[512,256]{1,0:T(8,128)(2,1)} %param.9), channel_id=1, source_target_pairs={{0,16},{1,3},{2,18},{3,5},{4,20},{5,7},{6,22},{7,1},{8,24},{9,11},... | collective-permute-start | bytes 786440 | tf_op jit(solution)/shard_map/ppermute | solution.py:55
  1.7 9.5 %collective-permute-start.1 = (bf16[512,256]{1,0:T(8,128)(2,1)}, bf16[512,256]{1,0:T(8,128)(2,1)S(1)}, u32[]{:S(2)}, u32[]{:S(2)}) collective-permute-start(bf16[512,256]{1,0:T(8,128)(2,1)} %param.9), channel_id=1, source_target_pairs={{0,48},{1,7},{2,50},{3,1},{4,52},{5,3},{6,54},{7,5},{8,56},{9,15},... | collective-permute-start | bytes 786440 | tf_op jit(solution)/shard_map/ppermute | solution.py:55
  3.3 8.7 %collective-permute-start.2 = (bf16[512,256]{1,0:T(8,128)(2,1)}, bf16[512,256]{1,0:T(8,128)(2,1)S(1)}, u32[]{:S(2)}, u32[]{:S(2)}) collective-permute-start(bf16[512,256]{1,0:T(8,128)(2,1)} %param.9), channel_id=1, source_target_pairs={{0,32},{1,5},{2,34},{3,7},{4,36},{5,1},{6,38},{7,3},{8,40},{9,13},... | collective-permute-start | bytes 786440 | tf_op jit(solution)/shard_map/ppermute | solution.py:55
  5.4 9.6 %collective-permute-start.3 = (bf16[512,256]{1,0:T(8,128)(2,1)}, bf16[512,256]{1,0:T(8,128)(2,1)S(1)}, u32[]{:S(2)}, u32[]{:S(2)}) collective-permute-start(bf16[512,256]{1,0:T(8,128)(2,1)} %param.9), channel_id=1, source_target_pairs={{0,8},{1,9},{2,10},{3,11},{4,12},{5,13},{6,14},{7,15},{8,0},{9,1},... | collective-permute-start | bytes 786440 | tf_op jit(solution)/shard_map/ppermute | solution.py:55
  15.1 6.6 %collective-permute-start.9 = (bf16[2048,256]{1,0:T(8,128)(2,1)S(1)}, bf16[2048,256]{1,0:T(8,128)(2,1)S(1)}, u32[]{:S(2)}, u32[]{:S(2)}) collective-permute-start(bf16[2048,256]{1,0:T(8,128)(2,1)S(1)} %constant_dynamic-update-slice_fusion.2), channel_id=1, source_target_pairs={{0,1},{1,0},{2,3},{3,2},{4,5},{5,4},{6,7},{7,6},{8,9},{9,8},{10,11... | collective-permute-start | bytes 3145736 | tf_op jit(solution)/shard_map/ppermute | solution.py:55
  15.2 16.1 %collective-permute-start.7 = (bf16[2048,256]{1,0:T(8,128)(2,1)S(1)}, bf16[2048,256]{1,0:T(8,128)(2,1)S(1)}, u32[]{:S(2)}, u32[]{:S(2)}) collective-permute-start(bf16[2048,256]{1,0:T(8,128)(2,1)S(1)} %constant_dynamic-update-slice_fusion.2), channel_id=1, source_target_pairs={{0,2},{1,17},{2,4},{3,19},{4,6},{5,21},{6,0},{7,23},{8,10},{9,25},... | collective-permute-start | bytes 3145736 | tf_op jit(solution)/shard_map/ppermute | solution.py:55
  16.3 15.0 %collective-permute-start.8 = (bf16[2048,256]{1,0:T(8,128)(2,1)S(1)}, bf16[2048,256]{1,0:T(8,128)(2,1)S(1)}, u32[]{:S(2)}, u32[]{:S(2)}) collective-permute-start(bf16[2048,256]{1,0:T(8,128)(2,1)S(1)} %constant_dynamic-update-slice_fusion.2), channel_id=1, source_target_pairs={{0,6},{1,49},{2,0},{3,51},{4,2},{5,53},{6,4},{7,55},{8,14},{9,57},... | collective-permute-start | bytes 3145736 | tf_op jit(solution)/shard_map/ppermute | solution.py:55
  18.5 20.9 %collective-permute-start.4 = (bf16[1536,256]{1,0:T(8,128)(2,1)S(1)}, bf16[1536,256]{1,0:T(8,128)(2,1)S(1)}, u32[]{:S(2)}, u32[]{:S(2)}) collective-permute-start(bf16[1536,256]{1,0:T(8,128)(2,1)S(1)} %pad_maximum_fusion), channel_id=1, source_target_pairs={{0,8},{1,9},{2,10},{3,11},{4,12},{5,13},{6,14},{7,15},{8,0},{9,1},... | collective-permute-start | bytes 2359304 | tf_op jit(solution)/shard_map/ppermute | solution.py:55
  31.2 12.5 %collective-permute-start.12 = (bf16[2048,256]{1,0:T(8,128)(2,1)S(1)}, bf16[2048,256]{1,0:T(8,128)(2,1)S(1)}, u32[]{:S(2)}, u32[]{:S(2)}) collective-permute-start(bf16[2048,256]{1,0:T(8,128)(2,1)S(1)} %collective-permute-done.7), channel_id=1, source_target_pairs={{0,1},{1,0},{2,3},{3,2},{4,5},{5,4},{6,7},{7,6},{8,9},{9,8},{10,11... | collective-permute-start | bytes 3145736 | tf_op jit(solution)/shard_map/ppermute | solution.py:55
  31.3 10.5 %collective-permute-start.10 = (bf16[1024,256]{1,0:T(8,128)(2,1)S(1)}, bf16[1024,256]{1,0:T(8,128)(2,1)S(1)}, u32[]{:S(2)}, u32[]{:S(2)}) collective-permute-start(bf16[1024,256]{1,0:T(8,128)(2,1)S(1)} %slice.14), channel_id=1, source_target_pairs={{0,2},{1,17},{2,4},{3,19},{4,6},{5,21},{6,0},{7,23},{8,10},{9,25},... | collective-permute-start | bytes 1572872 | tf_op jit(solution)/shard_map/ppermute | solution.py:55
  32.5 11.8 %collective-permute-start.13 = (bf16[2048,256]{1,0:T(8,128)(2,1)S(1)}, bf16[2048,256]{1,0:T(8,128)(2,1)S(1)}, u32[]{:S(2)}, u32[]{:S(2)}) collective-permute-start(bf16[2048,256]{1,0:T(8,128)(2,1)S(1)} %collective-permute-done.8), channel_id=1, source_target_pairs={{0,1},{1,0},{2,3},{3,2},{4,5},{5,4},{6,7},{7,6},{8,9},{9,8},{10,11... | collective-permute-start | bytes 3145736 | tf_op jit(solution)/shard_map/ppermute | solution.py:55
  33.3 10.5 %collective-permute-start.11 = (bf16[1024,256]{1,0:T(8,128)(2,1)S(1)}, bf16[1024,256]{1,0:T(8,128)(2,1)S(1)}, u32[]{:S(2)}, u32[]{:S(2)}) collective-permute-start(bf16[1024,256]{1,0:T(8,128)(2,1)S(1)} %slice.15), channel_id=1, source_target_pairs={{0,6},{1,49},{2,0},{3,51},{4,2},{5,53},{6,4},{7,55},{8,14},{9,57},... | collective-permute-start | bytes 1572872 | tf_op jit(solution)/shard_map/ppermute | solution.py:55
  39.5 16.1 %collective-permute-start.5 = (bf16[2048,256]{1,0:T(8,128)(2,1)S(1)}, bf16[2048,256]{1,0:T(8,128)(2,1)S(1)}, u32[]{:S(2)}, u32[]{:S(2)}) collective-permute-start(bf16[2048,256]{1,0:T(8,128)(2,1)S(1)} %constant_dynamic-update-slice_fusion), channel_id=1, source_target_pairs={{0,2},{1,17},{2,4},{3,19},{4,6},{5,21},{6,0},{7,23},{8,10},{9,25},... | collective-permute-start | bytes 3145736 | tf_op jit(solution)/shard_map/ppermute | solution.py:55
  41.8 14.8 %collective-permute-start.6 = (bf16[2048,256]{1,0:T(8,128)(2,1)S(1)}, bf16[2048,256]{1,0:T(8,128)(2,1)S(1)}, u32[]{:S(2)}, u32[]{:S(2)}) collective-permute-start(bf16[2048,256]{1,0:T(8,128)(2,1)S(1)} %constant_dynamic-update-slice_fusion), channel_id=1, source_target_pairs={{0,6},{1,49},{2,0},{3,51},{4,2},{5,53},{6,4},{7,55},{8,14},{9,57},... | collective-permute-start | bytes 3145736 | tf_op jit(solution)/shard_map/ppermute | solution.py:55
  43.8 1.9 %collective-permute-start.14 = (bf16[1024,256]{1,0:T(8,128)(2,1)S(1)}, bf16[1024,256]{1,0:T(8,128)(2,1)S(1)}, u32[]{:S(2)}, u32[]{:S(2)}) collective-permute-start(bf16[1024,256]{1,0:T(8,128)(2,1)S(1)} %collective-permute-done.10), channel_id=1, source_target_pairs={{0,1},{1,0},{2,3},{3,2},{4,5},{5,4},{6,7},{7,6},{8,9},{9,8},{10,11... | collective-permute-start | bytes 1572872 | tf_op jit(solution)/shard_map/ppermute | solution.py:55
  43.8 2.7 %collective-permute-start.15 = (bf16[1024,256]{1,0:T(8,128)(2,1)S(1)}, bf16[1024,256]{1,0:T(8,128)(2,1)S(1)}, u32[]{:S(2)}, u32[]{:S(2)}) collective-permute-start(bf16[1024,256]{1,0:T(8,128)(2,1)S(1)} %collective-permute-done.11), channel_id=1, source_target_pairs={{0,1},{1,0},{2,3},{3,2},{4,5},{5,4},{6,7},{7,6},{8,9},{9,8},{10,11... | collective-permute-start | bytes 1572872 | tf_op jit(solution)/shard_map/ppermute | solution.py:55
  44.3 16.4 %collective-permute-start.18 = (bf16[2048,256]{1,0:T(8,128)(2,1)S(1)}, bf16[2048,256]{1,0:T(8,128)(2,1)S(1)}, u32[]{:S(2)}, u32[]{:S(2)}) collective-permute-start(bf16[2048,256]{1,0:T(8,128)(2,1)S(1)} %constant_dynamic-update-slice_fusion), channel_id=1, source_target_pairs={{0,1},{1,0},{2,3},{3,2},{4,5},{5,4},{6,7},{7,6},{8,9},{9,8},{10,11... | collective-permute-start | bytes 3145736 | tf_op jit(solution)/shard_map/ppermute | solution.py:55
  56.6 5.7 %collective-permute-start.19 = (bf16[2048,256]{1,0:T(8,128)(2,1)S(1)}, bf16[2048,256]{1,0:T(8,128)(2,1)S(1)}, u32[]{:S(2)}, u32[]{:S(2)}) collective-permute-start(bf16[2048,256]{1,0:T(8,128)(2,1)S(1)} %collective-permute-done.5), channel_id=1, source_target_pairs={{0,1},{1,0},{2,3},{3,2},{4,5},{5,4},{6,7},{7,6},{8,9},{9,8},{10,11... | collective-permute-start | bytes 3145736 | tf_op jit(solution)/shard_map/ppermute | solution.py:55
  56.6 5.7 %collective-permute-start.20 = (bf16[2048,256]{1,0:T(8,128)(2,1)S(1)}, bf16[2048,256]{1,0:T(8,128)(2,1)S(1)}, u32[]{:S(2)}, u32[]{:S(2)}) collective-permute-start(bf16[2048,256]{1,0:T(8,128)(2,1)S(1)} %collective-permute-done.6), channel_id=1, source_target_pairs={{0,1},{1,0},{2,3},{3,2},{4,5},{5,4},{6,7},{7,6},{8,9},{9,8},{10,11... | collective-permute-start | bytes 3145736 | tf_op jit(solution)/shard_map/ppermute | solution.py:55
  57.1 12.1 %collective-permute-start.16 = (bf16[1024,256]{1,0:T(8,128)(2,1)S(1)}, bf16[1024,256]{1,0:T(8,128)(2,1)S(1)}, u32[]{:S(2)}, u32[]{:S(2)}) collective-permute-start(bf16[1024,256]{1,0:T(8,128)(2,1)S(1)} %slice.16), channel_id=1, source_target_pairs={{0,2},{1,17},{2,4},{3,19},{4,6},{5,21},{6,0},{7,23},{8,10},{9,25},... | collective-permute-start | bytes 1572872 | tf_op jit(solution)/shard_map/ppermute | solution.py:55
  57.2 12.0 %collective-permute-start.17 = (bf16[1024,256]{1,0:T(8,128)(2,1)S(1)}, bf16[1024,256]{1,0:T(8,128)(2,1)S(1)}, u32[]{:S(2)}, u32[]{:S(2)}) collective-permute-start(bf16[1024,256]{1,0:T(8,128)(2,1)S(1)} %slice.17), channel_id=1, source_target_pairs={{0,6},{1,49},{2,0},{3,51},{4,2},{5,53},{6,4},{7,55},{8,14},{9,57},... | collective-permute-start | bytes 1572872 | tf_op jit(solution)/shard_map/ppermute | solution.py:55
  60.7 13.1 %collective-permute-start.21 = (f32[4,128,256]{2,1,0:T(8,128)S(1)}, f32[4,128,256]{2,1,0:T(8,128)S(1)}, u32[]{:S(2)}, u32[]{:S(2)}) collective-permute-start(f32[4,128,256]{2,1,0:T(8,128)S(1)} %get-tuple-element.36), channel_id=1, source_target_pairs={{0,64},{64,0},{1,65},{65,1},{2,66},{66,2},{3,67},{67,3},{4,68},{68... | collective-permute-start | bytes 1572872 | tf_op jit(solution)/shard_map/ppermute | solution.py:252
  73.9 1.9 %collective-permute-start.22 = (bf16[1024,256]{1,0:T(8,128)(2,1)S(1)}, bf16[1024,256]{1,0:T(8,128)(2,1)S(1)}, u32[]{:S(2)}, u32[]{:S(2)}) collective-permute-start(bf16[1024,256]{1,0:T(8,128)(2,1)S(1)} %collective-permute-done.16), channel_id=1, source_target_pairs={{0,1},{1,0},{2,3},{3,2},{4,5},{5,4},{6,7},{7,6},{8,9},{9,8},{10,11... | collective-permute-start | bytes 1572872 | tf_op jit(solution)/shard_map/ppermute | solution.py:55
  73.9 2.7 %collective-permute-start.23 = (bf16[1024,256]{1,0:T(8,128)(2,1)S(1)}, bf16[1024,256]{1,0:T(8,128)(2,1)S(1)}, u32[]{:S(2)}, u32[]{:S(2)}) collective-permute-start(bf16[1024,256]{1,0:T(8,128)(2,1)S(1)} %collective-permute-done.17), channel_id=1, source_target_pairs={{0,1},{1,0},{2,3},{3,2},{4,5},{5,4},{6,7},{7,6},{8,9},{9,8},{10,11... | collective-permute-start | bytes 1572872 | tf_op jit(solution)/shard_map/ppermute | solution.py:55
  76.5 6.1 %copy-start.5 = (s32[512]{0:T(512)S(1)}, s32[512]{0:T(512)}, u32[]{:S(2)}) copy-start(s32[512]{0:T(512)} %param.14) | copy-start | bytes 6148
  76.5 6.1 %copy-start.6 = (f32[256]{0:T(256)S(1)}, f32[256]{0:T(256)}, u32[]{:S(2)}) copy-start(f32[256]{0:T(256)} %param.17) | copy-start | bytes 3076
  80.6 9.2 %copy-start.2 = (bf16[256,256]{1,0:T(8,128)(2,1)S(1)}, bf16[256,256]{1,0:T(8,128)(2,1)}, u32[]{:S(2)}) copy-start(bf16[256,256]{1,0:T(8,128)(2,1)} %param.16) | copy-start | bytes 393220
  80.6 8.9 %collective-permute-start.24 = (bf16[4,128,256]{2,1,0:T(8,128)(2,1)S(1)}, bf16[4,128,256]{2,1,0:T(8,128)(2,1)S(1)}, u32[]{:S(2)}, u32[]{:S(2)}) collective-permute-start(bf16[4,128,256]{2,1,0:T(8,128)(2,1)S(1)} %get-tuple-element.42), channel_id=1, source_target_pairs={{0,64},{64,0},{1,65},{65,1},{2,66},{66,2},{3,67},{67,3},{4,68},{68... | collective-permute-start | bytes 786440 | tf_op jit(solution)/shard_map/ppermute | solution.py:260

commit v3 on v2

--- a/solution.py
+++ b/solution.py
@@ -255,8 +255,10 @@
     last_tail = send(other_plus[2 * DEV_ROWS :], along_second(-1))
 
     total = run_phase(2, meta, tile_vals, both((other, other_minus, other_plus)), near)
-    last_head, last_tail, total, early = hold((last_head, last_tail, total, early))
-    near, away = run_phase(3, meta, tile_vals, both((last_head, last_tail)), total)
+    last_head, last_tail, total = hold((last_head, last_tail, total))
+    last = both((last_head, last_tail))
+    total, early = hold((total, early))
+    near, away = run_phase(3, meta, tile_vals, last, total)
     late = lax.ppermute(away, "rep", swap)
     summed = (near + early + late.astype(jnp.float32)).reshape(features.shape)
     neighbours = (summed / jnp.sqrt(degree.astype(jnp.float32))[:, None]).astype(jnp.bfloat16)

time: 91 us -> 87.9 us (0.966)
  waiting for transfers between devices: 32.1 us -> 25.5 us
  Pallas kernels: 22.3 us -> 27.5 us
  starting transfers between devices: 31.6 us -> 30.4 us
    pallas_call x4, Pallas kernels: 22.3 us -> 27.5 us  [run_phase(): pl.pallas_call(functools.partial(phase_kernel, phase, counts), out_shape=...]
    ppermute x23, waiting for transfers between devices: 20.9 us -> 15.9 us  [send(): return lax.ppermute(rows, 'row', pairs)]
    ppermute x1, waiting for transfers between devices: 4.61 us -> 2.09 us  [on_device(): early = lax.ppermute(away, 'rep', swap)]
    ppermute x1, starting transfers between devices: 2.04 us -> 0.73 us  [on_device(): late = lax.ppermute(away, 'rep', swap)]
  transfers between devices with their start and end apart: 25 -> 25, of which waited for: 13 -> 11; matrix products, arithmetic and copies ran while one was open for 3% -> 3% of each run, Pallas kernels for 20% -> 26%
where the time goes in v3:
time: 87.9 us; the launch traced here: 88.1 us
  starting transfers between devices  30.4 us (35%)
  Pallas kernels  27.5 us (31%)
  waiting for transfers between devices  25.5 us (29%)
  other arithmetic  1.99 us (2%)
  matrix products  1.17 us (1%)
  between operations  0.95 us (1%)
    ppermute x23, starting transfers between devices, send(): return lax.ppermute(rows, 'row', pairs)  28.2 us
    pallas_call x4, Pallas kernels, run_phase(): pl.pallas_call(functools.partial(phase_kernel, phase, counts), out_shape=...  27.5 us
    ppermute x23, waiting for transfers between devices, send(): return lax.ppermute(rows, 'row', pairs)  15.9 us
    ppermute x1, waiting for transfers between devices, on_device(): late = lax.ppermute(away, 'rep', swap)  7.45 us
    ppermute x1, waiting for transfers between devices, on_device(): early = lax.ppermute(away, 'rep', swap)  2.09 us
  transfers between devices with their start and end apart: 25, of which 11 were waited for; matrix products, arithmetic and copies ran while one was open for 3% of the time, Pallas kernels for 26%

profile of v3, /device:TPU:0, one launch (start us, length us, event | category | flops | bytes accessed | tf_op | source)
XLA Modules:
  0.0 88.1 jit_solution(2114353786622662581)
XLA Ops:
  0.0 1.7 %collective-permute-start = (bf16[512,256]{1,0:T(8,128)(2,1)}, bf16[512,256]{1,0:T(8,128)(2,1)S(1)}, u32[]{:S(2)}, u32[]{:S(2)}) collective-permute-start(bf16[512,256]{1,0:T(8,128)(2,1)} %param.9), channel_id=1, source_target_pairs={{0,16},{1,3},{2,18},{3,5},{4,20},{5,7},{6,22},{7,1},{8,24},{9,11},... | collective-permute-start | bytes 786440 | tf_op jit(solution)/shard_map/ppermute | solution.py:55
  1.7 1.6 %collective-permute-start.1 = (bf16[512,256]{1,0:T(8,128)(2,1)}, bf16[512,256]{1,0:T(8,128)(2,1)S(1)}, u32[]{:S(2)}, u32[]{:S(2)}) collective-permute-start(bf16[512,256]{1,0:T(8,128)(2,1)} %param.9), channel_id=1, source_target_pairs={{0,48},{1,7},{2,50},{3,1},{4,52},{5,3},{6,54},{7,5},{8,56},{9,15},... | collective-permute-start | bytes 786440 | tf_op jit(solution)/shard_map/ppermute | solution.py:55
  3.3 2.1 %collective-permute-start.2 = (bf16[512,256]{1,0:T(8,128)(2,1)}, bf16[512,256]{1,0:T(8,128)(2,1)S(1)}, u32[]{:S(2)}, u32[]{:S(2)}) collective-permute-start(bf16[512,256]{1,0:T(8,128)(2,1)} %param.9), channel_id=1, source_target_pairs={{0,32},{1,5},{2,34},{3,7},{4,36},{5,1},{6,38},{7,3},{8,40},{9,13},... | collective-permute-start | bytes 786440 | tf_op jit(solution)/shard_map/ppermute | solution.py:55
  5.4 3.0 %collective-permute-start.3 = (bf16[512,256]{1,0:T(8,128)(2,1)}, bf16[512,256]{1,0:T(8,128)(2,1)S(1)}, u32[]{:S(2)}, u32[]{:S(2)}) collective-permute-start(bf16[512,256]{1,0:T(8,128)(2,1)} %param.9), channel_id=1, source_target_pairs={{0,8},{1,9},{2,10},{3,11},{4,12},{5,13},{6,14},{7,15},{8,0},{9,1},... | collective-permute-start | bytes 786440 | tf_op jit(solution)/shard_map/ppermute | solution.py:55
  9.1 0.1 stack.259
  9.3 0.2 convert_reduce_fusion.2
  9.5 0.1 fusion.4
  9.6 0.3 convert_reduce_fusion
  10.0 0.1 convert_reduce_fusion.1
  10.1 0.7 select_reduce_fusion
  10.9 0.1 sub.124
  11.0 0.1 fusion.14
  11.1 0.1 concatenate.12.meta
  11.2 0.8 collective-permute-done.2
  12.0 3.0 %collective-permute-done.3 = bf16[512,256]{1,0:T(8,128)(2,1)S(1)} collective-permute-done((bf16[512,256]{1,0:T(8,128)(2,1)}, bf16[512,256]{1,0:T(8,128)(2,1)S(1)}, u32[]{:S(2)}, u32[]{:S(2)}) %collective-permute-start.3) | collective-permute-done | bytes 262176 | tf_op jit(solution)/shard_map/ppermute | solution.py:55
  15.1 0.1 collective-permute-start.9
  15.2 1.1 %collective-permute-start.7 = (bf16[2048,256]{1,0:T(8,128)(2,1)S(1)}, bf16[2048,256]{1,0:T(8,128)(2,1)S(1)}, u32[]{:S(2)}, u32[]{:S(2)}) collective-permute-start(bf16[2048,256]{1,0:T(8,128)(2,1)S(1)} %constant_dynamic-update-slice_fusion.2), channel_id=1, source_target_pairs={{0,2},{1,17},{2,4},{3,19},{4,6},{5,21},{6,0},{7,23},{8,10},{9,25},... | collective-permute-start | bytes 3145736 | tf_op jit(solution)/shard_map/ppermute | solution.py:55
  16.3 2.2 %collective-permute-start.8 = (bf16[2048,256]{1,0:T(8,128)(2,1)S(1)}, bf16[2048,256]{1,0:T(8,128)(2,1)S(1)}, u32[]{:S(2)}, u32[]{:S(2)}) collective-permute-start(bf16[2048,256]{1,0:T(8,128)(2,1)S(1)} %constant_dynamic-update-slice_fusion.2), channel_id=1, source_target_pairs={{0,6},{1,49},{2,0},{3,51},{4,2},{5,53},{6,4},{7,55},{8,14},{9,57},... | collective-permute-start | bytes 3145736 | tf_op jit(solution)/shard_map/ppermute | solution.py:55
  18.5 3.1 %collective-permute-start.4 = (bf16[1536,256]{1,0:T(8,128)(2,1)S(1)}, bf16[1536,256]{1,0:T(8,128)(2,1)S(1)}, u32[]{:S(2)}, u32[]{:S(2)}) collective-permute-start(bf16[1536,256]{1,0:T(8,128)(2,1)S(1)} %pad_maximum_fusion), channel_id=1, source_target_pairs={{0,8},{1,9},{2,10},{3,11},{4,12},{5,13},{6,14},{7,15},{8,0},{9,1},... | collective-permute-start | bytes 2359304 | tf_op jit(solution)/shard_map/ppermute | solution.py:55
  21.6 5.0 %phase.4.refs_8_ = f32[8,128,256]{2,1,0:T(8,128)S(1)} custom-call(s32[2185]{0:T(1024)S(1)} %concatenate.12.meta, bf16[704,128,128]{2,1,0:T(8,128)(2,1)} %tiles.7, bf16[16,128,256]{2,1,0:T(8,128)(2,1)S(1)} %bitcast.101, bf16[16,128,256]{2,1,0:T(8,128)(2,1)S(1)} %bitcast.108), custom_call_target="tpu_custom_call" | custom-call | flops 1073741824 | bytes 4194304 | tf_op jit(solution)/shard_map/phase/pallas_call | solution.py:195
  26.7 4.6 %collective-permute-done.7 = bf16[2048,256]{1,0:T(8,128)(2,1)S(1)} collective-permute-done((bf16[2048,256]{1,0:T(8,128)(2,1)S(1)}, bf16[2048,256]{1,0:T(8,128)(2,1)S(1)}, u32[]{:S(2)}, u32[]{:S(2)}) %collective-permute-start.7) | collective-permute-done | bytes 1048608 | tf_op jit(solution)/shard_map/ppermute | solution.py:55
  31.3 1.2 %collective-permute-start.10 = (bf16[1024,256]{1,0:T(8,128)(2,1)S(1)}, bf16[1024,256]{1,0:T(8,128)(2,1)S(1)}, u32[]{:S(2)}, u32[]{:S(2)}) collective-permute-start(bf16[1024,256]{1,0:T(8,128)(2,1)S(1)} %slice.14), channel_id=1, source_target_pairs={{0,2},{1,17},{2,4},{3,19},{4,6},{5,21},{6,0},{7,23},{8,10},{9,25},... | collective-permute-start | bytes 1572872 | tf_op jit(solution)/shard_map/ppermute | solution.py:55
  32.5 0.8 collective-permute-start.13
  33.3 3.2 %collective-permute-start.11 = (bf16[1024,256]{1,0:T(8,128)(2,1)S(1)}, bf16[1024,256]{1,0:T(8,128)(2,1)S(1)}, u32[]{:S(2)}, u32[]{:S(2)}) collective-permute-start(bf16[1024,256]{1,0:T(8,128)(2,1)S(1)} %slice.15), channel_id=1, source_target_pairs={{0,6},{1,49},{2,0},{3,51},{4,2},{5,53},{6,4},{7,55},{8,14},{9,57},... | collective-permute-start | bytes 1572872 | tf_op jit(solution)/shard_map/ppermute | solution.py:55
  36.5 2.9 %collective-permute-done.4 = bf16[1536,256]{1,0:T(8,128)(2,1)S(1)} collective-permute-done((bf16[1536,256]{1,0:T(8,128)(2,1)S(1)}, bf16[1536,256]{1,0:T(8,128)(2,1)S(1)}, u32[]{:S(2)}, u32[]{:S(2)}) %collective-permute-start.4) | collective-permute-done | bytes 786464 | tf_op jit(solution)/shard_map/ppermute | solution.py:55
  39.5 0.8 collective-permute-start.5
  40.3 1.5 %collective-permute-done.10 = bf16[1024,256]{1,0:T(8,128)(2,1)S(1)} collective-permute-done((bf16[1024,256]{1,0:T(8,128)(2,1)S(1)}, bf16[1024,256]{1,0:T(8,128)(2,1)S(1)}, u32[]{:S(2)}, u32[]{:S(2)}) %collective-permute-start.10) | collective-permute-done | bytes 524320 | tf_op jit(solution)/shard_map/ppermute | solution.py:55
  41.8 2.0 %collective-permute-start.6 = (bf16[2048,256]{1,0:T(8,128)(2,1)S(1)}, bf16[2048,256]{1,0:T(8,128)(2,1)S(1)}, u32[]{:S(2)}, u32[]{:S(2)}) collective-permute-start(bf16[2048,256]{1,0:T(8,128)(2,1)S(1)} %constant_dynamic-update-slice_fusion), channel_id=1, source_target_pairs={{0,6},{1,49},{2,0},{3,51},{4,2},{5,53},{6,4},{7,55},{8,14},{9,57},... | collective-permute-start | bytes 3145736 | tf_op jit(solution)/shard_map/ppermute | solution.py:55
  43.8 0.5 collective-permute-start.15
  44.3 0.1 collective-permute-start.18
  44.4 1.3 %collective-permute-done.14 = bf16[1024,256]{1,0:T(8,128)(2,1)S(1)} collective-permute-done((bf16[1024,256]{1,0:T(8,128)(2,1)S(1)}, bf16[1024,256]{1,0:T(8,128)(2,1)S(1)}, u32[]{:S(2)}, u32[]{:S(2)}) %collective-permute-start.14) | collective-permute-done | bytes 524320 | tf_op jit(solution)/shard_map/ppermute | solution.py:55
  45.7 0.7 collective-permute-done.15
  46.4 9.1 %phase.5 = (f32[4,128,256]{2,1,0:T(8,128)S(1)}, f32[4,128,256]{2,1,0:T(8,128)S(1)}) custom-call(s32[2185]{0:T(1024)S(1)} %concatenate.12.meta, bf16[704,128,128]{2,1,0:T(8,128)(2,1)} %tiles.7, bf16[16,128,256]{2,1,0:T(8,128)(2,1)S(1)} %bitcast.97, bf16[16,128,256]{2,1,0:T(8,128)(2,1)S(1)} %bitcast.98, bf16[8,128,256]{2,1,0:T(8,128)(2,1)S(1)} %bitcast.109, ...), custom_call_target="tpu_custom_call" | custom-call | flops 3221225472 | bytes 12582912 | tf_op jit(solution)/shard_map/phase/pallas_call | solution.py:195
  55.6 1.0 %collective-permute-done.6 = bf16[2048,256]{1,0:T(8,128)(2,1)S(1)} collective-permute-done((bf16[2048,256]{1,0:T(8,128)(2,1)S(1)}, bf16[2048,256]{1,0:T(8,128)(2,1)S(1)}, u32[]{:S(2)}, u32[]{:S(2)}) %collective-permute-start.6) | collective-permute-done | bytes 1048608 | tf_op jit(solution)/shard_map/ppermute | solution.py:55
  56.6 0.5 collective-permute-start.20
  57.2 3.5 %collective-permute-start.17 = (bf16[1024,256]{1,0:T(8,128)(2,1)S(1)}, bf16[1024,256]{1,0:T(8,128)(2,1)S(1)}, u32[]{:S(2)}, u32[]{:S(2)}) collective-permute-start(bf16[1024,256]{1,0:T(8,128)(2,1)S(1)} %slice.17), channel_id=1, source_target_pairs={{0,6},{1,49},{2,0},{3,51},{4,2},{5,53},{6,4},{7,55},{8,14},{9,57},... | collective-permute-start | bytes 1572872 | tf_op jit(solution)/shard_map/ppermute | solution.py:55
  60.7 1.5 %collective-permute-start.23 = (f32[4,128,256]{2,1,0:T(8,128)S(1)}, f32[4,128,256]{2,1,0:T(8,128)S(1)}, u32[]{:S(2)}, u32[]{:S(2)}) collective-permute-start(f32[4,128,256]{2,1,0:T(8,128)S(1)} %get-tuple-element.40), channel_id=1, source_target_pairs={{0,64},{64,0},{1,65},{65,1},{2,66},{66,2},{3,67},{67,3},{4,68},{68... | collective-permute-start | bytes 1572872 | tf_op jit(solution)/shard_map/ppermute | solution.py:252
  62.2 8.9 %phase.6.refs_4_ = f32[8,128,256]{2,1,0:T(8,128)S(1)} custom-call(s32[2185]{0:T(1024)S(1)} %concatenate.12.meta, bf16[704,128,128]{2,1,0:T(8,128)(2,1)} %tiles.7, bf16[16,128,256]{2,1,0:T(8,128)(2,1)S(1)} %bitcast.102, bf16[16,128,256]{2,1,0:T(8,128)(2,1)S(1)} %bitcast.99, bf16[16,128,256]{2,1,0:T(8,128)(2,1)S(1)} %bitcast.100, ...), custom_call_target="tpu_custom_call" | custom-call | flops 3221225472 | bytes 12582912 | tf_op jit(solution)/shard_map/phase/pallas_call | solution.py:195
  71.2 0.1 collective-permute-start.21
  71.3 0.5 collective-permute-start.22
  71.8 2.1 %collective-permute-done.23 = f32[4,128,256]{2,1,0:T(8,128)S(1)} collective-permute-done((f32[4,128,256]{2,1,0:T(8,128)S(1)}, f32[4,128,256]{2,1,0:T(8,128)S(1)}, u32[]{:S(2)}, u32[]{:S(2)}) %collective-permute-start.23) | collective-permute-done | bytes 524320 | tf_op jit(solution)/shard_map/ppermute | solution.py:252
  73.9 4.5 %phase.7 = (f32[4,128,256]{2,1,0:T(8,128)S(1)}, bf16[4,128,256]{2,1,0:T(8,128)(2,1)S(1)}) custom-call(s32[2185]{0:T(1024)S(1)} %concatenate.12.meta, bf16[704,128,128]{2,1,0:T(8,128)(2,1)} %tiles.7, bf16[8,128,256]{2,1,0:T(8,128)(2,1)S(1)} %bitcast.113, bf16[8,128,256]{2,1,0:T(8,128)(2,1)S(1)} %bitcast.114, bf16[8,128,256]{2,1,0:T(8,128)(2,1)S(1)} %bitcast.115, ...), custom_call_target="tpu_custom_call" | custom-call | flops 1073741824 | bytes 4194304 | tf_op jit(solution)/shard_map/phase/pallas_call | solution.py:195
  78.5 0.7 collective-permute-start.24
  79.2 0.2 convolution_add_fusion.1
  79.4 7.4 %collective-permute-done.24 = bf16[4,128,256]{2,1,0:T(8,128)(2,1)S(1)} collective-permute-done((bf16[4,128,256]{2,1,0:T(8,128)(2,1)S(1)}, bf16[4,128,256]{2,1,0:T(8,128)(2,1)S(1)}, u32[]{:S(2)}, u32[]{:S(2)}) %collective-permute-start.24) | collective-permute-done | bytes 262176 | tf_op jit(solution)/shard_map/ppermute | solution.py:262
  86.9 0.1 convert_add_fusion
  87.0 0.1 fusion.3
  87.1 0.9 %fusion.2 = bf16[512,256]{1,0:T(8,128)(2,1)} fusion(f32[512,256]{1,0:T(8,128)S(1)} %convolution_add_fusion.1, bf16[512,256]{1,0:T(8,128)(2,1)S(1)} %fusion.3, bf16[256,256]{1,0:T(8,128)(2,1)S(1)} %copy-done.2), kind=kOutput, calls=%fused_computation.8 | convolution fusion | flops 67502080 | bytes 1179648 | tf_op jit(solution)/shard_map/dot_general | solution.py:266
  (51 shorter events, 0.7 us)
Async XLA Ops:
  0.0 79.2 %copy-start = (bf16[256,256]{1,0:T(8,128)(2,1)S(1)}, bf16[256,256]{1,0:T(8,128)(2,1)}, u32[]{:S(2)}) copy-start(bf16[256,256]{1,0:T(8,128)(2,1)} %param.15) | copy-start | bytes 393220
  0.0 11.2 %copy-start.1 = (bf16[512,256]{1,0:T(8,128)(2,1)S(1)}, bf16[512,256]{1,0:T(8,128)(2,1)}, u32[]{:S(2)}) copy-start(bf16[512,256]{1,0:T(8,128)(2,1)} %param.9) | copy-start | bytes 786436
  0.0 9.1 %copy-start.4 = (s32[704]{0:T(1024)S(1)}, s32[704]{0:T(1024)}, u32[]{:S(2)}) copy-start(s32[704]{0:T(1024)} %param.12) | copy-start | bytes 8452
  0.0 9.6 %copy-start.3 = (s32[704]{0:T(1024)S(1)}, s32[704]{0:T(1024)}, u32[]{:S(2)}) copy-start(s32[704]{0:T(1024)} %param.11) | copy-start | bytes 8452
  0.0 11.2 %collective-permute-start = (bf16[512,256]{1,0:T(8,128)(2,1)}, bf16[512,256]{1,0:T(8,128)(2,1)S(1)}, u32[]{:S(2)}, u32[]{:S(2)}) collective-permute-start(bf16[512,256]{1,0:T(8,128)(2,1)} %param.9), channel_id=1, source_target_pairs={{0,16},{1,3},{2,18},{3,5},{4,20},{5,7},{6,22},{7,1},{8,24},{9,11},... | collective-permute-start | bytes 786440 | tf_op jit(solution)/shard_map/ppermute | solution.py:55
  1.7 9.5 %collective-permute-start.1 = (bf16[512,256]{1,0:T(8,128)(2,1)}, bf16[512,256]{1,0:T(8,128)(2,1)S(1)}, u32[]{:S(2)}, u32[]{:S(2)}) collective-permute-start(bf16[512,256]{1,0:T(8,128)(2,1)} %param.9), channel_id=1, source_target_pairs={{0,48},{1,7},{2,50},{3,1},{4,52},{5,3},{6,54},{7,5},{8,56},{9,15},... | collective-permute-start | bytes 786440 | tf_op jit(solution)/shard_map/ppermute | solution.py:55
  3.3 8.7 %collective-permute-start.2 = (bf16[512,256]{1,0:T(8,128)(2,1)}, bf16[512,256]{1,0:T(8,128)(2,1)S(1)}, u32[]{:S(2)}, u32[]{:S(2)}) collective-permute-start(bf16[512,256]{1,0:T(8,128)(2,1)} %param.9), channel_id=1, source_target_pairs={{0,32},{1,5},{2,34},{3,7},{4,36},{5,1},{6,38},{7,3},{8,40},{9,13},... | collective-permute-start | bytes 786440 | tf_op jit(solution)/shard_map/ppermute | solution.py:55
  5.4 9.6 %collective-permute-start.3 = (bf16[512,256]{1,0:T(8,128)(2,1)}, bf16[512,256]{1,0:T(8,128)(2,1)S(1)}, u32[]{:S(2)}, u32[]{:S(2)}) collective-permute-start(bf16[512,256]{1,0:T(8,128)(2,1)} %param.9), channel_id=1, source_target_pairs={{0,8},{1,9},{2,10},{3,11},{4,12},{5,13},{6,14},{7,15},{8,0},{9,1},... | collective-permute-start | bytes 786440 | tf_op jit(solution)/shard_map/ppermute | solution.py:55
  15.1 6.6 %collective-permute-start.9 = (bf16[2048,256]{1,0:T(8,128)(2,1)S(1)}, bf16[2048,256]{1,0:T(8,128)(2,1)S(1)}, u32[]{:S(2)}, u32[]{:S(2)}) collective-permute-start(bf16[2048,256]{1,0:T(8,128)(2,1)S(1)} %constant_dynamic-update-slice_fusion.2), channel_id=1, source_target_pairs={{0,1},{1,0},{2,3},{3,2},{4,5},{5,4},{6,7},{7,6},{8,9},{9,8},{10,11... | collective-permute-start | bytes 3145736 | tf_op jit(solution)/shard_map/ppermute | solution.py:55
  15.2 16.1 %collective-permute-start.7 = (bf16[2048,256]{1,0:T(8,128)(2,1)S(1)}, bf16[2048,256]{1,0:T(8,128)(2,1)S(1)}, u32[]{:S(2)}, u32[]{:S(2)}) collective-permute-start(bf16[2048,256]{1,0:T(8,128)(2,1)S(1)} %constant_dynamic-update-slice_fusion.2), channel_id=1, source_target_pairs={{0,2},{1,17},{2,4},{3,19},{4,6},{5,21},{6,0},{7,23},{8,10},{9,25},... | collective-permute-start | bytes 3145736 | tf_op jit(solution)/shard_map/ppermute | solution.py:55
  16.3 15.0 %collective-permute-start.8 = (bf16[2048,256]{1,0:T(8,128)(2,1)S(1)}, bf16[2048,256]{1,0:T(8,128)(2,1)S(1)}, u32[]{:S(2)}, u32[]{:S(2)}) collective-permute-start(bf16[2048,256]{1,0:T(8,128)(2,1)S(1)} %constant_dynamic-update-slice_fusion.2), channel_id=1, source_target_pairs={{0,6},{1,49},{2,0},{3,51},{4,2},{5,53},{6,4},{7,55},{8,14},{9,57},... | collective-permute-start | bytes 3145736 | tf_op jit(solution)/shard_map/ppermute | solution.py:55
  18.5 20.9 %collective-permute-start.4 = (bf16[1536,256]{1,0:T(8,128)(2,1)S(1)}, bf16[1536,256]{1,0:T(8,128)(2,1)S(1)}, u32[]{:S(2)}, u32[]{:S(2)}) collective-permute-start(bf16[1536,256]{1,0:T(8,128)(2,1)S(1)} %pad_maximum_fusion), channel_id=1, source_target_pairs={{0,8},{1,9},{2,10},{3,11},{4,12},{5,13},{6,14},{7,15},{8,0},{9,1},... | collective-permute-start | bytes 2359304 | tf_op jit(solution)/shard_map/ppermute | solution.py:55
  31.2 12.5 %collective-permute-start.12 = (bf16[2048,256]{1,0:T(8,128)(2,1)S(1)}, bf16[2048,256]{1,0:T(8,128)(2,1)S(1)}, u32[]{:S(2)}, u32[]{:S(2)}) collective-permute-start(bf16[2048,256]{1,0:T(8,128)(2,1)S(1)} %collective-permute-done.7), channel_id=1, source_target_pairs={{0,1},{1,0},{2,3},{3,2},{4,5},{5,4},{6,7},{7,6},{8,9},{9,8},{10,11... | collective-permute-start | bytes 3145736 | tf_op jit(solution)/shard_map/ppermute | solution.py:55
  31.3 10.5 %collective-permute-start.10 = (bf16[1024,256]{1,0:T(8,128)(2,1)S(1)}, bf16[1024,256]{1,0:T(8,128)(2,1)S(1)}, u32[]{:S(2)}, u32[]{:S(2)}) collective-permute-start(bf16[1024,256]{1,0:T(8,128)(2,1)S(1)} %slice.14), channel_id=1, source_target_pairs={{0,2},{1,17},{2,4},{3,19},{4,6},{5,21},{6,0},{7,23},{8,10},{9,25},... | collective-permute-start | bytes 1572872 | tf_op jit(solution)/shard_map/ppermute | solution.py:55
  32.5 11.8 %collective-permute-start.13 = (bf16[2048,256]{1,0:T(8,128)(2,1)S(1)}, bf16[2048,256]{1,0:T(8,128)(2,1)S(1)}, u32[]{:S(2)}, u32[]{:S(2)}) collective-permute-start(bf16[2048,256]{1,0:T(8,128)(2,1)S(1)} %collective-permute-done.8), channel_id=1, source_target_pairs={{0,1},{1,0},{2,3},{3,2},{4,5},{5,4},{6,7},{7,6},{8,9},{9,8},{10,11... | collective-permute-start | bytes 3145736 | tf_op jit(solution)/shard_map/ppermute | solution.py:55
  33.3 10.5 %collective-permute-start.11 = (bf16[1024,256]{1,0:T(8,128)(2,1)S(1)}, bf16[1024,256]{1,0:T(8,128)(2,1)S(1)}, u32[]{:S(2)}, u32[]{:S(2)}) collective-permute-start(bf16[1024,256]{1,0:T(8,128)(2,1)S(1)} %slice.15), channel_id=1, source_target_pairs={{0,6},{1,49},{2,0},{3,51},{4,2},{5,53},{6,4},{7,55},{8,14},{9,57},... | collective-permute-start | bytes 1572872 | tf_op jit(solution)/shard_map/ppermute | solution.py:55
  39.5 16.1 %collective-permute-start.5 = (bf16[2048,256]{1,0:T(8,128)(2,1)S(1)}, bf16[2048,256]{1,0:T(8,128)(2,1)S(1)}, u32[]{:S(2)}, u32[]{:S(2)}) collective-permute-start(bf16[2048,256]{1,0:T(8,128)(2,1)S(1)} %constant_dynamic-update-slice_fusion), channel_id=1, source_target_pairs={{0,2},{1,17},{2,4},{3,19},{4,6},{5,21},{6,0},{7,23},{8,10},{9,25},... | collective-permute-start | bytes 3145736 | tf_op jit(solution)/shard_map/ppermute | solution.py:55
  41.8 14.8 %collective-permute-start.6 = (bf16[2048,256]{1,0:T(8,128)(2,1)S(1)}, bf16[2048,256]{1,0:T(8,128)(2,1)S(1)}, u32[]{:S(2)}, u32[]{:S(2)}) collective-permute-start(bf16[2048,256]{1,0:T(8,128)(2,1)S(1)} %constant_dynamic-update-slice_fusion), channel_id=1, source_target_pairs={{0,6},{1,49},{2,0},{3,51},{4,2},{5,53},{6,4},{7,55},{8,14},{9,57},... | collective-permute-start | bytes 3145736 | tf_op jit(solution)/shard_map/ppermute | solution.py:55
  43.8 1.9 %collective-permute-start.14 = (bf16[1024,256]{1,0:T(8,128)(2,1)S(1)}, bf16[1024,256]{1,0:T(8,128)(2,1)S(1)}, u32[]{:S(2)}, u32[]{:S(2)}) collective-permute-start(bf16[1024,256]{1,0:T(8,128)(2,1)S(1)} %collective-permute-done.10), channel_id=1, source_target_pairs={{0,1},{1,0},{2,3},{3,2},{4,5},{5,4},{6,7},{7,6},{8,9},{9,8},{10,11... | collective-permute-start | bytes 1572872 | tf_op jit(solution)/shard_map/ppermute | solution.py:55
  43.8 2.7 %collective-permute-start.15 = (bf16[1024,256]{1,0:T(8,128)(2,1)S(1)}, bf16[1024,256]{1,0:T(8,128)(2,1)S(1)}, u32[]{:S(2)}, u32[]{:S(2)}) collective-permute-start(bf16[1024,256]{1,0:T(8,128)(2,1)S(1)} %collective-permute-done.11), channel_id=1, source_target_pairs={{0,1},{1,0},{2,3},{3,2},{4,5},{5,4},{6,7},{7,6},{8,9},{9,8},{10,11... | collective-permute-start | bytes 1572872 | tf_op jit(solution)/shard_map/ppermute | solution.py:55
  44.3 16.4 %collective-permute-start.18 = (bf16[2048,256]{1,0:T(8,128)(2,1)S(1)}, bf16[2048,256]{1,0:T(8,128)(2,1)S(1)}, u32[]{:S(2)}, u32[]{:S(2)}) collective-permute-start(bf16[2048,256]{1,0:T(8,128)(2,1)S(1)} %constant_dynamic-update-slice_fusion), channel_id=1, source_target_pairs={{0,1},{1,0},{2,3},{3,2},{4,5},{5,4},{6,7},{7,6},{8,9},{9,8},{10,11... | collective-permute-start | bytes 3145736 | tf_op jit(solution)/shard_map/ppermute | solution.py:55
  56.6 5.7 %collective-permute-start.19 = (bf16[2048,256]{1,0:T(8,128)(2,1)S(1)}, bf16[2048,256]{1,0:T(8,128)(2,1)S(1)}, u32[]{:S(2)}, u32[]{:S(2)}) collective-permute-start(bf16[2048,256]{1,0:T(8,128)(2,1)S(1)} %collective-permute-done.5), channel_id=1, source_target_pairs={{0,1},{1,0},{2,3},{3,2},{4,5},{5,4},{6,7},{7,6},{8,9},{9,8},{10,11... | collective-permute-start | bytes 3145736 | tf_op jit(solution)/shard_map/ppermute | solution.py:55
  56.6 5.7 %collective-permute-start.20 = (bf16[2048,256]{1,0:T(8,128)(2,1)S(1)}, bf16[2048,256]{1,0:T(8,128)(2,1)S(1)}, u32[]{:S(2)}, u32[]{:S(2)}) collective-permute-start(bf16[2048,256]{1,0:T(8,128)(2,1)S(1)} %collective-permute-done.6), channel_id=1, source_target_pairs={{0,1},{1,0},{2,3},{3,2},{4,5},{5,4},{6,7},{7,6},{8,9},{9,8},{10,11... | collective-permute-start | bytes 3145736 | tf_op jit(solution)/shard_map/ppermute | solution.py:55
  57.1 14.0 %collective-permute-start.16 = (bf16[1024,256]{1,0:T(8,128)(2,1)S(1)}, bf16[1024,256]{1,0:T(8,128)(2,1)S(1)}, u32[]{:S(2)}, u32[]{:S(2)}) collective-permute-start(bf16[1024,256]{1,0:T(8,128)(2,1)S(1)} %slice.16), channel_id=1, source_target_pairs={{0,2},{1,17},{2,4},{3,19},{4,6},{5,21},{6,0},{7,23},{8,10},{9,25},... | collective-permute-start | bytes 1572872 | tf_op jit(solution)/shard_map/ppermute | solution.py:55
  57.2 13.9 %collective-permute-start.17 = (bf16[1024,256]{1,0:T(8,128)(2,1)S(1)}, bf16[1024,256]{1,0:T(8,128)(2,1)S(1)}, u32[]{:S(2)}, u32[]{:S(2)}) collective-permute-start(bf16[1024,256]{1,0:T(8,128)(2,1)S(1)} %slice.17), channel_id=1, source_target_pairs={{0,6},{1,49},{2,0},{3,51},{4,2},{5,53},{6,4},{7,55},{8,14},{9,57},... | collective-permute-start | bytes 1572872 | tf_op jit(solution)/shard_map/ppermute | solution.py:55
  60.7 13.1 %collective-permute-start.23 = (f32[4,128,256]{2,1,0:T(8,128)S(1)}, f32[4,128,256]{2,1,0:T(8,128)S(1)}, u32[]{:S(2)}, u32[]{:S(2)}) collective-permute-start(f32[4,128,256]{2,1,0:T(8,128)S(1)} %get-tuple-element.40), channel_id=1, source_target_pairs={{0,64},{64,0},{1,65},{65,1},{2,66},{66,2},{3,67},{67,3},{4,68},{68... | collective-permute-start | bytes 1572872 | tf_op jit(solution)/shard_map/ppermute | solution.py:252
  71.2 2.7 %collective-permute-start.21 = (bf16[1024,256]{1,0:T(8,128)(2,1)S(1)}, bf16[1024,256]{1,0:T(8,128)(2,1)S(1)}, u32[]{:S(2)}, u32[]{:S(2)}) collective-permute-start(bf16[1024,256]{1,0:T(8,128)(2,1)S(1)} %collective-permute-done.16), channel_id=1, source_target_pairs={{0,1},{1,0},{2,3},{3,2},{4,5},{5,4},{6,7},{7,6},{8,9},{9,8},{10,11... | collective-permute-start | bytes 1572872 | tf_op jit(solution)/shard_map/ppermute | solution.py:55
  71.3 2.6 %collective-permute-start.22 = (bf16[1024,256]{1,0:T(8,128)(2,1)S(1)}, bf16[1024,256]{1,0:T(8,128)(2,1)S(1)}, u32[]{:S(2)}, u32[]{:S(2)}) collective-permute-start(bf16[1024,256]{1,0:T(8,128)(2,1)S(1)} %collective-permute-done.17), channel_id=1, source_target_pairs={{0,1},{1,0},{2,3},{3,2},{4,5},{5,4},{6,7},{7,6},{8,9},{9,8},{10,11... | collective-permute-start | bytes 1572872 | tf_op jit(solution)/shard_map/ppermute | solution.py:55
  73.9 5.3 %copy-start.5 = (s32[512]{0:T(512)S(1)}, s32[512]{0:T(512)}, u32[]{:S(2)}) copy-start(s32[512]{0:T(512)} %param.14) | copy-start | bytes 6148
  73.9 5.3 %copy-start.6 = (f32[256]{0:T(256)S(1)}, f32[256]{0:T(256)}, u32[]{:S(2)}) copy-start(f32[256]{0:T(256)} %param.17) | copy-start | bytes 3076
  78.4 8.7 %copy-start.2 = (bf16[256,256]{1,0:T(8,128)(2,1)S(1)}, bf16[256,256]{1,0:T(8,128)(2,1)}, u32[]{:S(2)}) copy-start(bf16[256,256]{1,0:T(8,128)(2,1)} %param.16) | copy-start | bytes 393220
  78.5 8.4 %collective-permute-start.24 = (bf16[4,128,256]{2,1,0:T(8,128)(2,1)S(1)}, bf16[4,128,256]{2,1,0:T(8,128)(2,1)S(1)}, u32[]{:S(2)}, u32[]{:S(2)}) collective-permute-start(bf16[4,128,256]{2,1,0:T(8,128)(2,1)S(1)} %get-tuple-element.44), channel_id=1, source_target_pairs={{0,64},{64,0},{1,65},{65,1},{2,66},{66,2},{3,67},{67,3},{4,68},{68... | collective-permute-start | bytes 786440 | tf_op jit(solution)/shard_map/ppermute | solution.py:262

commit v4 on v3

--- a/solution.py
+++ b/solution.py
@@ -23,9 +23,6 @@
 GROUP_STEPS = GROUP * DEV_BLOCKS // DEPTH
 SLOTS = STEP * GROUP_STEPS * GROUPS
 OWNERS = GROUP * GROUPS
-STARTS, FILLS = SLOTS, SLOTS + OWNERS
-STEPS_AT = FILLS + OWNERS
-HALF_AT = STEPS_AT + GROUPS
 SPLIT = (1, 3)
 VMEM_BYTES = 44 << 20
 LINE = (0, -1, 1, 2)
@@ -121,8 +118,11 @@
         before, refs = refs[0], refs[1:]
     fbuf, tbuf, acc, sem = refs[-4:]
     outs = refs[:-4]
-    half = meta[HALF_AT]
     groups = PHASE_GROUPS[phase]
+    starts_at = groups * GROUP_STEPS * STEP
+    fills_at = starts_at + groups * GROUP
+    steps_at = fills_at + groups * GROUP
+    half = meta[steps_at + groups]
     arrivals = [[] for _ in range(groups)]
     owner = 0
     for piece, count in zip(pieces, counts):
@@ -132,12 +132,12 @@
         owner += count
 
     def tile_copy(i, part):
-        start = meta[STARTS + GROUP_BASE[phase] * GROUP + i] + part * CHUNK
+        start = meta[starts_at + i] + part * CHUNK
         held = tbuf.at[pl.ds(i * OWNER_TILES + part * CHUNK, CHUNK)]
         return pltpu.make_async_copy(tiles.at[pl.ds(start, CHUNK)], held, sem.at[i // GROUP])
 
     def over(i):
-        return meta[FILLS + GROUP_BASE[phase] * GROUP + i] > CHUNK
+        return meta[fills_at + i] > CHUNK
 
     for group in range(groups):
         mine = range(group * GROUP, (group + 1) * GROUP)
@@ -160,7 +160,7 @@
             copy.wait()
         for i in range(group * GROUP, (group + 1) * GROUP):
             pl.when(over(i))(tile_copy(i, 1).wait)
-        listed = (GROUP_BASE[phase] + group) * GROUP_STEPS * STEP
+        listed = group * GROUP_STEPS * STEP
 
         def run(step, carry, listed=listed):
             for d in range(DSTS):
@@ -171,7 +171,7 @@
                 acc[d] += jnp.dot(left, right, preferred_element_type=jnp.float32)
             return carry
 
-        lax.fori_loop(0, meta[STEPS_AT + GROUP_BASE[phase] + group], run, 0)
+        lax.fori_loop(0, meta[steps_at + group], run, 0)
     if len(outs) == 2:
         near, away = outs
         near[...] = acc[pl.ds(half * DEV_BLOCKS, DEV_BLOCKS)]
@@ -231,13 +231,19 @@
     from_far = send(features, along_first(2))
     across = send(features, shift(x=1))
     listed, starts, fills, steps = work_list(tile_dst, tile_src, tile_count[0], row)
-    meta = jnp.concatenate([listed, starts, fills, steps, rep[None]]).astype(jnp.int32)
+    meta = []
+    for base, groups in zip(GROUP_BASE, PHASE_GROUPS):
+        parts = [
+            lax.slice_in_dim(values, base * size, (base + groups) * size)
+            for values, size in ((listed, GROUP_STEPS * STEP), (starts, GROUP), (fills, GROUP), (steps, 1))
+        ]
+        meta.append(jnp.concatenate(parts + [rep[None]]).astype(jnp.int32))
     from_minus, from_plus, from_far, across, meta = hold((from_minus, from_plus, from_far, across, meta))
     line = jnp.concatenate([features, from_minus, from_plus, from_far])
     rest = send(line[DEV_ROWS:], shift(x=1))
     minus = send(line, along_second(1))
     plus = send(line, along_second(-1))
-    total = run_phase(0, meta, tile_vals, both((line,)))
+    total = run_phase(0, meta[0], tile_vals, both((line,)))
     minus, plus, total = hold((minus, plus, total))
     far_head = send(minus[: 2 * DEV_ROWS], along_second(1))
     far_tail = send(plus[2 * DEV_ROWS :], along_second(-1))
@@ -248,17 +254,17 @@
     far_siblings = both((far_head, far_tail))[2:]
 
     pieces = [minus, plus, far_head, far_tail] + near_siblings + far_siblings
-    near, away = run_phase(1, meta, tile_vals, pieces, total)
+    near, away = run_phase(1, meta[1], tile_vals, pieces, total)
     early = lax.ppermute(away, "rep", swap)
     other_minus, other_plus, near = hold((other_minus, other_plus, near))
     last_head = send(other_minus[: 2 * DEV_ROWS], along_second(1))
     last_tail = send(other_plus[2 * DEV_ROWS :], along_second(-1))
 
-    total = run_phase(2, meta, tile_vals, both((other, other_minus, other_plus)), near)
+    total = run_phase(2, meta[2], tile_vals, both((other, other_minus, other_plus)), near)
     last_head, last_tail, total = hold((last_head, last_tail, total))
     last = both((last_head, last_tail))
     total, early = hold((total, early))
-    near, away = run_phase(3, meta, tile_vals, last, total)
+    near, away = run_phase(3, meta[3], tile_vals, last, total)
     late = lax.ppermute(away, "rep", swap)
     summed = (near + early + late.astype(jnp.float32)).reshape(features.shape)
     neighbours = (summed / jnp.sqrt(degree.astype(jnp.float32))[:, None]).astype(jnp.bfloat16)

time: 87.9 us -> 87.7 us (level)
  Pallas kernels: 27.5 us -> 22.1 us
  starting transfers between devices: 30.4 us -> 32.8 us
  local copies, waits for them, and re-layouts: 0.62 us -> 2.89 us
    pallas_call x4, Pallas kernels: 27.5 us -> 22.1 us  [run_phase(): pl.pallas_call(functools.partial(phase_kernel, phase, counts), out_shape=...]
    ppermute x1, starting transfers between devices: 0.73 us -> 3.11 us  [on_device(): late = lax.ppermute(away, 'rep', swap)]
    ppermute x1, waiting for transfers between devices: 7.45 us -> 5.34 us  [on_device(): late = lax.ppermute(away, 'rep', swap)]
    ppermute x1, waiting for transfers between devices: 2.09 us -> 3.85 us  [on_device(): early = lax.ppermute(away, 'rep', swap)]
    concatenate x1 -> x4, local copies, waits for them, and re-layouts: 0.08 us -> 1.53 us  [on_device(): meta.append(jnp.concatenate(parts + [rep[None]]).astype(jnp.int32))]
    ppermute x23, waiting for transfers between devices: 15.9 us -> 16.8 us  [send(): return lax.ppermute(rows, 'row', pairs)]
  transfers between devices with their start and end apart: 25 -> 25, of which waited for: 11 -> 10; matrix products, arithmetic and copies ran while one was open for 3% -> 5% of each run, Pallas kernels for 26% -> 21%
where the time goes in v4:
time: 87.7 us; the launch traced here: 87.8 us
  starting transfers between devices  32.8 us (37%)
  waiting for transfers between devices  26 us (30%)
  Pallas kernels  22.1 us (25%)
  local copies, waits for them, and re-layouts  2.89 us (3%)
  other arithmetic  1.99 us (2%)
  matrix products  1.16 us (1%)
  between operations  0.98 us (1%)
    ppermute x23, starting transfers between devices, send(): return lax.ppermute(rows, 'row', pairs)  28.1 us
    pallas_call x4, Pallas kernels, run_phase(): pl.pallas_call(functools.partial(phase_kernel, phase, counts), out_shape=...  22.1 us
    ppermute x23, waiting for transfers between devices, send(): return lax.ppermute(rows, 'row', pairs)  16.8 us
    ppermute x1, waiting for transfers between devices, on_device(): late = lax.ppermute(away, 'rep', swap)  5.34 us
    ppermute x1, waiting for transfers between devices, on_device(): early = lax.ppermute(away, 'rep', swap)  3.85 us
    ppermute x1, starting transfers between devices, on_device(): late = lax.ppermute(away, 'rep', swap)  3.11 us
  transfers between devices with their start and end apart: 25, of which 10 were waited for; matrix products, arithmetic and copies ran while one was open for 5% of the time, Pallas kernels for 21%

profile of v4, /device:TPU:0, one launch (start us, length us, event | category | flops | bytes accessed | tf_op | source)
XLA Modules:
  0.0 87.8 jit_solution(3067586094192768107)
XLA Ops:
  0.0 1.7 %collective-permute-start = (bf16[512,256]{1,0:T(8,128)(2,1)}, bf16[512,256]{1,0:T(8,128)(2,1)S(1)}, u32[]{:S(2)}, u32[]{:S(2)}) collective-permute-start(bf16[512,256]{1,0:T(8,128)(2,1)} %param.9), channel_id=1, source_target_pairs={{0,16},{1,3},{2,18},{3,5},{4,20},{5,7},{6,22},{7,1},{8,24},{9,11},... | collective-permute-start | bytes 786440 | tf_op jit(solution)/shard_map/ppermute | solution.py:52
  1.7 1.6 %collective-permute-start.1 = (bf16[512,256]{1,0:T(8,128)(2,1)}, bf16[512,256]{1,0:T(8,128)(2,1)S(1)}, u32[]{:S(2)}, u32[]{:S(2)}) collective-permute-start(bf16[512,256]{1,0:T(8,128)(2,1)} %param.9), channel_id=1, source_target_pairs={{0,48},{1,7},{2,50},{3,1},{4,52},{5,3},{6,54},{7,5},{8,56},{9,15},... | collective-permute-start | bytes 786440 | tf_op jit(solution)/shard_map/ppermute | solution.py:52
  3.3 2.1 %collective-permute-start.2 = (bf16[512,256]{1,0:T(8,128)(2,1)}, bf16[512,256]{1,0:T(8,128)(2,1)S(1)}, u32[]{:S(2)}, u32[]{:S(2)}) collective-permute-start(bf16[512,256]{1,0:T(8,128)(2,1)} %param.9), channel_id=1, source_target_pairs={{0,32},{1,5},{2,34},{3,7},{4,36},{5,1},{6,38},{7,3},{8,40},{9,13},... | collective-permute-start | bytes 786440 | tf_op jit(solution)/shard_map/ppermute | solution.py:52
  5.4 3.0 %collective-permute-start.3 = (bf16[512,256]{1,0:T(8,128)(2,1)}, bf16[512,256]{1,0:T(8,128)(2,1)S(1)}, u32[]{:S(2)}, u32[]{:S(2)}) collective-permute-start(bf16[512,256]{1,0:T(8,128)(2,1)} %param.9), channel_id=1, source_target_pairs={{0,8},{1,9},{2,10},{3,11},{4,12},{5,13},{6,14},{7,15},{8,0},{9,1},... | collective-permute-start | bytes 786440 | tf_op jit(solution)/shard_map/ppermute | solution.py:52
  9.1 0.1 stack.259
  9.3 0.2 convert_reduce_fusion.2
  9.5 0.1 fusion.4
  9.6 0.3 convert_reduce_fusion
  10.0 0.1 convert_reduce_fusion.1
  10.3 0.7 select_reduce_fusion
  11.1 0.1 fusion.14
  11.3 0.6 fusion.26
  11.8 0.7 concatenate.24.meta
  12.8 0.6 concatenate.21.meta
  13.5 1.5 %collective-permute-done.3 = bf16[512,256]{1,0:T(8,128)(2,1)S(1)} collective-permute-done((bf16[512,256]{1,0:T(8,128)(2,1)}, bf16[512,256]{1,0:T(8,128)(2,1)S(1)}, u32[]{:S(2)}, u32[]{:S(2)}) %collective-permute-start.3) | collective-permute-done | bytes 262176 | tf_op jit(solution)/shard_map/ppermute | solution.py:52
  15.1 0.1 collective-permute-start.9
  15.2 1.1 %collective-permute-start.7 = (bf16[2048,256]{1,0:T(8,128)(2,1)S(1)}, bf16[2048,256]{1,0:T(8,128)(2,1)S(1)}, u32[]{:S(2)}, u32[]{:S(2)}) collective-permute-start(bf16[2048,256]{1,0:T(8,128)(2,1)S(1)} %constant_dynamic-update-slice_fusion.2), channel_id=1, source_target_pairs={{0,2},{1,17},{2,4},{3,19},{4,6},{5,21},{6,0},{7,23},{8,10},{9,25},... | collective-permute-start | bytes 3145736 | tf_op jit(solution)/shard_map/ppermute | solution.py:52
  16.3 2.2 %collective-permute-start.8 = (bf16[2048,256]{1,0:T(8,128)(2,1)S(1)}, bf16[2048,256]{1,0:T(8,128)(2,1)S(1)}, u32[]{:S(2)}, u32[]{:S(2)}) collective-permute-start(bf16[2048,256]{1,0:T(8,128)(2,1)S(1)} %constant_dynamic-update-slice_fusion.2), channel_id=1, source_target_pairs={{0,6},{1,49},{2,0},{3,51},{4,2},{5,53},{6,4},{7,55},{8,14},{9,57},... | collective-permute-start | bytes 3145736 | tf_op jit(solution)/shard_map/ppermute | solution.py:52
  18.5 3.1 %collective-permute-start.4 = (bf16[1536,256]{1,0:T(8,128)(2,1)S(1)}, bf16[1536,256]{1,0:T(8,128)(2,1)S(1)}, u32[]{:S(2)}, u32[]{:S(2)}) collective-permute-start(bf16[1536,256]{1,0:T(8,128)(2,1)S(1)} %pad_maximum_fusion), channel_id=1, source_target_pairs={{0,8},{1,9},{2,10},{3,11},{4,12},{5,13},{6,14},{7,15},{8,0},{9,1},... | collective-permute-start | bytes 2359304 | tf_op jit(solution)/shard_map/ppermute | solution.py:52
  21.6 4.0 %phase.4.refs_8_ = f32[8,128,256]{2,1,0:T(8,128)S(1)} custom-call(s32[274]{0:T(512)S(1)} %concatenate.21.meta, bf16[704,128,128]{2,1,0:T(8,128)(2,1)} %tiles.7, bf16[16,128,256]{2,1,0:T(8,128)(2,1)S(1)} %bitcast.102, bf16[16,128,256]{2,1,0:T(8,128)(2,1)S(1)} %bitcast.108), custom_call_target="tpu_custom_call" | custom-call | flops 1073741824 | bytes 4194304 | tf_op jit(solution)/shard_map/phase/pallas_call | solution.py:195
  25.6 5.6 %collective-permute-done.7 = bf16[2048,256]{1,0:T(8,128)(2,1)S(1)} collective-permute-done((bf16[2048,256]{1,0:T(8,128)(2,1)S(1)}, bf16[2048,256]{1,0:T(8,128)(2,1)S(1)}, u32[]{:S(2)}, u32[]{:S(2)}) %collective-permute-start.7) | collective-permute-done | bytes 1048608 | tf_op jit(solution)/shard_map/ppermute | solution.py:52
  31.3 1.2 %collective-permute-start.10 = (bf16[1024,256]{1,0:T(8,128)(2,1)S(1)}, bf16[1024,256]{1,0:T(8,128)(2,1)S(1)}, u32[]{:S(2)}, u32[]{:S(2)}) collective-permute-start(bf16[1024,256]{1,0:T(8,128)(2,1)S(1)} %slice.78), channel_id=1, source_target_pairs={{0,2},{1,17},{2,4},{3,19},{4,6},{5,21},{6,0},{7,23},{8,10},{9,25},... | collective-permute-start | bytes 1572872 | tf_op jit(solution)/shard_map/ppermute | solution.py:52
  32.5 0.7 collective-permute-start.13
  33.3 3.2 %collective-permute-start.11 = (bf16[1024,256]{1,0:T(8,128)(2,1)S(1)}, bf16[1024,256]{1,0:T(8,128)(2,1)S(1)}, u32[]{:S(2)}, u32[]{:S(2)}) collective-permute-start(bf16[1024,256]{1,0:T(8,128)(2,1)S(1)} %slice.79), channel_id=1, source_target_pairs={{0,6},{1,49},{2,0},{3,51},{4,2},{5,53},{6,4},{7,55},{8,14},{9,57},... | collective-permute-start | bytes 1572872 | tf_op jit(solution)/shard_map/ppermute | solution.py:52
  36.5 2.9 %collective-permute-done.4 = bf16[1536,256]{1,0:T(8,128)(2,1)S(1)} collective-permute-done((bf16[1536,256]{1,0:T(8,128)(2,1)S(1)}, bf16[1536,256]{1,0:T(8,128)(2,1)S(1)}, u32[]{:S(2)}, u32[]{:S(2)}) %collective-permute-start.4) | collective-permute-done | bytes 786464 | tf_op jit(solution)/shard_map/ppermute | solution.py:52
  39.5 0.8 collective-permute-start.5
  40.3 1.5 %collective-permute-done.10 = bf16[1024,256]{1,0:T(8,128)(2,1)S(1)} collective-permute-done((bf16[1024,256]{1,0:T(8,128)(2,1)S(1)}, bf16[1024,256]{1,0:T(8,128)(2,1)S(1)}, u32[]{:S(2)}, u32[]{:S(2)}) %collective-permute-start.10) | collective-permute-done | bytes 524320 | tf_op jit(solution)/shard_map/ppermute | solution.py:52
  41.8 2.0 %collective-permute-start.6 = (bf16[2048,256]{1,0:T(8,128)(2,1)S(1)}, bf16[2048,256]{1,0:T(8,128)(2,1)S(1)}, u32[]{:S(2)}, u32[]{:S(2)}) collective-permute-start(bf16[2048,256]{1,0:T(8,128)(2,1)S(1)} %constant_dynamic-update-slice_fusion), channel_id=1, source_target_pairs={{0,6},{1,49},{2,0},{3,51},{4,2},{5,53},{6,4},{7,55},{8,14},{9,57},... | collective-permute-start | bytes 3145736 | tf_op jit(solution)/shard_map/ppermute | solution.py:52
  43.8 0.5 collective-permute-start.15
  44.4 1.3 %collective-permute-done.14 = bf16[1024,256]{1,0:T(8,128)(2,1)S(1)} collective-permute-done((bf16[1024,256]{1,0:T(8,128)(2,1)S(1)}, bf16[1024,256]{1,0:T(8,128)(2,1)S(1)}, u32[]{:S(2)}, u32[]{:S(2)}) %collective-permute-start.14) | collective-permute-done | bytes 524320 | tf_op jit(solution)/shard_map/ppermute | solution.py:52
  45.7 0.7 collective-permute-done.15
  46.4 6.9 %phase.5 = (f32[4,128,256]{2,1,0:T(8,128)S(1)}, f32[4,128,256]{2,1,0:T(8,128)S(1)}) custom-call(s32[820]{0:T(1024)S(1)} %concatenate.22.meta, bf16[704,128,128]{2,1,0:T(8,128)(2,1)} %tiles.7, bf16[16,128,256]{2,1,0:T(8,128)(2,1)S(1)} %bitcast.97, bf16[16,128,256]{2,1,0:T(8,128)(2,1)S(1)} %bitcast.98, bf16[8,128,256]{2,1,0:T(8,128)(2,1)S(1)} %bitcast.109, ...), custom_call_target="tpu_custom_call" | custom-call | flops 3221225472 | bytes 12582912 | tf_op jit(solution)/shard_map/phase/pallas_call | solution.py:195
  53.3 2.3 %collective-permute-done.5 = bf16[2048,256]{1,0:T(8,128)(2,1)S(1)} collective-permute-done((bf16[2048,256]{1,0:T(8,128)(2,1)S(1)}, bf16[2048,256]{1,0:T(8,128)(2,1)S(1)}, u32[]{:S(2)}, u32[]{:S(2)}) %collective-permute-start.5) | collective-permute-done | bytes 1048608 | tf_op jit(solution)/shard_map/ppermute | solution.py:52
  55.6 1.0 %collective-permute-done.6 = bf16[2048,256]{1,0:T(8,128)(2,1)S(1)} collective-permute-done((bf16[2048,256]{1,0:T(8,128)(2,1)S(1)}, bf16[2048,256]{1,0:T(8,128)(2,1)S(1)}, u32[]{:S(2)}, u32[]{:S(2)}) %collective-permute-start.6) | collective-permute-done | bytes 1048608 | tf_op jit(solution)/shard_map/ppermute | solution.py:52
  56.6 0.5 collective-permute-start.20
  57.1 0.3 collective-permute-start.16
  57.4 3.3 %collective-permute-start.17 = (bf16[1024,256]{1,0:T(8,128)(2,1)S(1)}, bf16[1024,256]{1,0:T(8,128)(2,1)S(1)}, u32[]{:S(2)}, u32[]{:S(2)}) collective-permute-start(bf16[1024,256]{1,0:T(8,128)(2,1)S(1)} %slice.81), channel_id=1, source_target_pairs={{0,6},{1,49},{2,0},{3,51},{4,2},{5,53},{6,4},{7,55},{8,14},{9,57},... | collective-permute-start | bytes 1572872 | tf_op jit(solution)/shard_map/ppermute | solution.py:52
  60.7 1.5 %collective-permute-start.23 = (f32[4,128,256]{2,1,0:T(8,128)S(1)}, f32[4,128,256]{2,1,0:T(8,128)S(1)}, u32[]{:S(2)}, u32[]{:S(2)}) collective-permute-start(f32[4,128,256]{2,1,0:T(8,128)S(1)} %get-tuple-element.46), channel_id=1, source_target_pairs={{0,64},{64,0},{1,65},{65,1},{2,66},{66,2},{3,67},{67,3},{4,68},{68... | collective-permute-start | bytes 1572872 | tf_op jit(solution)/shard_map/ppermute | solution.py:258
  62.2 7.2 %phase.6.refs_4_ = f32[8,128,256]{2,1,0:T(8,128)S(1)} custom-call(s32[820]{0:T(1024)S(1)} %concatenate.23.meta, bf16[704,128,128]{2,1,0:T(8,128)(2,1)} %tiles.7, bf16[16,128,256]{2,1,0:T(8,128)(2,1)S(1)} %bitcast.101, bf16[16,128,256]{2,1,0:T(8,128)(2,1)S(1)} %bitcast.99, bf16[16,128,256]{2,1,0:T(8,128)(2,1)S(1)} %bitcast.100, ...), custom_call_target="tpu_custom_call" | custom-call | flops 3221225472 | bytes 12582912 | tf_op jit(solution)/shard_map/phase/pallas_call | solution.py:195
  69.6 0.5 collective-permute-start.22
  70.1 3.8 %collective-permute-done.23 = f32[4,128,256]{2,1,0:T(8,128)S(1)} collective-permute-done((f32[4,128,256]{2,1,0:T(8,128)S(1)}, f32[4,128,256]{2,1,0:T(8,128)S(1)}, u32[]{:S(2)}, u32[]{:S(2)}) %collective-permute-start.23) | collective-permute-done | bytes 524320 | tf_op jit(solution)/shard_map/ppermute | solution.py:258
  73.9 4.0 %phase.7 = (f32[4,128,256]{2,1,0:T(8,128)S(1)}, bf16[4,128,256]{2,1,0:T(8,128)(2,1)S(1)}) custom-call(s32[274]{0:T(512)S(1)} %concatenate.24.meta, bf16[704,128,128]{2,1,0:T(8,128)(2,1)} %tiles.7, bf16[8,128,256]{2,1,0:T(8,128)(2,1)S(1)} %bitcast.113, bf16[8,128,256]{2,1,0:T(8,128)(2,1)S(1)} %bitcast.114, bf16[8,128,256]{2,1,0:T(8,128)(2,1)S(1)} %bitcast.115, ...), custom_call_target="tpu_custom_call" | custom-call | flops 1073741824 | bytes 4194304 | tf_op jit(solution)/shard_map/phase/pallas_call | solution.py:195
  77.9 3.1 %collective-permute-start.24 = (bf16[4,128,256]{2,1,0:T(8,128)(2,1)S(1)}, bf16[4,128,256]{2,1,0:T(8,128)(2,1)S(1)}, u32[]{:S(2)}, u32[]{:S(2)}) collective-permute-start(bf16[4,128,256]{2,1,0:T(8,128)(2,1)S(1)} %get-tuple-element.50), channel_id=1, source_target_pairs={{0,64},{64,0},{1,65},{65,1},{2,66},{66,2},{3,67},{67,3},{4,68},{68... | collective-permute-start | bytes 786440 | tf_op jit(solution)/shard_map/ppermute | solution.py:268
  81.1 0.2 convolution_add_fusion.1
  81.3 5.3 %collective-permute-done.24 = bf16[4,128,256]{2,1,0:T(8,128)(2,1)S(1)} collective-permute-done((bf16[4,128,256]{2,1,0:T(8,128)(2,1)S(1)}, bf16[4,128,256]{2,1,0:T(8,128)(2,1)S(1)}, u32[]{:S(2)}, u32[]{:S(2)}) %collective-permute-start.24) | collective-permute-done | bytes 262176 | tf_op jit(solution)/shard_map/ppermute | solution.py:268
  86.6 0.1 convert_add_fusion
  86.7 0.1 fusion.3
  86.9 0.9 %fusion.2 = bf16[512,256]{1,0:T(8,128)(2,1)} fusion(f32[512,256]{1,0:T(8,128)S(1)} %convolution_add_fusion.1, bf16[512,256]{1,0:T(8,128)(2,1)S(1)} %fusion.3, bf16[256,256]{1,0:T(8,128)(2,1)S(1)} %copy-done.2), kind=kOutput, calls=%fused_computation.8 | convolution fusion | flops 67502080 | bytes 1179648 | tf_op jit(solution)/shard_map/dot_general | solution.py:272
  (60 shorter events, 1.1 us)
Async XLA Ops:
  0.0 81.1 %copy-start = (bf16[256,256]{1,0:T(8,128)(2,1)S(1)}, bf16[256,256]{1,0:T(8,128)(2,1)}, u32[]{:S(2)}) copy-start(bf16[256,256]{1,0:T(8,128)(2,1)} %param.15) | copy-start | bytes 393220
  0.0 13.4 %copy-start.1 = (bf16[512,256]{1,0:T(8,128)(2,1)S(1)}, bf16[512,256]{1,0:T(8,128)(2,1)}, u32[]{:S(2)}) copy-start(bf16[512,256]{1,0:T(8,128)(2,1)} %param.9) | copy-start | bytes 786436
  0.0 9.1 %copy-start.4 = (s32[704]{0:T(1024)S(1)}, s32[704]{0:T(1024)}, u32[]{:S(2)}) copy-start(s32[704]{0:T(1024)} %param.12) | copy-start | bytes 8452
  0.0 9.6 %copy-start.3 = (s32[704]{0:T(1024)S(1)}, s32[704]{0:T(1024)}, u32[]{:S(2)}) copy-start(s32[704]{0:T(1024)} %param.11) | copy-start | bytes 8452
  0.0 13.5 %collective-permute-start = (bf16[512,256]{1,0:T(8,128)(2,1)}, bf16[512,256]{1,0:T(8,128)(2,1)S(1)}, u32[]{:S(2)}, u32[]{:S(2)}) collective-permute-start(bf16[512,256]{1,0:T(8,128)(2,1)} %param.9), channel_id=1, source_target_pairs={{0,16},{1,3},{2,18},{3,5},{4,20},{5,7},{6,22},{7,1},{8,24},{9,11},... | collective-permute-start | bytes 786440 | tf_op jit(solution)/shard_map/ppermute | solution.py:52
  1.7 11.7 %collective-permute-start.1 = (bf16[512,256]{1,0:T(8,128)(2,1)}, bf16[512,256]{1,0:T(8,128)(2,1)S(1)}, u32[]{:S(2)}, u32[]{:S(2)}) collective-permute-start(bf16[512,256]{1,0:T(8,128)(2,1)} %param.9), channel_id=1, source_target_pairs={{0,48},{1,7},{2,50},{3,1},{4,52},{5,3},{6,54},{7,5},{8,56},{9,15},... | collective-permute-start | bytes 786440 | tf_op jit(solution)/shard_map/ppermute | solution.py:52
  3.3 10.2 %collective-permute-start.2 = (bf16[512,256]{1,0:T(8,128)(2,1)}, bf16[512,256]{1,0:T(8,128)(2,1)S(1)}, u32[]{:S(2)}, u32[]{:S(2)}) collective-permute-start(bf16[512,256]{1,0:T(8,128)(2,1)} %param.9), channel_id=1, source_target_pairs={{0,32},{1,5},{2,34},{3,7},{4,36},{5,1},{6,38},{7,3},{8,40},{9,13},... | collective-permute-start | bytes 786440 | tf_op jit(solution)/shard_map/ppermute | solution.py:52
  5.4 9.6 %collective-permute-start.3 = (bf16[512,256]{1,0:T(8,128)(2,1)}, bf16[512,256]{1,0:T(8,128)(2,1)S(1)}, u32[]{:S(2)}, u32[]{:S(2)}) collective-permute-start(bf16[512,256]{1,0:T(8,128)(2,1)} %param.9), channel_id=1, source_target_pairs={{0,8},{1,9},{2,10},{3,11},{4,12},{5,13},{6,14},{7,15},{8,0},{9,1},... | collective-permute-start | bytes 786440 | tf_op jit(solution)/shard_map/ppermute | solution.py:52
  15.1 6.6 %collective-permute-start.9 = (bf16[2048,256]{1,0:T(8,128)(2,1)S(1)}, bf16[2048,256]{1,0:T(8,128)(2,1)S(1)}, u32[]{:S(2)}, u32[]{:S(2)}) collective-permute-start(bf16[2048,256]{1,0:T(8,128)(2,1)S(1)} %constant_dynamic-update-slice_fusion.2), channel_id=1, source_target_pairs={{0,1},{1,0},{2,3},{3,2},{4,5},{5,4},{6,7},{7,6},{8,9},{9,8},{10,11... | collective-permute-start | bytes 3145736 | tf_op jit(solution)/shard_map/ppermute | solution.py:52
  15.2 16.1 %collective-permute-start.7 = (bf16[2048,256]{1,0:T(8,128)(2,1)S(1)}, bf16[2048,256]{1,0:T(8,128)(2,1)S(1)}, u32[]{:S(2)}, u32[]{:S(2)}) collective-permute-start(bf16[2048,256]{1,0:T(8,128)(2,1)S(1)} %constant_dynamic-update-slice_fusion.2), channel_id=1, source_target_pairs={{0,2},{1,17},{2,4},{3,19},{4,6},{5,21},{6,0},{7,23},{8,10},{9,25},... | collective-permute-start | bytes 3145736 | tf_op jit(solution)/shard_map/ppermute | solution.py:52
  16.3 15.0 %collective-permute-start.8 = (bf16[2048,256]{1,0:T(8,128)(2,1)S(1)}, bf16[2048,256]{1,0:T(8,128)(2,1)S(1)}, u32[]{:S(2)}, u32[]{:S(2)}) collective-permute-start(bf16[2048,256]{1,0:T(8,128)(2,1)S(1)} %constant_dynamic-update-slice_fusion.2), channel_id=1, source_target_pairs={{0,6},{1,49},{2,0},{3,51},{4,2},{5,53},{6,4},{7,55},{8,14},{9,57},... | collective-permute-start | bytes 3145736 | tf_op jit(solution)/shard_map/ppermute | solution.py:52
  18.5 20.9 %collective-permute-start.4 = (bf16[1536,256]{1,0:T(8,128)(2,1)S(1)}, bf16[1536,256]{1,0:T(8,128)(2,1)S(1)}, u32[]{:S(2)}, u32[]{:S(2)}) collective-permute-start(bf16[1536,256]{1,0:T(8,128)(2,1)S(1)} %pad_maximum_fusion), channel_id=1, source_target_pairs={{0,8},{1,9},{2,10},{3,11},{4,12},{5,13},{6,14},{7,15},{8,0},{9,1},... | collective-permute-start | bytes 2359304 | tf_op jit(solution)/shard_map/ppermute | solution.py:52
  31.2 12.5 %collective-permute-start.12 = (bf16[2048,256]{1,0:T(8,128)(2,1)S(1)}, bf16[2048,256]{1,0:T(8,128)(2,1)S(1)}, u32[]{:S(2)}, u32[]{:S(2)}) collective-permute-start(bf16[2048,256]{1,0:T(8,128)(2,1)S(1)} %collective-permute-done.7), channel_id=1, source_target_pairs={{0,1},{1,0},{2,3},{3,2},{4,5},{5,4},{6,7},{7,6},{8,9},{9,8},{10,11... | collective-permute-start | bytes 3145736 | tf_op jit(solution)/shard_map/ppermute | solution.py:52
  31.3 10.5 %collective-permute-start.10 = (bf16[1024,256]{1,0:T(8,128)(2,1)S(1)}, bf16[1024,256]{1,0:T(8,128)(2,1)S(1)}, u32[]{:S(2)}, u32[]{:S(2)}) collective-permute-start(bf16[1024,256]{1,0:T(8,128)(2,1)S(1)} %slice.78), channel_id=1, source_target_pairs={{0,2},{1,17},{2,4},{3,19},{4,6},{5,21},{6,0},{7,23},{8,10},{9,25},... | collective-permute-start | bytes 1572872 | tf_op jit(solution)/shard_map/ppermute | solution.py:52
  32.5 11.8 %collective-permute-start.13 = (bf16[2048,256]{1,0:T(8,128)(2,1)S(1)}, bf16[2048,256]{1,0:T(8,128)(2,1)S(1)}, u32[]{:S(2)}, u32[]{:S(2)}) collective-permute-start(bf16[2048,256]{1,0:T(8,128)(2,1)S(1)} %collective-permute-done.8), channel_id=1, source_target_pairs={{0,1},{1,0},{2,3},{3,2},{4,5},{5,4},{6,7},{7,6},{8,9},{9,8},{10,11... | collective-permute-start | bytes 3145736 | tf_op jit(solution)/shard_map/ppermute | solution.py:52
  33.3 10.5 %collective-permute-start.11 = (bf16[1024,256]{1,0:T(8,128)(2,1)S(1)}, bf16[1024,256]{1,0:T(8,128)(2,1)S(1)}, u32[]{:S(2)}, u32[]{:S(2)}) collective-permute-start(bf16[1024,256]{1,0:T(8,128)(2,1)S(1)} %slice.79), channel_id=1, source_target_pairs={{0,6},{1,49},{2,0},{3,51},{4,2},{5,53},{6,4},{7,55},{8,14},{9,57},... | collective-permute-start | bytes 1572872 | tf_op jit(solution)/shard_map/ppermute | solution.py:52
  39.5 16.1 %collective-permute-start.5 = (bf16[2048,256]{1,0:T(8,128)(2,1)S(1)}, bf16[2048,256]{1,0:T(8,128)(2,1)S(1)}, u32[]{:S(2)}, u32[]{:S(2)}) collective-permute-start(bf16[2048,256]{1,0:T(8,128)(2,1)S(1)} %constant_dynamic-update-slice_fusion), channel_id=1, source_target_pairs={{0,2},{1,17},{2,4},{3,19},{4,6},{5,21},{6,0},{7,23},{8,10},{9,25},... | collective-permute-start | bytes 3145736 | tf_op jit(solution)/shard_map/ppermute | solution.py:52
  41.8 14.8 %collective-permute-start.6 = (bf16[2048,256]{1,0:T(8,128)(2,1)S(1)}, bf16[2048,256]{1,0:T(8,128)(2,1)S(1)}, u32[]{:S(2)}, u32[]{:S(2)}) collective-permute-start(bf16[2048,256]{1,0:T(8,128)(2,1)S(1)} %constant_dynamic-update-slice_fusion), channel_id=1, source_target_pairs={{0,6},{1,49},{2,0},{3,51},{4,2},{5,53},{6,4},{7,55},{8,14},{9,57},... | collective-permute-start | bytes 3145736 | tf_op jit(solution)/shard_map/ppermute | solution.py:52
  43.8 1.9 %collective-permute-start.14 = (bf16[1024,256]{1,0:T(8,128)(2,1)S(1)}, bf16[1024,256]{1,0:T(8,128)(2,1)S(1)}, u32[]{:S(2)}, u32[]{:S(2)}) collective-permute-start(bf16[1024,256]{1,0:T(8,128)(2,1)S(1)} %collective-permute-done.10), channel_id=1, source_target_pairs={{0,1},{1,0},{2,3},{3,2},{4,5},{5,4},{6,7},{7,6},{8,9},{9,8},{10,11... | collective-permute-start | bytes 1572872 | tf_op jit(solution)/shard_map/ppermute | solution.py:52
  43.8 2.7 %collective-permute-start.15 = (bf16[1024,256]{1,0:T(8,128)(2,1)S(1)}, bf16[1024,256]{1,0:T(8,128)(2,1)S(1)}, u32[]{:S(2)}, u32[]{:S(2)}) collective-permute-start(bf16[1024,256]{1,0:T(8,128)(2,1)S(1)} %collective-permute-done.11), channel_id=1, source_target_pairs={{0,1},{1,0},{2,3},{3,2},{4,5},{5,4},{6,7},{7,6},{8,9},{9,8},{10,11... | collective-permute-start | bytes 1572872 | tf_op jit(solution)/shard_map/ppermute | solution.py:52
  44.3 16.4 %collective-permute-start.18 = (bf16[2048,256]{1,0:T(8,128)(2,1)S(1)}, bf16[2048,256]{1,0:T(8,128)(2,1)S(1)}, u32[]{:S(2)}, u32[]{:S(2)}) collective-permute-start(bf16[2048,256]{1,0:T(8,128)(2,1)S(1)} %constant_dynamic-update-slice_fusion), channel_id=1, source_target_pairs={{0,1},{1,0},{2,3},{3,2},{4,5},{5,4},{6,7},{7,6},{8,9},{9,8},{10,11... | collective-permute-start | bytes 3145736 | tf_op jit(solution)/shard_map/ppermute | solution.py:52
  56.6 5.7 %collective-permute-start.19 = (bf16[2048,256]{1,0:T(8,128)(2,1)S(1)}, bf16[2048,256]{1,0:T(8,128)(2,1)S(1)}, u32[]{:S(2)}, u32[]{:S(2)}) collective-permute-start(bf16[2048,256]{1,0:T(8,128)(2,1)S(1)} %collective-permute-done.5), channel_id=1, source_target_pairs={{0,1},{1,0},{2,3},{3,2},{4,5},{5,4},{6,7},{7,6},{8,9},{9,8},{10,11... | collective-permute-start | bytes 3145736 | tf_op jit(solution)/shard_map/ppermute | solution.py:52
  56.6 5.7 %collective-permute-start.20 = (bf16[2048,256]{1,0:T(8,128)(2,1)S(1)}, bf16[2048,256]{1,0:T(8,128)(2,1)S(1)}, u32[]{:S(2)}, u32[]{:S(2)}) collective-permute-start(bf16[2048,256]{1,0:T(8,128)(2,1)S(1)} %collective-permute-done.6), channel_id=1, source_target_pairs={{0,1},{1,0},{2,3},{3,2},{4,5},{5,4},{6,7},{7,6},{8,9},{9,8},{10,11... | collective-permute-start | bytes 3145736 | tf_op jit(solution)/shard_map/ppermute | solution.py:52
  57.1 12.3 %collective-permute-start.16 = (bf16[1024,256]{1,0:T(8,128)(2,1)S(1)}, bf16[1024,256]{1,0:T(8,128)(2,1)S(1)}, u32[]{:S(2)}, u32[]{:S(2)}) collective-permute-start(bf16[1024,256]{1,0:T(8,128)(2,1)S(1)} %slice.80), channel_id=1, source_target_pairs={{0,2},{1,17},{2,4},{3,19},{4,6},{5,21},{6,0},{7,23},{8,10},{9,25},... | collective-permute-start | bytes 1572872 | tf_op jit(solution)/shard_map/ppermute | solution.py:52
  57.4 12.1 %collective-permute-start.17 = (bf16[1024,256]{1,0:T(8,128)(2,1)S(1)}, bf16[1024,256]{1,0:T(8,128)(2,1)S(1)}, u32[]{:S(2)}, u32[]{:S(2)}) collective-permute-start(bf16[1024,256]{1,0:T(8,128)(2,1)S(1)} %slice.81), channel_id=1, source_target_pairs={{0,6},{1,49},{2,0},{3,51},{4,2},{5,53},{6,4},{7,55},{8,14},{9,57},... | collective-permute-start | bytes 1572872 | tf_op jit(solution)/shard_map/ppermute | solution.py:52
  60.7 13.2 %collective-permute-start.23 = (f32[4,128,256]{2,1,0:T(8,128)S(1)}, f32[4,128,256]{2,1,0:T(8,128)S(1)}, u32[]{:S(2)}, u32[]{:S(2)}) collective-permute-start(f32[4,128,256]{2,1,0:T(8,128)S(1)} %get-tuple-element.46), channel_id=1, source_target_pairs={{0,64},{64,0},{1,65},{65,1},{2,66},{66,2},{3,67},{67,3},{4,68},{68... | collective-permute-start | bytes 1572872 | tf_op jit(solution)/shard_map/ppermute | solution.py:258
  69.5 4.4 %collective-permute-start.21 = (bf16[1024,256]{1,0:T(8,128)(2,1)S(1)}, bf16[1024,256]{1,0:T(8,128)(2,1)S(1)}, u32[]{:S(2)}, u32[]{:S(2)}) collective-permute-start(bf16[1024,256]{1,0:T(8,128)(2,1)S(1)} %collective-permute-done.16), channel_id=1, source_target_pairs={{0,1},{1,0},{2,3},{3,2},{4,5},{5,4},{6,7},{7,6},{8,9},{9,8},{10,11... | collective-permute-start | bytes 1572872 | tf_op jit(solution)/shard_map/ppermute | solution.py:52
  69.6 4.3 %collective-permute-start.22 = (bf16[1024,256]{1,0:T(8,128)(2,1)S(1)}, bf16[1024,256]{1,0:T(8,128)(2,1)S(1)}, u32[]{:S(2)}, u32[]{:S(2)}) collective-permute-start(bf16[1024,256]{1,0:T(8,128)(2,1)S(1)} %collective-permute-done.17), channel_id=1, source_target_pairs={{0,1},{1,0},{2,3},{3,2},{4,5},{5,4},{6,7},{7,6},{8,9},{9,8},{10,11... | collective-permute-start | bytes 1572872 | tf_op jit(solution)/shard_map/ppermute | solution.py:52
  73.9 7.1 %copy-start.5 = (s32[512]{0:T(512)S(1)}, s32[512]{0:T(512)}, u32[]{:S(2)}) copy-start(s32[512]{0:T(512)} %param.14) | copy-start | bytes 6148
  73.9 7.1 %copy-start.6 = (f32[256]{0:T(256)S(1)}, f32[256]{0:T(256)}, u32[]{:S(2)}) copy-start(f32[256]{0:T(256)} %param.17) | copy-start | bytes 3076
  77.9 9.0 %copy-start.2 = (bf16[256,256]{1,0:T(8,128)(2,1)S(1)}, bf16[256,256]{1,0:T(8,128)(2,1)}, u32[]{:S(2)}) copy-start(bf16[256,256]{1,0:T(8,128)(2,1)} %param.16) | copy-start | bytes 393220
  77.9 8.7 %collective-permute-start.24 = (bf16[4,128,256]{2,1,0:T(8,128)(2,1)S(1)}, bf16[4,128,256]{2,1,0:T(8,128)(2,1)S(1)}, u32[]{:S(2)}, u32[]{:S(2)}) collective-permute-start(bf16[4,128,256]{2,1,0:T(8,128)(2,1)S(1)} %get-tuple-element.50), channel_id=1, source_target_pairs={{0,64},{64,0},{1,65},{65,1},{2,66},{66,2},{3,67},{67,3},{4,68},{68... | collective-permute-start | bytes 786440 | tf_op jit(solution)/shard_map/ppermute | solution.py:268

commit v5 on v4

--- a/solution.py
+++ b/solution.py
@@ -24,7 +24,7 @@
 SLOTS = STEP * GROUP_STEPS * GROUPS
 OWNERS = GROUP * GROUPS
 SPLIT = (1, 3)
-VMEM_BYTES = 44 << 20
+VMEM_BYTES = 39 << 20
 LINE = (0, -1, 1, 2)
 HEAD, TAIL = LINE[:2], LINE[2:]
 

time: 87.7 us -> 87.7 us (level); the launches traced: 87.8 us -> 86.5 us
  starting transfers between devices: 32.8 us -> 31.9 us
  transfers between devices with their start and end apart: 25 -> 25, of which waited for: 10 -> 10; matrix products, arithmetic and copies ran while one was open for 5% -> 6% of each run, Pallas kernels for 21% -> 21%
where the time goes in v5:
time: 87.7 us; the launch traced here: 86.5 us
  starting transfers between devices  31.9 us (36%)
  waiting for transfers between devices  25.4 us (29%)
  Pallas kernels  22.1 us (25%)
  local copies, waits for them, and re-layouts  2.89 us (3%)
  other arithmetic  1.99 us (2%)
  matrix products  1.17 us (1%)
  between operations  0.98 us (1%)
    ppermute x23, starting transfers between devices, send(): return lax.ppermute(rows, 'row', pairs)  28.2 us
    pallas_call x4, Pallas kernels, run_phase(): pl.pallas_call(functools.partial(phase_kernel, phase, counts), out_shape=...  22.1 us
    ppermute x23, waiting for transfers between devices, send(): return lax.ppermute(rows, 'row', pairs)  16.7 us
    ppermute x1, waiting for transfers between devices, on_device(): late = lax.ppermute(away, 'rep', swap)  5.1 us
    ppermute x1, waiting for transfers between devices, on_device(): early = lax.ppermute(away, 'rep', swap)  3.65 us
    ppermute x1, starting transfers between devices, on_device(): late = lax.ppermute(away, 'rep', swap)  2.26 us
  transfers between devices with their start and end apart: 25, of which 10 were waited for; matrix products, arithmetic and copies ran while one was open for 6% of the time, Pallas kernels for 21%

profile of v5, /device:TPU:0, one launch (start us, length us, event | category | flops | bytes accessed | tf_op | source)
XLA Modules:
  0.0 86.5 jit_solution(16981343756348968577)
XLA Ops:
  0.0 1.7 %collective-permute-start = (bf16[512,256]{1,0:T(8,128)(2,1)}, bf16[512,256]{1,0:T(8,128)(2,1)S(1)}, u32[]{:S(2)}, u32[]{:S(2)}) collective-permute-start(bf16[512,256]{1,0:T(8,128)(2,1)} %param.9), channel_id=1, source_target_pairs={{0,16},{1,3},{2,18},{3,5},{4,20},{5,7},{6,22},{7,1},{8,24},{9,11},... | collective-permute-start | bytes 786440 | tf_op jit(solution)/shard_map/ppermute | solution.py:52
  1.7 1.6 %collective-permute-start.1 = (bf16[512,256]{1,0:T(8,128)(2,1)}, bf16[512,256]{1,0:T(8,128)(2,1)S(1)}, u32[]{:S(2)}, u32[]{:S(2)}) collective-permute-start(bf16[512,256]{1,0:T(8,128)(2,1)} %param.9), channel_id=1, source_target_pairs={{0,48},{1,7},{2,50},{3,1},{4,52},{5,3},{6,54},{7,5},{8,56},{9,15},... | collective-permute-start | bytes 786440 | tf_op jit(solution)/shard_map/ppermute | solution.py:52
  3.3 2.1 %collective-permute-start.2 = (bf16[512,256]{1,0:T(8,128)(2,1)}, bf16[512,256]{1,0:T(8,128)(2,1)S(1)}, u32[]{:S(2)}, u32[]{:S(2)}) collective-permute-start(bf16[512,256]{1,0:T(8,128)(2,1)} %param.9), channel_id=1, source_target_pairs={{0,32},{1,5},{2,34},{3,7},{4,36},{5,1},{6,38},{7,3},{8,40},{9,13},... | collective-permute-start | bytes 786440 | tf_op jit(solution)/shard_map/ppermute | solution.py:52
  5.4 3.0 %collective-permute-start.3 = (bf16[512,256]{1,0:T(8,128)(2,1)}, bf16[512,256]{1,0:T(8,128)(2,1)S(1)}, u32[]{:S(2)}, u32[]{:S(2)}) collective-permute-start(bf16[512,256]{1,0:T(8,128)(2,1)} %param.9), channel_id=1, source_target_pairs={{0,8},{1,9},{2,10},{3,11},{4,12},{5,13},{6,14},{7,15},{8,0},{9,1},... | collective-permute-start | bytes 786440 | tf_op jit(solution)/shard_map/ppermute | solution.py:52
  9.1 0.1 stack.259
  9.3 0.2 convert_reduce_fusion.2
  9.5 0.1 fusion.4
  9.6 0.3 convert_reduce_fusion
  10.0 0.1 convert_reduce_fusion.1
  10.3 0.7 select_reduce_fusion
  11.1 0.1 fusion.14
  11.3 0.6 fusion.26
  11.8 0.7 concatenate.24.meta
  12.8 0.6 concatenate.21.meta
  13.5 1.5 %collective-permute-done.3 = bf16[512,256]{1,0:T(8,128)(2,1)S(1)} collective-permute-done((bf16[512,256]{1,0:T(8,128)(2,1)}, bf16[512,256]{1,0:T(8,128)(2,1)S(1)}, u32[]{:S(2)}, u32[]{:S(2)}) %collective-permute-start.3) | collective-permute-done | bytes 262176 | tf_op jit(solution)/shard_map/ppermute | solution.py:52
  15.1 0.1 collective-permute-start.9
  15.2 1.1 %collective-permute-start.7 = (bf16[2048,256]{1,0:T(8,128)(2,1)S(1)}, bf16[2048,256]{1,0:T(8,128)(2,1)S(1)}, u32[]{:S(2)}, u32[]{:S(2)}) collective-permute-start(bf16[2048,256]{1,0:T(8,128)(2,1)S(1)} %constant_dynamic-update-slice_fusion.2), channel_id=1, source_target_pairs={{0,2},{1,17},{2,4},{3,19},{4,6},{5,21},{6,0},{7,23},{8,10},{9,25},... | collective-permute-start | bytes 3145736 | tf_op jit(solution)/shard_map/ppermute | solution.py:52
  16.3 2.2 %collective-permute-start.8 = (bf16[2048,256]{1,0:T(8,128)(2,1)S(1)}, bf16[2048,256]{1,0:T(8,128)(2,1)S(1)}, u32[]{:S(2)}, u32[]{:S(2)}) collective-permute-start(bf16[2048,256]{1,0:T(8,128)(2,1)S(1)} %constant_dynamic-update-slice_fusion.2), channel_id=1, source_target_pairs={{0,6},{1,49},{2,0},{3,51},{4,2},{5,53},{6,4},{7,55},{8,14},{9,57},... | collective-permute-start | bytes 3145736 | tf_op jit(solution)/shard_map/ppermute | solution.py:52
  18.5 3.1 %collective-permute-start.4 = (bf16[1536,256]{1,0:T(8,128)(2,1)S(1)}, bf16[1536,256]{1,0:T(8,128)(2,1)S(1)}, u32[]{:S(2)}, u32[]{:S(2)}) collective-permute-start(bf16[1536,256]{1,0:T(8,128)(2,1)S(1)} %pad_maximum_fusion), channel_id=1, source_target_pairs={{0,8},{1,9},{2,10},{3,11},{4,12},{5,13},{6,14},{7,15},{8,0},{9,1},... | collective-permute-start | bytes 2359304 | tf_op jit(solution)/shard_map/ppermute | solution.py:52
  21.6 3.4 %phase.4.refs_8_ = f32[8,128,256]{2,1,0:T(8,128)S(1)} custom-call(s32[274]{0:T(512)S(1)} %concatenate.21.meta, bf16[704,128,128]{2,1,0:T(8,128)(2,1)} %tiles.7, bf16[16,128,256]{2,1,0:T(8,128)(2,1)S(1)} %bitcast.102, bf16[16,128,256]{2,1,0:T(8,128)(2,1)S(1)} %bitcast.108), custom_call_target="tpu_custom_call" | custom-call | flops 1073741824 | bytes 4194304 | tf_op jit(solution)/shard_map/phase/pallas_call | solution.py:195
  25.1 6.2 %collective-permute-done.7 = bf16[2048,256]{1,0:T(8,128)(2,1)S(1)} collective-permute-done((bf16[2048,256]{1,0:T(8,128)(2,1)S(1)}, bf16[2048,256]{1,0:T(8,128)(2,1)S(1)}, u32[]{:S(2)}, u32[]{:S(2)}) %collective-permute-start.7) | collective-permute-done | bytes 1048608 | tf_op jit(solution)/shard_map/ppermute | solution.py:52
  31.3 1.2 %collective-permute-start.10 = (bf16[1024,256]{1,0:T(8,128)(2,1)S(1)}, bf16[1024,256]{1,0:T(8,128)(2,1)S(1)}, u32[]{:S(2)}, u32[]{:S(2)}) collective-permute-start(bf16[1024,256]{1,0:T(8,128)(2,1)S(1)} %slice.78), channel_id=1, source_target_pairs={{0,2},{1,17},{2,4},{3,19},{4,6},{5,21},{6,0},{7,23},{8,10},{9,25},... | collective-permute-start | bytes 1572872 | tf_op jit(solution)/shard_map/ppermute | solution.py:52
  32.5 0.7 collective-permute-start.13
  33.3 3.2 %collective-permute-start.11 = (bf16[1024,256]{1,0:T(8,128)(2,1)S(1)}, bf16[1024,256]{1,0:T(8,128)(2,1)S(1)}, u32[]{:S(2)}, u32[]{:S(2)}) collective-permute-start(bf16[1024,256]{1,0:T(8,128)(2,1)S(1)} %slice.79), channel_id=1, source_target_pairs={{0,6},{1,49},{2,0},{3,51},{4,2},{5,53},{6,4},{7,55},{8,14},{9,57},... | collective-permute-start | bytes 1572872 | tf_op jit(solution)/shard_map/ppermute | solution.py:52
  36.5 2.9 %collective-permute-done.4 = bf16[1536,256]{1,0:T(8,128)(2,1)S(1)} collective-permute-done((bf16[1536,256]{1,0:T(8,128)(2,1)S(1)}, bf16[1536,256]{1,0:T(8,128)(2,1)S(1)}, u32[]{:S(2)}, u32[]{:S(2)}) %collective-permute-start.4) | collective-permute-done | bytes 786464 | tf_op jit(solution)/shard_map/ppermute | solution.py:52
  39.5 0.8 collective-permute-start.5
  40.3 1.5 %collective-permute-done.10 = bf16[1024,256]{1,0:T(8,128)(2,1)S(1)} collective-permute-done((bf16[1024,256]{1,0:T(8,128)(2,1)S(1)}, bf16[1024,256]{1,0:T(8,128)(2,1)S(1)}, u32[]{:S(2)}, u32[]{:S(2)}) %collective-permute-start.10) | collective-permute-done | bytes 524320 | tf_op jit(solution)/shard_map/ppermute | solution.py:52
  41.8 2.0 %collective-permute-start.6 = (bf16[2048,256]{1,0:T(8,128)(2,1)S(1)}, bf16[2048,256]{1,0:T(8,128)(2,1)S(1)}, u32[]{:S(2)}, u32[]{:S(2)}) collective-permute-start(bf16[2048,256]{1,0:T(8,128)(2,1)S(1)} %constant_dynamic-update-slice_fusion), channel_id=1, source_target_pairs={{0,6},{1,49},{2,0},{3,51},{4,2},{5,53},{6,4},{7,55},{8,14},{9,57},... | collective-permute-start | bytes 3145736 | tf_op jit(solution)/shard_map/ppermute | solution.py:52
  43.8 0.5 collective-permute-start.15
  44.4 1.3 %collective-permute-done.14 = bf16[1024,256]{1,0:T(8,128)(2,1)S(1)} collective-permute-done((bf16[1024,256]{1,0:T(8,128)(2,1)S(1)}, bf16[1024,256]{1,0:T(8,128)(2,1)S(1)}, u32[]{:S(2)}, u32[]{:S(2)}) %collective-permute-start.14) | collective-permute-done | bytes 524320 | tf_op jit(solution)/shard_map/ppermute | solution.py:52
  45.7 0.7 collective-permute-done.15
  46.4 7.6 %phase.5 = (f32[4,128,256]{2,1,0:T(8,128)S(1)}, f32[4,128,256]{2,1,0:T(8,128)S(1)}) custom-call(s32[820]{0:T(1024)S(1)} %concatenate.22.meta, bf16[704,128,128]{2,1,0:T(8,128)(2,1)} %tiles.7, bf16[16,128,256]{2,1,0:T(8,128)(2,1)S(1)} %bitcast.97, bf16[16,128,256]{2,1,0:T(8,128)(2,1)S(1)} %bitcast.98, bf16[8,128,256]{2,1,0:T(8,128)(2,1)S(1)} %bitcast.109, ...), custom_call_target="tpu_custom_call" | custom-call | flops 3221225472 | bytes 12582912 | tf_op jit(solution)/shard_map/phase/pallas_call | solution.py:195
  54.0 1.5 %collective-permute-done.5 = bf16[2048,256]{1,0:T(8,128)(2,1)S(1)} collective-permute-done((bf16[2048,256]{1,0:T(8,128)(2,1)S(1)}, bf16[2048,256]{1,0:T(8,128)(2,1)S(1)}, u32[]{:S(2)}, u32[]{:S(2)}) %collective-permute-start.5) | collective-permute-done | bytes 1048608 | tf_op jit(solution)/shard_map/ppermute | solution.py:52
  55.6 1.0 %collective-permute-done.6 = bf16[2048,256]{1,0:T(8,128)(2,1)S(1)} collective-permute-done((bf16[2048,256]{1,0:T(8,128)(2,1)S(1)}, bf16[2048,256]{1,0:T(8,128)(2,1)S(1)}, u32[]{:S(2)}, u32[]{:S(2)}) %collective-permute-start.6) | collective-permute-done | bytes 1048608 | tf_op jit(solution)/shard_map/ppermute | solution.py:52
  56.6 0.5 collective-permute-start.20
  57.1 0.3 collective-permute-start.16
  57.4 3.3 %collective-permute-start.17 = (bf16[1024,256]{1,0:T(8,128)(2,1)S(1)}, bf16[1024,256]{1,0:T(8,128)(2,1)S(1)}, u32[]{:S(2)}, u32[]{:S(2)}) collective-permute-start(bf16[1024,256]{1,0:T(8,128)(2,1)S(1)} %slice.81), channel_id=1, source_target_pairs={{0,6},{1,49},{2,0},{3,51},{4,2},{5,53},{6,4},{7,55},{8,14},{9,57},... | collective-permute-start | bytes 1572872 | tf_op jit(solution)/shard_map/ppermute | solution.py:52
  60.7 1.5 %collective-permute-start.23 = (f32[4,128,256]{2,1,0:T(8,128)S(1)}, f32[4,128,256]{2,1,0:T(8,128)S(1)}, u32[]{:S(2)}, u32[]{:S(2)}) collective-permute-start(f32[4,128,256]{2,1,0:T(8,128)S(1)} %get-tuple-element.46), channel_id=1, source_target_pairs={{0,64},{64,0},{1,65},{65,1},{2,66},{66,2},{3,67},{67,3},{4,68},{68... | collective-permute-start | bytes 1572872 | tf_op jit(solution)/shard_map/ppermute | solution.py:258
  62.2 7.4 %phase.6.refs_4_ = f32[8,128,256]{2,1,0:T(8,128)S(1)} custom-call(s32[820]{0:T(1024)S(1)} %concatenate.23.meta, bf16[704,128,128]{2,1,0:T(8,128)(2,1)} %tiles.7, bf16[16,128,256]{2,1,0:T(8,128)(2,1)S(1)} %bitcast.101, bf16[16,128,256]{2,1,0:T(8,128)(2,1)S(1)} %bitcast.99, bf16[16,128,256]{2,1,0:T(8,128)(2,1)S(1)} %bitcast.100, ...), custom_call_target="tpu_custom_call" | custom-call | flops 3221225472 | bytes 12582912 | tf_op jit(solution)/shard_map/phase/pallas_call | solution.py:195
  69.8 0.5 collective-permute-start.22
  70.3 3.6 %collective-permute-done.23 = f32[4,128,256]{2,1,0:T(8,128)S(1)} collective-permute-done((f32[4,128,256]{2,1,0:T(8,128)S(1)}, f32[4,128,256]{2,1,0:T(8,128)S(1)}, u32[]{:S(2)}, u32[]{:S(2)}) %collective-permute-start.23) | collective-permute-done | bytes 524320 | tf_op jit(solution)/shard_map/ppermute | solution.py:258
  73.9 3.7 %phase.7 = (f32[4,128,256]{2,1,0:T(8,128)S(1)}, bf16[4,128,256]{2,1,0:T(8,128)(2,1)S(1)}) custom-call(s32[274]{0:T(512)S(1)} %concatenate.24.meta, bf16[704,128,128]{2,1,0:T(8,128)(2,1)} %tiles.7, bf16[8,128,256]{2,1,0:T(8,128)(2,1)S(1)} %bitcast.113, bf16[8,128,256]{2,1,0:T(8,128)(2,1)S(1)} %bitcast.114, bf16[8,128,256]{2,1,0:T(8,128)(2,1)S(1)} %bitcast.115, ...), custom_call_target="tpu_custom_call" | custom-call | flops 1073741824 | bytes 4194304 | tf_op jit(solution)/shard_map/phase/pallas_call | solution.py:195
  77.7 2.3 %collective-permute-start.24 = (bf16[4,128,256]{2,1,0:T(8,128)(2,1)S(1)}, bf16[4,128,256]{2,1,0:T(8,128)(2,1)S(1)}, u32[]{:S(2)}, u32[]{:S(2)}) collective-permute-start(bf16[4,128,256]{2,1,0:T(8,128)(2,1)S(1)} %get-tuple-element.50), channel_id=1, source_target_pairs={{0,64},{64,0},{1,65},{65,1},{2,66},{66,2},{3,67},{67,3},{4,68},{68... | collective-permute-start | bytes 786440 | tf_op jit(solution)/shard_map/ppermute | solution.py:268
  79.9 0.2 convolution_add_fusion.1
  80.2 5.1 %collective-permute-done.24 = bf16[4,128,256]{2,1,0:T(8,128)(2,1)S(1)} collective-permute-done((bf16[4,128,256]{2,1,0:T(8,128)(2,1)S(1)}, bf16[4,128,256]{2,1,0:T(8,128)(2,1)S(1)}, u32[]{:S(2)}, u32[]{:S(2)}) %collective-permute-start.24) | collective-permute-done | bytes 262176 | tf_op jit(solution)/shard_map/ppermute | solution.py:268
  85.3 0.1 convert_add_fusion
  85.4 0.1 fusion.3
  85.5 0.9 %fusion.2 = bf16[512,256]{1,0:T(8,128)(2,1)} fusion(f32[512,256]{1,0:T(8,128)S(1)} %convolution_add_fusion.1, bf16[512,256]{1,0:T(8,128)(2,1)S(1)} %fusion.3, bf16[256,256]{1,0:T(8,128)(2,1)S(1)} %copy-done.2), kind=kOutput, calls=%fused_computation.8 | convolution fusion | flops 67502080 | bytes 1179648 | tf_op jit(solution)/shard_map/dot_general | solution.py:272
  (60 shorter events, 1.1 us)
Async XLA Ops:
  0.0 79.9 %copy-start = (bf16[256,256]{1,0:T(8,128)(2,1)S(1)}, bf16[256,256]{1,0:T(8,128)(2,1)}, u32[]{:S(2)}) copy-start(bf16[256,256]{1,0:T(8,128)(2,1)} %param.15) | copy-start | bytes 393220
  0.0 13.4 %copy-start.1 = (bf16[512,256]{1,0:T(8,128)(2,1)S(1)}, bf16[512,256]{1,0:T(8,128)(2,1)}, u32[]{:S(2)}) copy-start(bf16[512,256]{1,0:T(8,128)(2,1)} %param.9) | copy-start | bytes 786436
  0.0 9.1 %copy-start.4 = (s32[704]{0:T(1024)S(1)}, s32[704]{0:T(1024)}, u32[]{:S(2)}) copy-start(s32[704]{0:T(1024)} %param.12) | copy-start | bytes 8452
  0.0 9.6 %copy-start.3 = (s32[704]{0:T(1024)S(1)}, s32[704]{0:T(1024)}, u32[]{:S(2)}) copy-start(s32[704]{0:T(1024)} %param.11) | copy-start | bytes 8452
  0.0 13.5 %collective-permute-start = (bf16[512,256]{1,0:T(8,128)(2,1)}, bf16[512,256]{1,0:T(8,128)(2,1)S(1)}, u32[]{:S(2)}, u32[]{:S(2)}) collective-permute-start(bf16[512,256]{1,0:T(8,128)(2,1)} %param.9), channel_id=1, source_target_pairs={{0,16},{1,3},{2,18},{3,5},{4,20},{5,7},{6,22},{7,1},{8,24},{9,11},... | collective-permute-start | bytes 786440 | tf_op jit(solution)/shard_map/ppermute | solution.py:52
  1.7 11.7 %collective-permute-start.1 = (bf16[512,256]{1,0:T(8,128)(2,1)}, bf16[512,256]{1,0:T(8,128)(2,1)S(1)}, u32[]{:S(2)}, u32[]{:S(2)}) collective-permute-start(bf16[512,256]{1,0:T(8,128)(2,1)} %param.9), channel_id=1, source_target_pairs={{0,48},{1,7},{2,50},{3,1},{4,52},{5,3},{6,54},{7,5},{8,56},{9,15},... | collective-permute-start | bytes 786440 | tf_op jit(solution)/shard_map/ppermute | solution.py:52
  3.3 10.2 %collective-permute-start.2 = (bf16[512,256]{1,0:T(8,128)(2,1)}, bf16[512,256]{1,0:T(8,128)(2,1)S(1)}, u32[]{:S(2)}, u32[]{:S(2)}) collective-permute-start(bf16[512,256]{1,0:T(8,128)(2,1)} %param.9), channel_id=1, source_target_pairs={{0,32},{1,5},{2,34},{3,7},{4,36},{5,1},{6,38},{7,3},{8,40},{9,13},... | collective-permute-start | bytes 786440 | tf_op jit(solution)/shard_map/ppermute | solution.py:52
  5.4 9.6 %collective-permute-start.3 = (bf16[512,256]{1,0:T(8,128)(2,1)}, bf16[512,256]{1,0:T(8,128)(2,1)S(1)}, u32[]{:S(2)}, u32[]{:S(2)}) collective-permute-start(bf16[512,256]{1,0:T(8,128)(2,1)} %param.9), channel_id=1, source_target_pairs={{0,8},{1,9},{2,10},{3,11},{4,12},{5,13},{6,14},{7,15},{8,0},{9,1},... | collective-permute-start | bytes 786440 | tf_op jit(solution)/shard_map/ppermute | solution.py:52
  15.1 6.6 %collective-permute-start.9 = (bf16[2048,256]{1,0:T(8,128)(2,1)S(1)}, bf16[2048,256]{1,0:T(8,128)(2,1)S(1)}, u32[]{:S(2)}, u32[]{:S(2)}) collective-permute-start(bf16[2048,256]{1,0:T(8,128)(2,1)S(1)} %constant_dynamic-update-slice_fusion.2), channel_id=1, source_target_pairs={{0,1},{1,0},{2,3},{3,2},{4,5},{5,4},{6,7},{7,6},{8,9},{9,8},{10,11... | collective-permute-start | bytes 3145736 | tf_op jit(solution)/shard_map/ppermute | solution.py:52
  15.2 16.1 %collective-permute-start.7 = (bf16[2048,256]{1,0:T(8,128)(2,1)S(1)}, bf16[2048,256]{1,0:T(8,128)(2,1)S(1)}, u32[]{:S(2)}, u32[]{:S(2)}) collective-permute-start(bf16[2048,256]{1,0:T(8,128)(2,1)S(1)} %constant_dynamic-update-slice_fusion.2), channel_id=1, source_target_pairs={{0,2},{1,17},{2,4},{3,19},{4,6},{5,21},{6,0},{7,23},{8,10},{9,25},... | collective-permute-start | bytes 3145736 | tf_op jit(solution)/shard_map/ppermute | solution.py:52
  16.3 15.0 %collective-permute-start.8 = (bf16[2048,256]{1,0:T(8,128)(2,1)S(1)}, bf16[2048,256]{1,0:T(8,128)(2,1)S(1)}, u32[]{:S(2)}, u32[]{:S(2)}) collective-permute-start(bf16[2048,256]{1,0:T(8,128)(2,1)S(1)} %constant_dynamic-update-slice_fusion.2), channel_id=1, source_target_pairs={{0,6},{1,49},{2,0},{3,51},{4,2},{5,53},{6,4},{7,55},{8,14},{9,57},... | collective-permute-start | bytes 3145736 | tf_op jit(solution)/shard_map/ppermute | solution.py:52
  18.5 20.9 %collective-permute-start.4 = (bf16[1536,256]{1,0:T(8,128)(2,1)S(1)}, bf16[1536,256]{1,0:T(8,128)(2,1)S(1)}, u32[]{:S(2)}, u32[]{:S(2)}) collective-permute-start(bf16[1536,256]{1,0:T(8,128)(2,1)S(1)} %pad_maximum_fusion), channel_id=1, source_target_pairs={{0,8},{1,9},{2,10},{3,11},{4,12},{5,13},{6,14},{7,15},{8,0},{9,1},... | collective-permute-start | bytes 2359304 | tf_op jit(solution)/shard_map/ppermute | solution.py:52
  31.2 12.5 %collective-permute-start.12 = (bf16[2048,256]{1,0:T(8,128)(2,1)S(1)}, bf16[2048,256]{1,0:T(8,128)(2,1)S(1)}, u32[]{:S(2)}, u32[]{:S(2)}) collective-permute-start(bf16[2048,256]{1,0:T(8,128)(2,1)S(1)} %collective-permute-done.7), channel_id=1, source_target_pairs={{0,1},{1,0},{2,3},{3,2},{4,5},{5,4},{6,7},{7,6},{8,9},{9,8},{10,11... | collective-permute-start | bytes 3145736 | tf_op jit(solution)/shard_map/ppermute | solution.py:52
  31.3 10.5 %collective-permute-start.10 = (bf16[1024,256]{1,0:T(8,128)(2,1)S(1)}, bf16[1024,256]{1,0:T(8,128)(2,1)S(1)}, u32[]{:S(2)}, u32[]{:S(2)}) collective-permute-start(bf16[1024,256]{1,0:T(8,128)(2,1)S(1)} %slice.78), channel_id=1, source_target_pairs={{0,2},{1,17},{2,4},{3,19},{4,6},{5,21},{6,0},{7,23},{8,10},{9,25},... | collective-permute-start | bytes 1572872 | tf_op jit(solution)/shard_map/ppermute | solution.py:52
  32.5 11.8 %collective-permute-start.13 = (bf16[2048,256]{1,0:T(8,128)(2,1)S(1)}, bf16[2048,256]{1,0:T(8,128)(2,1)S(1)}, u32[]{:S(2)}, u32[]{:S(2)}) collective-permute-start(bf16[2048,256]{1,0:T(8,128)(2,1)S(1)} %collective-permute-done.8), channel_id=1, source_target_pairs={{0,1},{1,0},{2,3},{3,2},{4,5},{5,4},{6,7},{7,6},{8,9},{9,8},{10,11... | collective-permute-start | bytes 3145736 | tf_op jit(solution)/shard_map/ppermute | solution.py:52
  33.3 10.5 %collective-permute-start.11 = (bf16[1024,256]{1,0:T(8,128)(2,1)S(1)}, bf16[1024,256]{1,0:T(8,128)(2,1)S(1)}, u32[]{:S(2)}, u32[]{:S(2)}) collective-permute-start(bf16[1024,256]{1,0:T(8,128)(2,1)S(1)} %slice.79), channel_id=1, source_target_pairs={{0,6},{1,49},{2,0},{3,51},{4,2},{5,53},{6,4},{7,55},{8,14},{9,57},... | collective-permute-start | bytes 1572872 | tf_op jit(solution)/shard_map/ppermute | solution.py:52
  39.5 16.1 %collective-permute-start.5 = (bf16[2048,256]{1,0:T(8,128)(2,1)S(1)}, bf16[2048,256]{1,0:T(8,128)(2,1)S(1)}, u32[]{:S(2)}, u32[]{:S(2)}) collective-permute-start(bf16[2048,256]{1,0:T(8,128)(2,1)S(1)} %constant_dynamic-update-slice_fusion), channel_id=1, source_target_pairs={{0,2},{1,17},{2,4},{3,19},{4,6},{5,21},{6,0},{7,23},{8,10},{9,25},... | collective-permute-start | bytes 3145736 | tf_op jit(solution)/shard_map/ppermute | solution.py:52
  41.8 14.8 %collective-permute-start.6 = (bf16[2048,256]{1,0:T(8,128)(2,1)S(1)}, bf16[2048,256]{1,0:T(8,128)(2,1)S(1)}, u32[]{:S(2)}, u32[]{:S(2)}) collective-permute-start(bf16[2048,256]{1,0:T(8,128)(2,1)S(1)} %constant_dynamic-update-slice_fusion), channel_id=1, source_target_pairs={{0,6},{1,49},{2,0},{3,51},{4,2},{5,53},{6,4},{7,55},{8,14},{9,57},... | collective-permute-start | bytes 3145736 | tf_op jit(solution)/shard_map/ppermute | solution.py:52
  43.8 1.9 %collective-permute-start.14 = (bf16[1024,256]{1,0:T(8,128)(2,1)S(1)}, bf16[1024,256]{1,0:T(8,128)(2,1)S(1)}, u32[]{:S(2)}, u32[]{:S(2)}) collective-permute-start(bf16[1024,256]{1,0:T(8,128)(2,1)S(1)} %collective-permute-done.10), channel_id=1, source_target_pairs={{0,1},{1,0},{2,3},{3,2},{4,5},{5,4},{6,7},{7,6},{8,9},{9,8},{10,11... | collective-permute-start | bytes 1572872 | tf_op jit(solution)/shard_map/ppermute | solution.py:52
  43.8 2.7 %collective-permute-start.15 = (bf16[1024,256]{1,0:T(8,128)(2,1)S(1)}, bf16[1024,256]{1,0:T(8,128)(2,1)S(1)}, u32[]{:S(2)}, u32[]{:S(2)}) collective-permute-start(bf16[1024,256]{1,0:T(8,128)(2,1)S(1)} %collective-permute-done.11), channel_id=1, source_target_pairs={{0,1},{1,0},{2,3},{3,2},{4,5},{5,4},{6,7},{7,6},{8,9},{9,8},{10,11... | collective-permute-start | bytes 1572872 | tf_op jit(solution)/shard_map/ppermute | solution.py:52
  44.3 16.4 %collective-permute-start.18 = (bf16[2048,256]{1,0:T(8,128)(2,1)S(1)}, bf16[2048,256]{1,0:T(8,128)(2,1)S(1)}, u32[]{:S(2)}, u32[]{:S(2)}) collective-permute-start(bf16[2048,256]{1,0:T(8,128)(2,1)S(1)} %constant_dynamic-update-slice_fusion), channel_id=1, source_target_pairs={{0,1},{1,0},{2,3},{3,2},{4,5},{5,4},{6,7},{7,6},{8,9},{9,8},{10,11... | collective-permute-start | bytes 3145736 | tf_op jit(solution)/shard_map/ppermute | solution.py:52
  56.6 5.7 %collective-permute-start.19 = (bf16[2048,256]{1,0:T(8,128)(2,1)S(1)}, bf16[2048,256]{1,0:T(8,128)(2,1)S(1)}, u32[]{:S(2)}, u32[]{:S(2)}) collective-permute-start(bf16[2048,256]{1,0:T(8,128)(2,1)S(1)} %collective-permute-done.5), channel_id=1, source_target_pairs={{0,1},{1,0},{2,3},{3,2},{4,5},{5,4},{6,7},{7,6},{8,9},{9,8},{10,11... | collective-permute-start | bytes 3145736 | tf_op jit(solution)/shard_map/ppermute | solution.py:52
  56.6 5.7 %collective-permute-start.20 = (bf16[2048,256]{1,0:T(8,128)(2,1)S(1)}, bf16[2048,256]{1,0:T(8,128)(2,1)S(1)}, u32[]{:S(2)}, u32[]{:S(2)}) collective-permute-start(bf16[2048,256]{1,0:T(8,128)(2,1)S(1)} %collective-permute-done.6), channel_id=1, source_target_pairs={{0,1},{1,0},{2,3},{3,2},{4,5},{5,4},{6,7},{7,6},{8,9},{9,8},{10,11... | collective-permute-start | bytes 3145736 | tf_op jit(solution)/shard_map/ppermute | solution.py:52
  57.1 12.5 %collective-permute-start.16 = (bf16[1024,256]{1,0:T(8,128)(2,1)S(1)}, bf16[1024,256]{1,0:T(8,128)(2,1)S(1)}, u32[]{:S(2)}, u32[]{:S(2)}) collective-permute-start(bf16[1024,256]{1,0:T(8,128)(2,1)S(1)} %slice.80), channel_id=1, source_target_pairs={{0,2},{1,17},{2,4},{3,19},{4,6},{5,21},{6,0},{7,23},{8,10},{9,25},... | collective-permute-start | bytes 1572872 | tf_op jit(solution)/shard_map/ppermute | solution.py:52
  57.4 12.3 %collective-permute-start.17 = (bf16[1024,256]{1,0:T(8,128)(2,1)S(1)}, bf16[1024,256]{1,0:T(8,128)(2,1)S(1)}, u32[]{:S(2)}, u32[]{:S(2)}) collective-permute-start(bf16[1024,256]{1,0:T(8,128)(2,1)S(1)} %slice.81), channel_id=1, source_target_pairs={{0,6},{1,49},{2,0},{3,51},{4,2},{5,53},{6,4},{7,55},{8,14},{9,57},... | collective-permute-start | bytes 1572872 | tf_op jit(solution)/shard_map/ppermute | solution.py:52
  60.7 13.2 %collective-permute-start.23 = (f32[4,128,256]{2,1,0:T(8,128)S(1)}, f32[4,128,256]{2,1,0:T(8,128)S(1)}, u32[]{:S(2)}, u32[]{:S(2)}) collective-permute-start(f32[4,128,256]{2,1,0:T(8,128)S(1)} %get-tuple-element.46), channel_id=1, source_target_pairs={{0,64},{64,0},{1,65},{65,1},{2,66},{66,2},{3,67},{67,3},{4,68},{68... | collective-permute-start | bytes 1572872 | tf_op jit(solution)/shard_map/ppermute | solution.py:258
  69.7 4.2 %collective-permute-start.21 = (bf16[1024,256]{1,0:T(8,128)(2,1)S(1)}, bf16[1024,256]{1,0:T(8,128)(2,1)S(1)}, u32[]{:S(2)}, u32[]{:S(2)}) collective-permute-start(bf16[1024,256]{1,0:T(8,128)(2,1)S(1)} %collective-permute-done.16), channel_id=1, source_target_pairs={{0,1},{1,0},{2,3},{3,2},{4,5},{5,4},{6,7},{7,6},{8,9},{9,8},{10,11... | collective-permute-start | bytes 1572872 | tf_op jit(solution)/shard_map/ppermute | solution.py:52
  69.8 4.2 %collective-permute-start.22 = (bf16[1024,256]{1,0:T(8,128)(2,1)S(1)}, bf16[1024,256]{1,0:T(8,128)(2,1)S(1)}, u32[]{:S(2)}, u32[]{:S(2)}) collective-permute-start(bf16[1024,256]{1,0:T(8,128)(2,1)S(1)} %collective-permute-done.17), channel_id=1, source_target_pairs={{0,1},{1,0},{2,3},{3,2},{4,5},{5,4},{6,7},{7,6},{8,9},{9,8},{10,11... | collective-permute-start | bytes 1572872 | tf_op jit(solution)/shard_map/ppermute | solution.py:52
  73.9 6.0 %copy-start.5 = (s32[512]{0:T(512)S(1)}, s32[512]{0:T(512)}, u32[]{:S(2)}) copy-start(s32[512]{0:T(512)} %param.14) | copy-start | bytes 6148
  73.9 6.0 %copy-start.6 = (f32[256]{0:T(256)S(1)}, f32[256]{0:T(256)}, u32[]{:S(2)}) copy-start(f32[256]{0:T(256)} %param.17) | copy-start | bytes 3076
  77.6 7.9 %copy-start.2 = (bf16[256,256]{1,0:T(8,128)(2,1)S(1)}, bf16[256,256]{1,0:T(8,128)(2,1)}, u32[]{:S(2)}) copy-start(bf16[256,256]{1,0:T(8,128)(2,1)} %param.16) | copy-start | bytes 393220
  77.7 7.6 %collective-permute-start.24 = (bf16[4,128,256]{2,1,0:T(8,128)(2,1)S(1)}, bf16[4,128,256]{2,1,0:T(8,128)(2,1)S(1)}, u32[]{:S(2)}, u32[]{:S(2)}) collective-permute-start(bf16[4,128,256]{2,1,0:T(8,128)(2,1)S(1)} %get-tuple-element.50), channel_id=1, source_target_pairs={{0,64},{64,0},{1,65},{65,1},{2,66},{66,2},{3,67},{67,3},{4,68},{68... | collective-permute-start | bytes 786440 | tf_op jit(solution)/shard_map/ppermute | solution.py:268
